TPU v7x, 768 devices: a whole 4x8x12 slice. The times are simulated.
768 devices in a mesh: dp: 24 (over y_lo, z), fsdp: 32 (over y_hi, x, core).
Axes of the slice: x: 4, y: 8 (y_hi: 4, y_lo: 2; y = y_hi * 2 + y_lo), z: 12, core: 2. Of those that a mesh axis runs over, the one named last changes fastest.
Arguments:
- rollout: bfloat16 [147456, 2048], P(('dp', 'fsdp')), may hold values from -6 to 6
- flows: int32 [24, 32], P(None, 'fsdp'), may hold values from -32 to 32, as said below
- route_ids: int32 [98304, 8], P(('dp', 'fsdp')), may hold values from 0 to 127, all different within a row; in each aligned block of 128 rows (0 to 127, 128 to 255, ...) at most 12 rows name the same one
- route_logits: float32 [98304, 8], P(('dp', 'fsdp')), may hold values from -18 to 406
- grad_out: bfloat16 [98304, 2048], P(('dp', 'fsdp')), may hold values from -0.099609375 to 0.099609375
- w_gate: bfloat16 [32, 2048, 768], P('fsdp'), may hold values from -0.125 to 0.125
- w_up: bfloat16 [32, 2048, 768], P('fsdp'), may hold values from -0.125 to 0.125
- w_down: bfloat16 [32, 768, 2048], P('fsdp'), may hold values from -0.21875 to 0.21875
Outputs:
- moe_out: bfloat16 [98304, 2048], P(('dp', 'fsdp'))
- router_grad: float32 [128, 2048], P('fsdp')
Inputs may be any that keep to these rules, and one draw needn't show every extreme that they name: `route_ids`: each row names 8 different experts; in the rows of one device (aligned blocks of 128 rows) no expert is named more than 12 times. flows[r, j] live tokens pass from data rank r to rank (r + 1) mod 24 in fsdp column j; a negative entry passes -flows[r, j] tokens from rank (r + 1) mod 24 to rank r. Both 32 and -32 occur.
All inputs are finite; a program needn't handle non-finite values.
Results may differ from a plain program's by a relative error of at most 0.0057.
Values may be sent and summed in bfloat16 or wider, within the bound.
No kernel may reach another device: no remote copies, remote signals or barrier semaphores. Data moves between devices by JAX's collectives and lax.ppermute only.
A program may use at most 64 MiB of HBM per device.

v0:
```python
import jax
import jax.numpy as jnp
from jax import lax
from jax.sharding import PartitionSpec as P

D = 2048
EXPERTS = 128
TOK_DEV = 128
MOVE = 32
CAP = 12


def extended(cells, sides, width):
    for axis, dim in sides:
        count = lax.axis_size(axis)
        head = lax.slice_in_dim(cells, 0, width, axis=dim)
        tail = lax.slice_in_dim(cells, cells.shape[dim] - width, cells.shape[dim], axis=dim)
        cells = jnp.concatenate(
            [
                lax.ppermute(tail, axis, [(i, (i + 1) % count) for i in range(count)]),
                cells,
                lax.ppermute(head, axis, [((i + 1) % count, i) for i in range(count)]),
            ],
            axis=dim,
        )
    return cells


def arrange(chosen, experts_here):
    member = chosen[:, :, None] == jnp.arange(experts_here, dtype=jnp.int32)[None, None, :]
    picked = jnp.any(member, axis=1).astype(jnp.int32)
    slot_order = jnp.cumsum(picked, axis=0, dtype=jnp.int32) - 1
    slot_place = (picked[:, :, None] == 1) & (
        slot_order[:, :, None] == jnp.arange(CAP, dtype=jnp.int32)[None, None, :]
    )
    return (slot_order, slot_place)


def dispatch_rows(token_block, chosen, experts_here):
    slot_place = arrange(chosen, experts_here)[1]
    place_matrix = slot_place.reshape(TOK_DEV, experts_here * CAP).astype(jnp.bfloat16)
    gathered = jnp.dot(place_matrix.T, token_block, preferred_element_type=jnp.float32)
    return gathered.astype(jnp.bfloat16).reshape(experts_here, CAP, D)


def expert_apply(slot_rows, gate_matrix, up_matrix, down_matrix):
    gate_act = jnp.dot(slot_rows, gate_matrix, preferred_element_type=jnp.float32)
    up_act = jnp.dot(slot_rows, up_matrix, preferred_element_type=jnp.float32)
    hidden = (jax.nn.silu(gate_act) * up_act).astype(jnp.bfloat16)
    return jnp.dot(hidden, down_matrix, preferred_element_type=jnp.float32).astype(jnp.bfloat16)


def combine(token_block, chosen, logits, cotangent, returned, experts_here):
    slot_order = arrange(chosen, experts_here)[0]
    route_weight = jax.nn.softmax(logits, axis=1)
    clamped = jnp.minimum(chosen, experts_here - 1)
    order_at = jnp.take_along_axis(slot_order, clamped, axis=1)
    inside = chosen < experts_here
    slot_count = experts_here * CAP
    flat_index = jnp.where(inside, clamped * CAP + order_at, slot_count)
    slot_table = returned.reshape(slot_count, D)
    columns = jnp.arange(slot_count, dtype=jnp.int32)
    pick = (flat_index[:, :, None] == columns[None, None, :]).astype(jnp.float32)
    weight_matrix = jnp.sum(route_weight[:, :, None] * pick, axis=1)
    layer_out = jnp.dot(
        weight_matrix, slot_table.astype(jnp.float32), precision=lax.Precision.HIGHEST
    ).astype(jnp.bfloat16)
    slot_scores = jnp.dot(cotangent, slot_table.T, preferred_element_type=jnp.float32)
    slot_scores = jnp.concatenate(
        [slot_scores, jnp.zeros((slot_scores.shape[0], 1), jnp.float32)], axis=1
    )
    scores = jnp.take_along_axis(slot_scores, flat_index, axis=1)
    logit_grad = route_weight * (scores - jnp.sum(route_weight * scores, axis=1, keepdims=True))
    one_hot = (chosen[:, :, None] == jnp.arange(EXPERTS, dtype=jnp.int32)[None, None, :]).astype(
        jnp.float32
    )
    expert_grad = jnp.sum(logit_grad[:, :, None] * one_hot, axis=1)
    router_term = jnp.dot(
        expert_grad.T, token_block.astype(jnp.float32), precision=lax.Precision.HIGHEST
    )
    return (layer_out, router_term)


def settle(held, left_edge, right_edge, live_count, left_flow):
    sectioning = jnp.concatenate([left_edge, held, jnp.zeros((MOVE, D), jnp.bfloat16)], axis=0)
    sectioning = lax.dynamic_update_slice_in_dim(sectioning, right_edge, MOVE + live_count, 0)
    return lax.dynamic_slice_in_dim(sectioning, MOVE - left_flow, TOK_DEV, 0)


def shards(rollout, flows, route_ids, route_logits, grad_out, w_gate, w_up, w_down):
    data_rank = lax.axis_index("dp")
    data_ranks = lax.axis_size("dp")
    own_flow = flows[data_rank, 0]
    left_flow = flows[(data_rank + data_ranks - 1) % data_ranks, 0]
    live_count = TOK_DEV + own_flow - left_flow
    head_rows = rollout[:MOVE]
    tail_rows = lax.dynamic_slice_in_dim(rollout, live_count - MOVE, MOVE, 0)
    border = extended(jnp.concatenate([head_rows, tail_rows], axis=0), (("dp", 0),), MOVE)
    balanced = settle(rollout, border[:MOVE], border[3 * MOVE :], live_count, left_flow)
    experts_here = lax.axis_size("fsdp")
    outgoing = dispatch_rows(balanced, route_ids, experts_here)
    slot_rows = lax.all_to_all(outgoing, "fsdp", split_axis=0, concat_axis=0, tiled=True)
    sources = slot_rows.shape[0]
    slot_count = slot_rows.shape[1]
    computed = expert_apply(
        slot_rows.reshape(sources * slot_count, D), w_gate[0], w_up[0], w_down[0]
    )
    returned = lax.all_to_all(
        computed.reshape(sources, slot_count, D), "fsdp", split_axis=0, concat_axis=0, tiled=True
    )
    layer_out, router_term = combine(
        balanced, route_ids, route_logits, grad_out, returned, experts_here
    )
    rows_here = EXPERTS // experts_here
    summed = lax.psum(router_term, ("dp", "fsdp"))
    router_grad = lax.dynamic_slice_in_dim(summed, lax.axis_index("fsdp") * rows_here, rows_here, 0)
    return (layer_out, router_grad)


def solution(mesh):
    return jax.shard_map(
        shards,
        mesh=mesh,
        in_specs=(
            P(("dp", "fsdp"), None),
            P(None, "fsdp"),
            P(("dp", "fsdp"), None),
            P(("dp", "fsdp"), None),
            P(("dp", "fsdp"), None),
            P("fsdp", None, None),
            P("fsdp", None, None),
            P("fsdp", None, None),
        ),
        out_specs=(P(("dp", "fsdp"), None), P("fsdp", None)),
        check_vma=False,
    )
```

profile of v0, /device:TPU:28, one launch (start us, length us, event | category | flops | bytes accessed | tf_op | source)
XLA Modules:
  0.0 669.8 jit_solution(3491359950943383464)
XLA Ops:
  7.2 0.0 copy-start
  7.2 1.4 constant_dynamic-slice_fusion.2
  9.9 1.7 fusion.31
  11.6 4.3 collective-permute-start
  15.9 12.1 %collective-permute-start.1 = (bf16[32,2048]{1,0:T(8,128)(2,1)}, bf16[32,2048]{1,0:T(8,128)(2,1)}, u32[]{:S(2)}, u32[]{:S(2)}) collective-permute-start(bf16[32,2048]{1,0:T(8,128)(2,1)} %get-tuple-element.6), channel_id=1, source_target_pairs={{32,0},{64,32},{96,64},{128,96},{160,128},{192,160},{224,192},{256... | collective-permute-start | bytes 393224 | tf_op jit(solution)/shard_map/ppermute | solution.py:22
  29.3 0.7 fusion.23
  30.1 0.1 copy.34
  30.2 0.2 reduce_window_sum.12
  30.3 0.1 copy.39
  30.4 0.7 eq.88
  31.1 0.0 copy-start.1
  31.2 0.1 eq.90
  31.3 0.1 pad.3.clone
  31.4 0.0 collective-permute-done
  31.4 2.4 maximum_maximum_fusion
  33.8 0.0 collective-permute-done.1
  33.8 1.8 dynamic_update_slice.3
  35.6 0.0 copy-done.1
  35.6 2.8 convolution_convert_fusion
  38.4 3.6 reshape.69
  42.0 58.7 %all_to_all.10 = bf16[32,12,2048]{2,1,0:T(8,128)(2,1)} all-to-all(bf16[32,12,2048]{2,1,0:T(8,128)(2,1)} %reshape.69), channel_id=1, replica_groups=mesh['dp'=24,'fsdp'=32] {'fsdp'}, dimensions={0} | all-to-all | bytes 3145728 | tf_op jit(solution)/shard_map/all_to_all | solution.py:102
  100.8 3.6 reshape.70
  104.4 4.8 fusion.4
  109.2 0.0 copy-done
  109.2 6.9 %fusion.6 = bf16[384,2048]{1,0:T(8,128)(2,1)} fusion(bf16[1,768,2048]{2,1,0:T(8,128)(2,1)S(1)} %copy-done, bf16[384,2048]{1,0:T(8,128)(2,1)} %reshape.70, bf16[1,2048,768]{2,1,0:T(8,128)(2,1)} %param.14, f32[384,768]{1,0:T(8,128)} %fusion.4), kind=kOutput, calls=%fused_computation.8 | convolution fusion | flops 2418475008 | bytes 10616832 | tf_op jit(solution)/shard_map/dot_general | solution.py:50
  116.1 3.6 reshape.71
  119.7 0.0 copy-start.2
  119.7 8.5 %all-to-all-start.1 = ((bf16[32,12,2048]{2,1,0:T(8,128)(2,1)}), bf16[32,12,2048]{2,1,0:T(8,128)(2,1)}, u32[]{:S(2)}, u32[]{:S(2)}) async-start(bf16[32,12,2048]{2,1,0:T(8,128)(2,1)} %reshape.71), calls=%async_computation.1 | async-start | bytes 4194304 | tf_op jit(solution)/shard_map/all_to_all | solution.py:108
  128.2 0.0 all-reduce.3.cloned.1.call-start
  128.3 0.0 copy-done.2
  128.3 0.1 copy.40
  128.4 0.1 copy.35
  128.5 0.1 reshape.74
  128.6 0.0 copy-start.3
  128.6 7.1 %gather_fusion = s32[1024]{0:T(1024)S(1)} fusion(s32[128,32]{1,0:T(8,128)S(1)} %broadcast_add_fusion, s32[1024]{0:T(1024)S(1)} %reshape.74), kind=kCustom, calls=%fused_computation | custom fusion | bytes 16384 | tf_op jit(solution)/shard_map/jit(take_along_axis)/gather | solution.py:57
  135.7 0.1 reshape.77
  135.9 0.1 copy.41
  136.0 0.1 reshape.80
  136.1 0.0 copy-done.3
  136.1 40.6 %all-to-all-done.1 = bf16[32,12,2048]{2,1,0:T(8,128)(2,1)} async-done(((bf16[32,12,2048]{2,1,0:T(8,128)(2,1)}), bf16[32,12,2048]{2,1,0:T(8,128)(2,1)}, u32[]{:S(2)}, u32[]{:S(2)}) %all-to-all-start.1) | async-done | bytes 1572896 | tf_op jit(solution)/shard_map/all_to_all | solution.py:108
  176.7 3.6 reshape.72
  180.3 2.1 convolution_bitcast_fusion
  182.4 7.0 %gather_fusion.1 = f32[1024]{0:T(1024)S(1)} fusion(f32[128,385]{0,1:T(8,128)S(1)} %concatenate.7, s32[1024]{0:T(1024)S(1)} %reshape.80), kind=kCustom, calls=%fused_computation.1 | custom fusion | bytes 16384 | tf_op jit(solution)/shard_map/jit(take_along_axis)/gather | solution.py:72
  189.4 0.1 reshape.83
  189.6 0.1 copy.43
  189.7 0.3 select_reduce_fusion.1
  190.1 2.7 fusion.18
  192.7 0.0 all-reduce.3.cloned.1.call-update
  192.8 0.1 copy.37
  192.9 0.1 copy.38
  193.0 0.5 select_reduce_fusion
  193.5 3.2 convolution_convert_fusion.1
  196.7 464.7 %all-reduce.3.cloned.1.call-done = f32[128,2048]{1,0:T(8,128)} async-done(((f32[128,2048]{1,0:T(8,128)}), f32[128,2048]{1,0:T(8,128)}) %all-reduce.3.cloned.1.call-update) | async-done | bytes 1048592 | tf_op jit(solution)/shard_map/psum | solution.py:115
  661.5 1.5 constant_dynamic-slice_fusion
  (16 shorter events, 0.4 us)
Async XLA Ops:
  7.2 102.0 %copy-start = (bf16[1,768,2048]{2,1,0:T(8,128)(2,1)S(1)}, bf16[1,768,2048]{2,1,0:T(8,128)(2,1)}, u32[]{:S(2)}) copy-start(bf16[1,768,2048]{2,1,0:T(8,128)(2,1)} %param.15) | copy-start | bytes 9437188
  11.6 19.8 %collective-permute-start = (bf16[32,2048]{1,0:T(8,128)(2,1)}, bf16[32,2048]{1,0:T(8,128)(2,1)}, u32[]{:S(2)}, u32[]{:S(2)}) collective-permute-start(bf16[32,2048]{1,0:T(8,128)(2,1)} %get-tuple-element.7), channel_id=1, source_target_pairs={{0,32},{32,64},{64,96},{96,128},{128,160},{160,192},{192,224},{224... | collective-permute-start | bytes 393224 | tf_op jit(solution)/shard_map/ppermute | solution.py:20
  15.9 17.9 %collective-permute-start.1 = (bf16[32,2048]{1,0:T(8,128)(2,1)}, bf16[32,2048]{1,0:T(8,128)(2,1)}, u32[]{:S(2)}, u32[]{:S(2)}) collective-permute-start(bf16[32,2048]{1,0:T(8,128)(2,1)} %get-tuple-element.6), channel_id=1, source_target_pairs={{32,0},{64,32},{96,64},{128,96},{160,128},{192,160},{224,192},{256... | collective-permute-start | bytes 393224 | tf_op jit(solution)/shard_map/ppermute | solution.py:22
  31.1 4.5 copy-start.1
  119.7 8.6 %copy-start.2 = (s32[128,8]{0,1:T(8,128)S(1)}, s32[128,8]{0,1:T(8,128)}, u32[]{:S(2)}) copy-start(s32[128,8]{0,1:T(8,128)} %param.10) | copy-start | bytes 12292
  119.7 57.0 %all-to-all-start.1 = ((bf16[32,12,2048]{2,1,0:T(8,128)(2,1)}), bf16[32,12,2048]{2,1,0:T(8,128)(2,1)}, u32[]{:S(2)}, u32[]{:S(2)}) async-start(bf16[32,12,2048]{2,1,0:T(8,128)(2,1)} %reshape.71), calls=%async_computation.1 | async-start | bytes 4194304 | tf_op jit(solution)/shard_map/all_to_all | solution.py:108
  128.2 533.2 %all-reduce.3.cloned.1.call-start = ((), (), s32[]{:S(2)}) async-start(), calls=%async_computation.2 | async-start | bytes 2097152 | tf_op jit(solution)/shard_map/psum | solution.py:115
  128.6 7.5 %copy-start.3 = (f32[128,8]{0,1:T(8,128)S(1)}, f32[128,8]{0,1:T(8,128)}, u32[]{:S(2)}) copy-start(f32[128,8]{0,1:T(8,128)} %param.11) | copy-start | bytes 12292
Sparse Core Ops, SparseCore 0:
  192.9 468.5 all-reduce.2
where the time goes:
time: 671 us; the launch traced here: 670 us
  waiting for transfers between devices  505 us (75%)
  blocking collectives  58.7 us (9%)
  local copies, waits for them, and re-layouts  37.2 us (6%)
  starting transfers between devices  25 us (4%)
  matrix products  22.4 us (3%)
  between operations  16.9 us (3%)
    psum x1, waiting for transfers between devices, shards(): summed = lax.psum(router_term, ('dp', 'fsdp'))  465 us
    all_to_all x1, blocking collectives, shards(): lax.all_to_all(outgoing, 'fsdp', split_axis=0, concat_axis=0, tiled=True)  58.7 us
    all_to_all x1, waiting for transfers between devices, shards(): lax.all_to_all(computed.reshape(sources, slot_count, D), 'fsdp', split_ax...  40.6 us
  transfers between devices with their start and end apart: 4, of which 2 were waited for; matrix products, arithmetic and copies ran while one was open for 2% of the time, Pallas kernels for 0%

commit v1 on v0

--- a/solution.py
+++ b/solution.py
@@ -1,6 +1,7 @@
 import jax
 import jax.numpy as jnp
 from jax import lax
+from jax.sharding import Mesh
 from jax.sharding import PartitionSpec as P
 
 D = 2048
@@ -8,6 +9,7 @@
 TOK_DEV = 128
 MOVE = 32
 CAP = 12
+DP = ("yl", "z")
 
 
 def extended(cells, sides, width):
@@ -87,15 +89,28 @@
     return lax.dynamic_slice_in_dim(sectioning, MOVE - left_flow, TOK_DEV, 0)
 
 
+def exchange(blocks, axes):
+    return lax.all_to_all(blocks, axes, split_axis=0, concat_axis=0, tiled=True)
+
+
+def router_sum(router_term):
+    blocks = router_term.reshape(32, 4, 2, 2, 512).transpose(2, 0, 3, 1, 4).reshape(64, 8, 512)
+    terms = exchange(blocks.astype(jnp.bfloat16), ("yl", "fsdp"))
+    part = jnp.sum(terms.astype(jnp.float32), axis=0).astype(jnp.bfloat16)
+    parts = exchange(jnp.broadcast_to(part[None], (24, 8, 512)), ("yl", "z"))
+    halves = jnp.sum(parts.astype(jnp.float32).reshape(2, 12, 2, 4, 512), axis=1)
+    return halves.transpose(2, 0, 1, 3).reshape(4, D)
+
+
 def shards(rollout, flows, route_ids, route_logits, grad_out, w_gate, w_up, w_down):
-    data_rank = lax.axis_index("dp")
-    data_ranks = lax.axis_size("dp")
+    data_rank = lax.axis_index(DP)
+    data_ranks = lax.axis_size(DP)
     own_flow = flows[data_rank, 0]
     left_flow = flows[(data_rank + data_ranks - 1) % data_ranks, 0]
     live_count = TOK_DEV + own_flow - left_flow
     head_rows = rollout[:MOVE]
     tail_rows = lax.dynamic_slice_in_dim(rollout, live_count - MOVE, MOVE, 0)
-    border = extended(jnp.concatenate([head_rows, tail_rows], axis=0), (("dp", 0),), MOVE)
+    border = extended(jnp.concatenate([head_rows, tail_rows], axis=0), ((DP, 0),), MOVE)
     balanced = settle(rollout, border[:MOVE], border[3 * MOVE :], live_count, left_flow)
     experts_here = lax.axis_size("fsdp")
     outgoing = dispatch_rows(balanced, route_ids, experts_here)
@@ -111,26 +126,26 @@
     layer_out, router_term = combine(
         balanced, route_ids, route_logits, grad_out, returned, experts_here
     )
-    rows_here = EXPERTS // experts_here
-    summed = lax.psum(router_term, ("dp", "fsdp"))
-    router_grad = lax.dynamic_slice_in_dim(summed, lax.axis_index("fsdp") * rows_here, rows_here, 0)
+    router_grad = router_sum(router_term)
     return (layer_out, router_grad)
 
 
 def solution(mesh):
+    fine = Mesh(mesh.devices.reshape(2, 12, 32), ("yl", "z", "fsdp"))
+    rows = P(("yl", "z", "fsdp"), None)
     return jax.shard_map(
         shards,
-        mesh=mesh,
+        mesh=fine,
         in_specs=(
-            P(("dp", "fsdp"), None),
+            rows,
             P(None, "fsdp"),
-            P(("dp", "fsdp"), None),
-            P(("dp", "fsdp"), None),
-            P(("dp", "fsdp"), None),
+            rows,
+            rows,
+            rows,
             P("fsdp", None, None),
             P("fsdp", None, None),
             P("fsdp", None, None),
         ),
-        out_specs=(P(("dp", "fsdp"), None), P("fsdp", None)),
+        out_specs=(rows, P("fsdp", None)),
         check_vma=False,
     )

time: 671 us -> 240 us (0.36)
  the two profiles are of different devices: /device:TPU:28 before, /device:TPU:2 now
where the time goes in v1:
time: 240 us; the launch traced here: 239 us
  blocking collectives  87 us (36%)
  waiting for transfers between devices  42 us (18%)
  local copies, waits for them, and re-layouts  41.9 us (17%)
  starting transfers between devices  37 us (15%)
  matrix products  21.4 us (9%)
  other arithmetic  6.09 us (3%)
  between operations  3.51 us (1%)
    all_to_all x1, blocking collectives, shards(): lax.all_to_all(outgoing, 'fsdp', split_axis=0, concat_axis=0, tiled=True)  50.9 us
    all_to_all x1, blocking collectives, exchange(): return lax.all_to_all(blocks, axes, split_axis=0, concat_axis=0, tiled=True)  36.1 us
    all_to_all x1, waiting for transfers between devices, shards(): lax.all_to_all(computed.reshape(sources, slot_count, D), 'fsdp', split_ax...  28.1 us
    ppermute x1, starting transfers between devices, extended(): lax.ppermute(head, axis, [((i + 1) % count, i) for i in range(count)])  15.6 us
    all_to_all x1, starting transfers between devices, shards(): lax.all_to_all(computed.reshape(sources, slot_count, D), 'fsdp', split_ax...  15 us
    all_to_all x1, waiting for transfers between devices, exchange(): return lax.all_to_all(blocks, axes, split_axis=0, concat_axis=0, tiled=True)  9.88 us
    gather x5, local copies, waits for them, and re-layouts, combine(): order_at = jnp.take_along_axis(slot_order, clamped, axis=1)  7.39 us
    gather x5, local copies, waits for them, and re-layouts, combine(): scores = jnp.take_along_axis(slot_scores, flat_index, axis=1)  7.34 us
  transfers between devices with their start and end apart: 4, of which 3 were waited for; matrix products, arithmetic and copies ran while one was open for 8% of the time, Pallas kernels for 0%

profile of v1, /device:TPU:2, one launch (start us, length us, event | category | flops | bytes accessed | tf_op | source)
XLA Modules:
  0.0 238.9 jit_solution(5127752951345898045)
XLA Ops:
  0.6 0.0 copy-start
  0.7 1.4 constant_dynamic-slice_fusion.1
  3.4 1.7 fusion.30
  5.1 15.6 %collective-permute-start.1 = (bf16[32,2048]{1,0:T(8,128)(2,1)}, bf16[32,2048]{1,0:T(8,128)(2,1)}, u32[]{:S(2)}, u32[]{:S(2)}) collective-permute-start(bf16[32,2048]{1,0:T(8,128)(2,1)} %get-tuple-element.6), channel_id=1, source_target_pairs={{32,0},{64,32},{96,64},{128,96},{160,128},{192,160},{224,192},{256... | collective-permute-start | bytes 393224 | tf_op jit(solution)/shard_map/ppermute | solution.py:24
  20.7 1.9 collective-permute-start
  23.9 0.7 fusion.22
  24.6 0.1 eq.90
  24.8 0.1 copy.57
  24.9 0.2 reduce_window_sum.12
  25.0 0.1 copy.62
  25.2 0.7 eq.88
  25.9 0.0 copy-start.1
  25.9 0.1 pad.3.clone
  26.0 4.0 %collective-permute-done = bf16[32,2048]{1,0:T(8,128)(2,1)} collective-permute-done((bf16[32,2048]{1,0:T(8,128)(2,1)}, bf16[32,2048]{1,0:T(8,128)(2,1)}, u32[]{:S(2)}, u32[]{:S(2)}) %collective-permute-start) | collective-permute-done | bytes 131104 | tf_op jit(solution)/shard_map/ppermute | solution.py:22
  30.0 2.4 maximum_maximum_fusion
  32.3 0.0 collective-permute-done.1
  32.3 1.8 dynamic_update_slice.3
  34.2 0.0 copy-done.1
  34.2 2.8 %convolution_convert_fusion = bf16[384,2048]{1,0:T(8,128)(2,1)} fusion(bf16[256,2048]{1,0:T(8,128)(2,1)} %dynamic_update_slice.3, s32[]{:T(128)S(6)} %select_n.50, pred[128,384]{0,1:T(32,128)(4,1)S(1)} %and.28, s32[128,384]{0,1:T(8,128)S(1)} %copy-done.1, s32[384]{0:T(512)S(1)} %eq.90), kind=kOutput, calls=%fused_computation.9 | convolution fusion | flops 202211328 | bytes 2344452 | tf_op jit(solution)/shard_map/dot_general | solution.py:44
  37.0 3.6 %reshape.84 = bf16[32,12,2048]{2,1,0:T(8,128)(2,1)} reshape(bf16[384,2048]{1,0:T(8,128)(2,1)} %convolution_convert_fusion) | data formatting | bytes 3145728 | tf_op jit(solution)/shard_map/reshape | solution.py:45
  40.6 50.9 %all_to_all.20 = bf16[32,12,2048]{2,1,0:T(8,128)(2,1)} all-to-all(bf16[32,12,2048]{2,1,0:T(8,128)(2,1)} %reshape.84), channel_id=1, replica_groups=mesh['yl'=2,'z'=12,'fsdp'=32] {'fsdp'}, dimensions={0} | all-to-all | bytes 3145728 | tf_op jit(solution)/shard_map/all_to_all | solution.py:117
  91.5 3.6 %reshape.85 = bf16[384,2048]{1,0:T(8,128)(2,1)} reshape(bf16[32,12,2048]{2,1,0:T(8,128)(2,1)} %all_to_all.20) | data formatting | bytes 3145728 | tf_op jit(solution)/shard_map/reshape | solution.py:121
  95.2 4.8 %fusion.4 = f32[384,768]{1,0:T(8,128)} fusion(bf16[384,2048]{1,0:T(8,128)(2,1)} %reshape.85, bf16[1,2048,768]{2,1,0:T(8,128)(2,1)} %param.13), kind=kOutput, calls=%fused_computation.6 | convolution fusion | flops 1207959552 | bytes 5898240 | tf_op jit(solution)/shard_map/dot_general | solution.py:49
  99.9 0.0 copy-done
  99.9 6.9 %fusion.6 = bf16[384,2048]{1,0:T(8,128)(2,1)} fusion(bf16[1,768,2048]{2,1,0:T(8,128)(2,1)S(1)} %copy-done, bf16[384,2048]{1,0:T(8,128)(2,1)} %reshape.85, bf16[1,2048,768]{2,1,0:T(8,128)(2,1)} %param.14, f32[384,768]{1,0:T(8,128)} %fusion.4), kind=kOutput, calls=%fused_computation.8 | convolution fusion | flops 2418475008 | bytes 10616832 | tf_op jit(solution)/shard_map/dot_general | solution.py:52
  106.9 3.6 %reshape.86 = bf16[32,12,2048]{2,1,0:T(8,128)(2,1)} reshape(bf16[384,2048]{1,0:T(8,128)(2,1)} %fusion.6) | data formatting | bytes 3145728 | tf_op jit(solution)/shard_map/reshape | solution.py:124
  110.4 0.0 copy-start.2
  110.5 15.0 %all-to-all-start.1 = ((bf16[32,12,2048]{2,1,0:T(8,128)(2,1)}), bf16[32,12,2048]{2,1,0:T(8,128)(2,1)}, u32[]{:S(2)}, u32[]{:S(2)}) async-start(bf16[32,12,2048]{2,1,0:T(8,128)(2,1)} %reshape.86), calls=%async_computation.1 | async-start | bytes 4194304 | tf_op jit(solution)/shard_map/all_to_all | solution.py:123
  125.4 0.0 copy-done.2
  125.4 0.1 copy.63
  125.6 0.1 copy.58
  125.7 0.1 reshape.94
  125.8 0.0 copy-start.3
  125.8 7.1 %gather_fusion = s32[1024]{0:T(1024)S(1)} fusion(s32[128,32]{1,0:T(8,128)S(1)} %broadcast_add_fusion, s32[1024]{0:T(1024)S(1)} %reshape.94), kind=kCustom, calls=%fused_computation | custom fusion | bytes 16384 | tf_op jit(solution)/shard_map/jit(take_along_axis)/gather | solution.py:59
  132.8 0.1 reshape.97
  133.0 0.1 copy.64
  133.1 0.1 reshape.100
  133.2 0.0 copy-done.3
  133.3 2.0 dynamic-slice_bitcast_fusion
  135.3 2.0 copy.68
  137.3 28.1 %all-to-all-done.1 = bf16[32,12,2048]{2,1,0:T(8,128)(2,1)} async-done(((bf16[32,12,2048]{2,1,0:T(8,128)(2,1)}), bf16[32,12,2048]{2,1,0:T(8,128)(2,1)}, u32[]{:S(2)}, u32[]{:S(2)}) %all-to-all-start.1) | async-done | bytes 1572896 | tf_op jit(solution)/shard_map/all_to_all | solution.py:123
  165.4 3.6 %reshape.87 = bf16[384,2048]{1,0:T(8,128)(2,1)} reshape(bf16[32,12,2048]{2,1,0:T(8,128)(2,1)} %all-to-all-done.1) | data formatting | bytes 3145728 | tf_op jit(solution)/shard_map/reshape | solution.py:63
  169.0 2.1 convolution_bitcast_fusion
  171.2 7.0 %gather_fusion.1 = f32[1024]{0:T(1024)S(1)} fusion(f32[128,385]{0,1:T(8,128)S(1)} %concatenate.7, s32[1024]{0:T(1024)S(1)} %reshape.100), kind=kCustom, calls=%fused_computation.1 | custom fusion | bytes 16384 | tf_op jit(solution)/shard_map/jit(take_along_axis)/gather | solution.py:74
  178.2 0.1 reshape.103
  178.4 0.1 copy.66
  178.5 0.3 select_reduce_fusion.1
  178.8 0.1 copy.67
  178.9 1.6 fusion.15
  180.6 0.3 copy.71
  180.9 36.1 %all_to_all.21 = bf16[64,8,512]{2,1,0:T(8,128)(2,1)} all-to-all(bf16[64,8,512]{2,1,0:T(8,128)(2,1)S(1)} %copy.71), channel_id=1, replica_groups=mesh['yl'=2,'z'=12,'fsdp'=32] {'yl','fsdp'}, dimensions={0} | all-to-all | bytes 1048576 | tf_op jit(solution)/shard_map/all_to_all | solution.py:93
  217.0 1.1 reduce_sum.61
  218.2 0.7 broadcast_in_dim.20
  218.9 4.5 %all-to-all-start.3 = ((bf16[24,8,512]{2,1,0:T(8,128)(2,1)}), bf16[24,8,512]{2,1,0:T(8,128)(2,1)}, u32[]{:S(2)}, u32[]{:S(2)}) async-start(bf16[24,8,512]{2,1,0:T(8,128)(2,1)} %broadcast_in_dim.20), calls=%async_computation.3 | async-start | bytes 393216 | tf_op jit(solution)/shard_map/all_to_all | solution.py:93
  223.4 0.1 copy.60
  223.5 0.1 copy.61
  223.6 0.5 select_reduce_fusion
  224.1 3.2 %convolution_convert_fusion.1 = bf16[128,2048]{1,0:T(8,128)(2,1)} fusion(f32[128,384]{1,0:T(8,128)S(1)} %select_reduce_fusion, bf16[384,2048]{1,0:T(8,128)(2,1)} %reshape.87), kind=kOutput, calls=%fused_computation.10 | convolution fusion | flops 1208221696 | bytes 2293760 | tf_op jit(solution)/shard_map/dot_general | solution.py:67
  227.3 9.9 %all-to-all-done.3 = bf16[24,8,512]{2,1,0:T(8,128)(2,1)} async-done(((bf16[24,8,512]{2,1,0:T(8,128)(2,1)}), bf16[24,8,512]{2,1,0:T(8,128)(2,1)}, u32[]{:S(2)}, u32[]{:S(2)}) %all-to-all-start.3) | async-done | bytes 196640 | tf_op jit(solution)/shard_map/all_to_all | solution.py:93
  237.2 1.1 reshape.93
  238.3 0.7 reduce_sum.62
  (17 shorter events, 0.4 us)
Async XLA Ops:
  0.6 99.3 %copy-start = (bf16[1,768,2048]{2,1,0:T(8,128)(2,1)S(1)}, bf16[1,768,2048]{2,1,0:T(8,128)(2,1)}, u32[]{:S(2)}) copy-start(bf16[1,768,2048]{2,1,0:T(8,128)(2,1)} %param.15) | copy-start | bytes 9437188
  5.1 27.2 %collective-permute-start.1 = (bf16[32,2048]{1,0:T(8,128)(2,1)}, bf16[32,2048]{1,0:T(8,128)(2,1)}, u32[]{:S(2)}, u32[]{:S(2)}) collective-permute-start(bf16[32,2048]{1,0:T(8,128)(2,1)} %get-tuple-element.6), channel_id=1, source_target_pairs={{32,0},{64,32},{96,64},{128,96},{160,128},{192,160},{224,192},{256... | collective-permute-start | bytes 393224 | tf_op jit(solution)/shard_map/ppermute | solution.py:24
  20.7 9.3 %collective-permute-start = (bf16[32,2048]{1,0:T(8,128)(2,1)}, bf16[32,2048]{1,0:T(8,128)(2,1)}, u32[]{:S(2)}, u32[]{:S(2)}) collective-permute-start(bf16[32,2048]{1,0:T(8,128)(2,1)} %get-tuple-element.7), channel_id=1, source_target_pairs={{0,32},{32,64},{64,96},{96,128},{128,160},{160,192},{192,224},{224... | collective-permute-start | bytes 393224 | tf_op jit(solution)/shard_map/ppermute | solution.py:22
  25.9 8.3 %copy-start.1 = (s32[128,384]{0,1:T(8,128)S(1)}, s32[128,384]{0,1:T(8,128)}, u32[]{:S(2)}) copy-start(s32[128,384]{0,1:T(8,128)} %eq.88) | copy-start | bytes 589828
  110.4 15.0 %copy-start.2 = (s32[128,8]{0,1:T(8,128)S(1)}, s32[128,8]{0,1:T(8,128)}, u32[]{:S(2)}) copy-start(s32[128,8]{0,1:T(8,128)} %param.10) | copy-start | bytes 12292
  110.5 55.0 %all-to-all-start.1 = ((bf16[32,12,2048]{2,1,0:T(8,128)(2,1)}), bf16[32,12,2048]{2,1,0:T(8,128)(2,1)}, u32[]{:S(2)}, u32[]{:S(2)}) async-start(bf16[32,12,2048]{2,1,0:T(8,128)(2,1)} %reshape.86), calls=%async_computation.1 | async-start | bytes 4194304 | tf_op jit(solution)/shard_map/all_to_all | solution.py:123
  125.8 7.5 %copy-start.3 = (f32[128,8]{0,1:T(8,128)S(1)}, f32[128,8]{0,1:T(8,128)}, u32[]{:S(2)}) copy-start(f32[128,8]{0,1:T(8,128)} %param.11) | copy-start | bytes 12292
  218.9 18.3 %all-to-all-start.3 = ((bf16[24,8,512]{2,1,0:T(8,128)(2,1)}), bf16[24,8,512]{2,1,0:T(8,128)(2,1)}, u32[]{:S(2)}, u32[]{:S(2)}) async-start(bf16[24,8,512]{2,1,0:T(8,128)(2,1)} %broadcast_in_dim.20), calls=%async_computation.3 | async-start | bytes 393216 | tf_op jit(solution)/shard_map/all_to_all | solution.py:93

commit v2 on v1

v2 whole, which is shorter than its diff:
```python
import jax
import jax.numpy as jnp
from jax import lax
from jax.experimental import pallas as pl
from jax.experimental.pallas import tpu as pltpu
from jax.sharding import Mesh
from jax.sharding import PartitionSpec as P

D = 2048
HALF = D // 2
QUARTER = D // 4
FF = 768
EXPERTS = 128
WIN = 32
TOPK = 8
TOK_DEV = 128
SRC_DEV = 192
MOVE = 32
CAP = 12
PAIR = 2 * CAP
ROWS = WIN * PAIR
SLOTS = WIN * CAP
BLOCK = 8 * PAIR
DP = ("yl", "z")
FF_CHUNK = 256
bf16, f32, i32 = jnp.bfloat16, jnp.float32, jnp.int32
VMEM = pl.BlockSpec(memory_space=pltpu.VMEM)
SMEM = pl.BlockSpec(memory_space=pltpu.SMEM)
ANY = pl.BlockSpec(memory_space=pl.ANY)


def iota(shape, dim):
    return lax.broadcasted_iota(i32, shape, dim)


def mm(a, b):
    return jnp.dot(a, b, preferred_element_type=f32)


def whole_div(v, by):
    return jnp.floor((v.astype(f32) + 0.5) * (1.0 / by)).astype(i32)


def split2(v):
    high = v.astype(bf16)
    return high, (v - high.astype(f32)).astype(bf16)


def call(kernel, outs, in_specs, flops, scratch=(), limit=24 << 20):
    many = isinstance(outs, list)
    nbytes = sum(o.size * o.dtype.itemsize for o in (outs if many else [outs]))
    return pl.pallas_call(
        kernel,
        out_shape=outs,
        in_specs=in_specs,
        out_specs=[VMEM] * len(outs) if many else VMEM,
        scratch_shapes=list(scratch),
        cost_estimate=pl.CostEstimate(
            flops=flops, bytes_accessed=2 * nbytes, transcendentals=0
        ),
        compiler_params=pltpu.CompilerParams(vmem_limit_bytes=limit),
    )


def live_of(rank_ref, flows_ref):
    rank = rank_ref[0]
    own = flows_ref[0, rank]
    left = flows_ref[0, jnp.where(rank == 0, 23, rank - 1)]
    return left, TOK_DEV + own - left


def border_kernel(rank_ref, flows_ref, rollout_ref, head_ref, tail_ref):
    _, live = live_of(rank_ref, flows_ref)
    at = iota((MOVE, SRC_DEV), 0) + (live - MOVE)
    pick = (iota((MOVE, SRC_DEV), 1) == at).astype(bf16)
    head_ref[...] = rollout_ref[:MOVE, :]
    tail_ref[...] = mm(pick, rollout_ref[...]).astype(bf16)


def route_kernel(ids_ref, logits_ref, place_ref, weight_ref, high_ref, low_ref):
    logits = logits_ref[...]
    raised = jnp.exp(logits - jnp.max(logits, axis=0, keepdims=True))
    share = raised / jnp.sum(raised, axis=0, keepdims=True)
    expert = iota((EXPERTS, TOK_DEV), 0)
    weight = jnp.zeros((EXPERTS, TOK_DEV), f32)
    named = jnp.zeros((EXPERTS, TOK_DEV), f32)
    for k in range(TOPK):
        hit = ids_ref[k : k + 1, :] == expert
        weight = jnp.where(hit, share[k : k + 1, :], weight)
        named = jnp.where(hit, 1.0, named)
    weight_ref[...] = weight
    upto = (iota((TOK_DEV, TOK_DEV), 0) <= iota((TOK_DEV, TOK_DEV), 1)).astype(bf16)
    count = mm(named[:WIN].astype(bf16), upto)
    code = jnp.where(named[:WIN] > 0.0, count, 0.0).astype(bf16)
    row, of = iota((ROWS, WIN), 0), iota((ROWS, WIN), 1)
    spread = ((row >= of * PAIR) & (row < of * PAIR + PAIR)).astype(bf16)
    high, low = split2(weight[:WIN])
    rows = iota((ROWS, TOK_DEV), 0)
    within = rows - PAIR * whole_div(rows, PAIR)
    second = within >= CAP
    slot = (within - jnp.where(second, CAP, 0) + 1).astype(f32)
    here = mm(spread, code) == slot
    for half in range(2):
        mine = here & (second == (half == 1))
        cols = slice(half * TOK_DEV, (half + 1) * TOK_DEV)
        place_ref[:, cols] = mine.astype(bf16)
        for part, out in ((high, high_ref), (low, low_ref)):
            out[cols, :] = jnp.where(mine, mm(spread, part), 0.0).T.astype(bf16)


def dispatch_kernel(
    rank_ref, flows_ref, left_ref, right_ref, rollout_ref, place_ref, out_ref, bal_ref
):
    left, live = live_of(rank_ref, flows_ref)
    span = SRC_DEV + 2 * MOVE
    at = iota((TOK_DEV, span), 0) + (MOVE - left)
    at = jnp.where(at < MOVE + live, at, at + (SRC_DEV - live))
    settle = (iota((TOK_DEV, span), 1) == at).astype(bf16)
    for half in range(2):
        cols = slice(half * HALF, (half + 1) * HALF)
        rows = jnp.concatenate(
            [left_ref[:, cols], rollout_ref[:, cols], right_ref[:, cols]], axis=0
        )
        bal_ref[half * TOK_DEV : (half + 1) * TOK_DEV, :] = mm(settle, rows).astype(bf16)
    out_ref[...] = mm(place_ref[...], bal_ref[...]).astype(bf16)


def block_source(shape, dim):
    row = iota(shape, dim)
    half = (row >= 8 * CAP).astype(i32)
    rest = row - half * (8 * CAP)
    source = whole_div(rest, CAP)
    return PAIR * source + CAP * half + (rest - CAP * source)


def ffn_kernel(
    rows_ref, gate_hbm, up_hbm, down_hbm, out_ref, gate, up, down, x, hidden, sems
):
    parts = FF // FF_CHUNK
    copies = []
    for f in range(parts):
        cols = pl.ds(f * FF_CHUNK, FF_CHUNK)
        copies.append(
            (
                pltpu.make_async_copy(gate_hbm.at[0, :, cols], gate.at[f], sems.at[2 * f]),
                pltpu.make_async_copy(up_hbm.at[0, :, cols], up.at[f], sems.at[2 * f + 1]),
            )
        )
        copies[f][0].start()
        copies[f][1].start()
    down_copy = pltpu.make_async_copy(down_hbm.at[0], down, sems.at[2 * parts])
    down_copy.start()
    ordered = (iota((BLOCK, BLOCK), 1) == block_source((BLOCK, BLOCK), 0)).astype(bf16)
    back = (iota((BLOCK, BLOCK), 0) == block_source((BLOCK, BLOCK), 1)).astype(bf16)
    part_rows = BLOCK // 2
    for b in range(ROWS // BLOCK):
        y = mm(ordered, rows_ref[b * BLOCK : (b + 1) * BLOCK, :]).astype(bf16)
        x[b * part_rows : (b + 1) * part_rows, :HALF] = y[:part_rows]
        x[b * part_rows : (b + 1) * part_rows, HALF:] = y[part_rows:]
    for f in range(parts):
        copies[f][0].wait()
        g = mm(x[...], gate[f])
        copies[f][1].wait()
        u = mm(x[...], up[f])
        act = g / (1.0 + jnp.exp(-g)) * u
        hidden[:, f * FF_CHUNK : (f + 1) * FF_CHUNK] = act.astype(bf16)
    down_copy.wait()
    for half in range(2):
        cols = slice(half * HALF, (half + 1) * HALF)
        x[:, cols] = mm(hidden[...], down[:, cols]).astype(bf16)
    for b in range(ROWS // BLOCK):
        mine = slice(b * part_rows, (b + 1) * part_rows)
        y = jnp.concatenate([x[mine, :HALF], x[mine, HALF:]], axis=0)
        out_ref[b * BLOCK : (b + 1) * BLOCK, :] = mm(back, y).astype(bf16)


def terms_kernel(rows_ref, grad_ref, bal_ref, place_ref, weight_ref, out_ref):
    cotangent = jnp.concatenate([grad_ref[:, :HALF], grad_ref[:, HALF:]], axis=0)
    scores = lax.dot_general(
        rows_ref[...], cotangent, (((1,), (1,)), ((), ())), preferred_element_type=f32
    )
    high, low = split2(scores * place_ref[...].astype(f32))
    of, row = iota((WIN, ROWS), 0), iota((WIN, ROWS), 1)
    gather = ((row >= of * PAIR) & (row < of * PAIR + PAIR)).astype(bf16)
    both = mm(gather, high) + mm(gather, low)
    score = both[:, :TOK_DEV] + both[:, TOK_DEV:]
    weight = weight_ref[...]
    total = jnp.sum(weight[:WIN] * score, axis=0, keepdims=True)
    grad = jnp.concatenate(
        [weight[:WIN] * (score - total), weight[WIN:] * (0.0 - total)], axis=0
    )
    high, low = split2(grad)
    line = iota((2 * EXPERTS, EXPERTS), 0)
    order = (iota((2 * EXPERTS, EXPERTS), 1) == (line >> 3) * 4 + (line & 3)).astype(bf16)
    factor = jnp.concatenate(
        [mm(order, high).astype(bf16), mm(order, low).astype(bf16)], axis=1
    )
    first = (iota((2 * EXPERTS, QUARTER), 0) & 4) == 0
    for half in range(2):
        tokens = bal_ref[half * TOK_DEV : (half + 1) * TOK_DEV, :]
        term = mm(factor, jnp.concatenate([tokens, tokens], axis=0))
        out_ref[half * 2 * EXPERTS : (half + 1) * 2 * EXPERTS, :] = jnp.where(
            first, term[:, :QUARTER], term[:, QUARTER:]
        ).astype(bf16)


def output_kernel(rows_ref, high_ref, low_ref, out_ref):
    rows = rows_ref[...]
    both = mm(high_ref[...], rows) + mm(low_ref[...], rows)
    out_ref[:, :HALF] = both[:TOK_DEV].astype(bf16)
    out_ref[:, HALF:] = both[TOK_DEV:].astype(bf16)


def part_kernel(terms_ref, out_ref):
    part = jnp.sum(terms_ref[...].astype(f32).reshape(64, 8, QUARTER), axis=0)
    two = jnp.concatenate([part, part], axis=0).astype(bf16)
    for i in range(12):
        out_ref[16 * i : 16 * (i + 1), :] = two


def last_kernel(parts_ref, out_ref):
    parts = jnp.sum(parts_ref[...].astype(f32).reshape(2, 12, 8, QUARTER), axis=1)
    for half in range(2):
        for quarter in range(2):
            at = half * HALF + quarter * QUARTER
            out_ref[:, at : at + QUARTER] = parts[half, 4 * quarter : 4 * quarter + 4]


def shape(dims, dtype):
    return jax.ShapeDtypeStruct(dims, dtype)


def exchange(blocks, axes, peers):
    rows, cols = blocks.shape
    apart = blocks.reshape(peers, rows // peers, cols)
    return lax.all_to_all(apart, axes, split_axis=0, concat_axis=0, tiled=True).reshape(rows, cols)


def borders(rank, flows, rollout):
    return call(
        border_kernel, [shape((MOVE, D), bf16)] * 2, [SMEM, SMEM, VMEM], 25_000_000
    )(rank, flows, rollout)


def routes(ids, logits):
    return call(
        route_kernel,
        [
            shape((ROWS, 2 * TOK_DEV), bf16),
            shape((EXPERTS, TOK_DEV), f32),
            shape((2 * TOK_DEV, ROWS), bf16),
            shape((2 * TOK_DEV, ROWS), bf16),
        ],
        [VMEM] * 2,
        500_000_000,
    )(ids, logits)


def dispatch(rank, flows, left, right, rollout, place):
    return call(
        dispatch_kernel,
        [shape((ROWS, HALF), bf16), shape((2 * TOK_DEV, HALF), bf16)],
        [SMEM, SMEM] + [VMEM] * 4,
        550_000_000,
    )(rank, flows, left, right, rollout, place)


def ffn(rows, w_gate, w_up, w_down):
    parts = FF // FF_CHUNK
    return call(
        ffn_kernel,
        shape((ROWS, HALF), bf16),
        [VMEM, ANY, ANY, ANY],
        3_700_000_000,
        [
            pltpu.VMEM((parts, D, FF_CHUNK), bf16),
            pltpu.VMEM((parts, D, FF_CHUNK), bf16),
            pltpu.VMEM((FF, D), bf16),
            pltpu.VMEM((SLOTS, D), bf16),
            pltpu.VMEM((SLOTS, FF), bf16),
            pltpu.SemaphoreType.DMA((2 * parts + 1,)),
        ],
        limit=40 << 20,
    )(rows, w_gate, w_up, w_down)


def router_terms(rows, grad_out, balanced, place, weight):
    return call(terms_kernel, shape((4 * EXPERTS, QUARTER), bf16), [VMEM] * 5, 700_000_000)(
        rows, grad_out, balanced, place, weight
    )


def layer_output(rows, high, low):
    return call(output_kernel, shape((TOK_DEV, D), bf16), [VMEM] * 3, 4_000_000_000)(
        rows, high, low
    )


def partial_sum(terms):
    return call(part_kernel, shape((192, QUARTER), bf16), [VMEM], 1_000_000)(terms)


def last_sum(parts):
    return call(last_kernel, shape((4, D), f32), [VMEM], 1_000_000)(parts)


def shards(rollout, flows, route_ids, route_logits, grad_out, w_gate, w_up, w_down):
    ranks = lax.axis_size(DP)
    rank = lax.axis_index(DP).reshape(1)
    flows = flows.T
    head, tail = borders(rank, flows, rollout)
    left = lax.ppermute(tail, DP, [(i, (i + 1) % ranks) for i in range(ranks)])
    right = lax.ppermute(head, DP, [((i + 1) % ranks, i) for i in range(ranks)])
    place, weight, high, low = routes(route_ids.T, route_logits.T)
    outgoing, balanced = dispatch(rank, flows, left, right, rollout, place)
    rows = exchange(outgoing, "fsdp", WIN)
    computed = ffn(rows, w_gate, w_up, w_down)
    returned = exchange(computed, "fsdp", WIN)
    terms = exchange(router_terms(returned, grad_out, balanced, place, weight), ("yl", "fsdp"), 64)
    layer_out = layer_output(returned, high, low)
    parts = exchange(partial_sum(terms), DP, 24)
    return (layer_out, last_sum(parts))


def solution(mesh):
    fine = Mesh(mesh.devices.reshape(2, 12, 32), ("yl", "z", "fsdp"))
    rows = P(("yl", "z", "fsdp"), None)
    expert = P("fsdp", None, None)
    return jax.shard_map(
        shards,
        mesh=fine,
        in_specs=(rows, P(None, "fsdp"), rows, rows, rows, expert, expert, expert),
        out_specs=(rows, P("fsdp", None)),
        check_vma=False,
    )
```

time: 240 us -> 180 us (0.75)
  the two profiles are of different devices: /device:TPU:2 before, /device:TPU:8 now
where the time goes in v2:
time: 180 us; the launch traced here: 179 us
  blocking collectives  120 us (67%)
  starting transfers between devices  25.8 us (14%)
  Pallas kernels  17.1 us (10%)
  waiting for transfers between devices  10.7 us (6%)
  local copies, waits for them, and re-layouts  5.06 us (3%)
    all_to_all x3, blocking collectives, exchange(): lax.all_to_all(apart, axes, split_axis=0, concat_axis=0, tiled=True)  120 us
    ppermute x1, starting transfers between devices, shards(): right = lax.ppermute(head, DP, [((i + 1) % ranks, i) for i in range(ranks)])  12.1 us
    all_to_all x1, waiting for transfers between devices, exchange(): lax.all_to_all(apart, axes, split_axis=0, concat_axis=0, tiled=True)  10.2 us
    all_to_all x1, starting transfers between devices, exchange(): lax.all_to_all(apart, axes, split_axis=0, concat_axis=0, tiled=True)  9.41 us
    pallas_call x1, Pallas kernels, ffn(): call(ffn_kernel, shape((ROWS, HALF), bf16), [VMEM, ANY, ANY, ANY], 370000...  8.83 us
    unnamed x20, local copies, waits for them, and re-layouts  5.06 us
    ppermute x1, starting transfers between devices, shards(): left = lax.ppermute(tail, DP, [(i, (i + 1) % ranks) for i in range(ranks)])  4.3 us
  transfers between devices with their start and end apart: 3, of which 2 were waited for; matrix products, arithmetic and copies ran while one was open for 0% of the time, Pallas kernels for 1%

profile of v2, /device:TPU:8, one launch (start us, length us, event | category | flops | bytes accessed | tf_op | source)
XLA Modules:
  0.0 179.2 jit_solution(5140946125479864558)
XLA Ops:
  0.6 0.0 copy-start.4
  0.7 0.0 copy-start
  0.7 1.1 copy-done
  1.8 0.0 copy-start.3
  1.8 0.7 copy-done.3
  2.4 0.0 copy-start.1
  2.4 0.8 shard_map.95
  3.2 4.3 %collective-permute-start = (bf16[32,2048]{1,0:T(8,128)(2,1)S(1)}, bf16[32,2048]{1,0:T(8,128)(2,1)S(1)}, u32[]{:S(2)}, u32[]{:S(2)}) collective-permute-start(bf16[32,2048]{1,0:T(8,128)(2,1)S(1)} %get-tuple-element.10), channel_id=1, source_target_pairs={{0,32},{32,64},{64,96},{96,128},{128,160},{160,192},{192,224},{224... | collective-permute-start | bytes 393224 | tf_op jit(solution)/shard_map/ppermute | solution.py:312
  7.5 12.1 %collective-permute-start.1 = (bf16[32,2048]{1,0:T(8,128)(2,1)S(1)}, bf16[32,2048]{1,0:T(8,128)(2,1)S(1)}, u32[]{:S(2)}, u32[]{:S(2)}) collective-permute-start(bf16[32,2048]{1,0:T(8,128)(2,1)S(1)} %get-tuple-element.11), channel_id=1, source_target_pairs={{32,0},{64,32},{96,64},{128,96},{160,128},{192,160},{224,192},{256... | collective-permute-start | bytes 393224 | tf_op jit(solution)/shard_map/ppermute | solution.py:313
  19.6 0.0 copy-start.8
  19.7 0.7 copy-done.8
  20.3 0.0 copy-start.9
  20.3 0.7 copy-done.9
  21.0 0.0 copy-start.6
  21.0 0.9 shard_map.96
  21.9 0.0 collective-permute-done.left_ref
  21.9 0.4 collective-permute-done.1.right_ref
  22.4 0.0 copy-done.4
  22.4 0.0 copy-done.1
  22.4 1.4 shard_map.97
  23.8 0.0 copy-start.5
  23.8 51.2 %all_to_all.20 = bf16[32,24,1024]{2,1,0:T(8,128)(2,1)S(1)} all-to-all(bf16[32,24,1024]{2,1,0:T(8,128)(2,1)S(1)} %bitcast.16), channel_id=1, replica_groups=mesh['yl'=2,'z'=12,'fsdp'=32] {'fsdp'}, dimensions={0} | all-to-all | bytes 3145728 | tf_op jit(solution)/shard_map/all_to_all | solution.py:236
  75.0 0.0 copy-done.6
  75.0 0.0 copy-done.5
  75.0 0.0 copy-start.7
  75.0 1.9 %copy-done.7 = bf16[1,768,2048]{2,1,0:T(8,128)(2,1)S(1)} copy-done((bf16[1,768,2048]{2,1,0:T(8,128)(2,1)S(1)}, bf16[1,768,2048]{2,1,0:T(8,128)(2,1)}, u32[]{:S(2)}) %copy-start.7) | copy-done | bytes 3145752
  76.9 8.8 %shard_map.98 = bf16[768,1024]{1,0:T(8,128)(2,1)S(1)} custom-call(bf16[768,1024]{1,0:T(8,128)(2,1)S(1)} %bitcast.17, bf16[1,2048,768]{2,1,0:T(8,128)(2,1)S(1)} %copy-done.5, bf16[1,2048,768]{2,1,0:T(8,128)(2,1)S(1)} %copy-done.6, bf16[1,768,2048]{2,1,0:T(8,128)(2,1)S(1)} %copy-done.7), custom_call_target="tpu_custom_call" | custom-call | flops 3700000000 | bytes 3145728 | tf_op jit(solution)/shard_map/pallas_call | solution.py:270
  85.7 0.0 copy-start.2
  85.7 45.2 %all_to_all.21 = bf16[32,24,1024]{2,1,0:T(8,128)(2,1)S(1)} all-to-all(bf16[32,24,1024]{2,1,0:T(8,128)(2,1)S(1)} %bitcast.18), channel_id=1, replica_groups=mesh['yl'=2,'z'=12,'fsdp'=32] {'fsdp'}, dimensions={0} | all-to-all | bytes 3145728 | tf_op jit(solution)/shard_map/all_to_all | solution.py:236
  130.9 0.0 copy-done.2
  130.9 2.1 %shard_map.100 = bf16[512,512]{1,0:T(8,128)(2,1)S(1)} custom-call(bf16[768,1024]{1,0:T(8,128)(2,1)S(1)} %bitcast.12, bf16[128,2048]{1,0:T(8,128)(2,1)S(1)} %copy-done.2, bf16[256,1024]{1,0:T(8,128)(2,1)S(1)} %get-tuple-element.16.bal_ref, bf16[768,256]{1,0:T(8,128)(2,1)S(1)} %get-tuple-element.12.place_ref, f32[128,128]{1,0:T(8,128)S(1)} %get-tuple-element.17.weight_ref), custom_call_target="tpu_custom_call" | custom-call | flops 700000000 | bytes 1048576 | tf_op jit(solution)/shard_map/pallas_call | solution.py:288
  133.0 23.4 %all_to_all.22 = bf16[64,8,512]{2,1,0:T(8,128)(2,1)S(1)} all-to-all(bf16[64,8,512]{2,1,0:T(8,128)(2,1)S(1)} %bitcast.14), channel_id=1, replica_groups=mesh['yl'=2,'z'=12,'fsdp'=32] {'yl','fsdp'}, dimensions={0} | all-to-all | bytes 1048576 | tf_op jit(solution)/shard_map/all_to_all | solution.py:236
  156.4 0.8 shard_map.101
  157.1 9.4 %all-to-all-start.3 = ((bf16[24,8,512]{2,1,0:T(8,128)(2,1)}), bf16[24,8,512]{2,1,0:T(8,128)(2,1)S(1)}, u32[]{:S(2)}, u32[]{:S(2)}) async-start(bf16[24,8,512]{2,1,0:T(8,128)(2,1)} %bitcast.10), calls=%async_computation.3 | async-start | bytes 393216 | tf_op jit(solution)/shard_map/all_to_all | solution.py:236
  166.5 1.8 shard_map.99
  168.3 10.2 %all-to-all-done.3 = bf16[24,8,512]{2,1,0:T(8,128)(2,1)S(1)} async-done(((bf16[24,8,512]{2,1,0:T(8,128)(2,1)}), bf16[24,8,512]{2,1,0:T(8,128)(2,1)S(1)}, u32[]{:S(2)}, u32[]{:S(2)}) %all-to-all-start.3) | async-done | bytes 196640 | tf_op jit(solution)/shard_map/all_to_all | solution.py:236
  178.6 0.6 shard_map.102
Async XLA Ops:
  0.6 21.7 %copy-start.4 = (s32[24,1]{0,1:T(1,128)S(1)}, s32[24,1]{0,1:T(1,128)}, u32[]{:S(2)}) copy-start(s32[24,1]{0,1:T(1,128)} %param.9) | copy-start | bytes 292
  0.7 1.1 copy-start
  1.8 0.7 copy-start.3
  2.4 19.9 %copy-start.1 = (bf16[192,2048]{1,0:T(8,128)(2,1)S(1)}, bf16[192,2048]{1,0:T(8,128)(2,1)}, u32[]{:S(2)}) copy-start(bf16[192,2048]{1,0:T(8,128)(2,1)} %rollout_ref.3) | copy-start | bytes 2359300
  3.2 18.7 %collective-permute-start = (bf16[32,2048]{1,0:T(8,128)(2,1)S(1)}, bf16[32,2048]{1,0:T(8,128)(2,1)S(1)}, u32[]{:S(2)}, u32[]{:S(2)}) collective-permute-start(bf16[32,2048]{1,0:T(8,128)(2,1)S(1)} %get-tuple-element.10), channel_id=1, source_target_pairs={{0,32},{32,64},{64,96},{96,128},{128,160},{160,192},{192,224},{224... | collective-permute-start | bytes 393224 | tf_op jit(solution)/shard_map/ppermute | solution.py:312
  7.5 14.9 %collective-permute-start.1 = (bf16[32,2048]{1,0:T(8,128)(2,1)S(1)}, bf16[32,2048]{1,0:T(8,128)(2,1)S(1)}, u32[]{:S(2)}, u32[]{:S(2)}) collective-permute-start(bf16[32,2048]{1,0:T(8,128)(2,1)S(1)} %get-tuple-element.11), channel_id=1, source_target_pairs={{32,0},{64,32},{96,64},{128,96},{160,128},{192,160},{224,192},{256... | collective-permute-start | bytes 393224 | tf_op jit(solution)/shard_map/ppermute | solution.py:313
  19.6 0.7 copy-start.8
  20.3 0.7 copy-start.9
  21.0 54.0 %copy-start.6 = (bf16[1,2048,768]{2,1,0:T(8,128)(2,1)S(1)}, bf16[1,2048,768]{2,1,0:T(8,128)(2,1)}, u32[]{:S(2)}) copy-start(bf16[1,2048,768]{2,1,0:T(8,128)(2,1)} %up_hbm.1) | copy-start | bytes 9437188
  23.8 51.2 %copy-start.5 = (bf16[1,2048,768]{2,1,0:T(8,128)(2,1)S(1)}, bf16[1,2048,768]{2,1,0:T(8,128)(2,1)}, u32[]{:S(2)}) copy-start(bf16[1,2048,768]{2,1,0:T(8,128)(2,1)} %gate_hbm.1) | copy-start | bytes 9437188
  75.0 1.9 %copy-start.7 = (bf16[1,768,2048]{2,1,0:T(8,128)(2,1)S(1)}, bf16[1,768,2048]{2,1,0:T(8,128)(2,1)}, u32[]{:S(2)}) copy-start(bf16[1,768,2048]{2,1,0:T(8,128)(2,1)} %down_hbm.1) | copy-start | bytes 9437188
  85.7 45.2 %copy-start.2 = (bf16[128,2048]{1,0:T(8,128)(2,1)S(1)}, bf16[128,2048]{1,0:T(8,128)(2,1)}, u32[]{:S(2)}) copy-start(bf16[128,2048]{1,0:T(8,128)(2,1)} %grad_ref.1) | copy-start | bytes 1572868
  157.1 21.4 %all-to-all-start.3 = ((bf16[24,8,512]{2,1,0:T(8,128)(2,1)}), bf16[24,8,512]{2,1,0:T(8,128)(2,1)S(1)}, u32[]{:S(2)}, u32[]{:S(2)}) async-start(bf16[24,8,512]{2,1,0:T(8,128)(2,1)} %bitcast.10), calls=%async_computation.3 | async-start | bytes 393216 | tf_op jit(solution)/shard_map/all_to_all | solution.py:236

commit v3 on v2

--- a/solution.py
+++ b/solution.py
@@ -16,6 +16,7 @@
 TOK_DEV = 128
 SRC_DEV = 192
 MOVE = 32
+NEAR = 48
 CAP = 12
 PAIR = 2 * CAP
 ROWS = WIN * PAIR
@@ -26,7 +27,7 @@
 bf16, f32, i32 = jnp.bfloat16, jnp.float32, jnp.int32
 VMEM = pl.BlockSpec(memory_space=pltpu.VMEM)
 SMEM = pl.BlockSpec(memory_space=pltpu.SMEM)
-ANY = pl.BlockSpec(memory_space=pl.ANY)
+HBM = pl.BlockSpec(memory_space=pltpu.HBM)
 
 
 def iota(shape, dim):
@@ -69,12 +70,21 @@
     return left, TOK_DEV + own - left
 
 
-def border_kernel(rank_ref, flows_ref, rollout_ref, head_ref, tail_ref):
-    _, live = live_of(rank_ref, flows_ref)
-    at = iota((MOVE, SRC_DEV), 0) + (live - MOVE)
-    pick = (iota((MOVE, SRC_DEV), 1) == at).astype(bf16)
-    head_ref[...] = rollout_ref[:MOVE, :]
-    tail_ref[...] = mm(pick, rollout_ref[...]).astype(bf16)
+def border_kernel(rank_ref, flows_hbm, rollout_hbm, head_ref, tail_ref, flows, near, sems):
+    head_copy = pltpu.make_async_copy(rollout_hbm.at[pl.ds(0, MOVE)], head_ref, sems.at[0])
+    flow_copy = pltpu.make_async_copy(flows_hbm, flows, sems.at[1])
+    flow_copy.start()
+    head_copy.start()
+    flow_copy.wait()
+    _, live = live_of(rank_ref, flows)
+    begin = pl.multiple_of(jnp.minimum((live - MOVE) >> 4, (SRC_DEV - NEAR) >> 4) * 16, 16)
+    near_copy = pltpu.make_async_copy(rollout_hbm.at[pl.ds(begin, NEAR)], near, sems.at[2])
+    near_copy.start()
+    at = iota((MOVE, NEAR), 0) + (live - MOVE - begin)
+    pick = (iota((MOVE, NEAR), 1) == at).astype(bf16)
+    near_copy.wait()
+    tail_ref[...] = mm(pick, near[...]).astype(bf16)
+    head_copy.wait()
 
 
 def route_kernel(ids_ref, logits_ref, place_ref, weight_ref, high_ref, low_ref):
@@ -133,22 +143,8 @@
     return PAIR * source + CAP * half + (rest - CAP * source)
 
 
-def ffn_kernel(
-    rows_ref, gate_hbm, up_hbm, down_hbm, out_ref, gate, up, down, x, hidden, sems
-):
-    parts = FF // FF_CHUNK
-    copies = []
-    for f in range(parts):
-        cols = pl.ds(f * FF_CHUNK, FF_CHUNK)
-        copies.append(
-            (
-                pltpu.make_async_copy(gate_hbm.at[0, :, cols], gate.at[f], sems.at[2 * f]),
-                pltpu.make_async_copy(up_hbm.at[0, :, cols], up.at[f], sems.at[2 * f + 1]),
-            )
-        )
-        copies[f][0].start()
-        copies[f][1].start()
-    down_copy = pltpu.make_async_copy(down_hbm.at[0], down, sems.at[2 * parts])
+def ffn_kernel(rows_ref, gate_ref, up_ref, down_hbm, out_ref, down, x, hidden, sem):
+    down_copy = pltpu.make_async_copy(down_hbm.at[0], down, sem)
     down_copy.start()
     ordered = (iota((BLOCK, BLOCK), 1) == block_source((BLOCK, BLOCK), 0)).astype(bf16)
     back = (iota((BLOCK, BLOCK), 0) == block_source((BLOCK, BLOCK), 1)).astype(bf16)
@@ -157,13 +153,11 @@
         y = mm(ordered, rows_ref[b * BLOCK : (b + 1) * BLOCK, :]).astype(bf16)
         x[b * part_rows : (b + 1) * part_rows, :HALF] = y[:part_rows]
         x[b * part_rows : (b + 1) * part_rows, HALF:] = y[part_rows:]
-    for f in range(parts):
-        copies[f][0].wait()
-        g = mm(x[...], gate[f])
-        copies[f][1].wait()
-        u = mm(x[...], up[f])
-        act = g / (1.0 + jnp.exp(-g)) * u
-        hidden[:, f * FF_CHUNK : (f + 1) * FF_CHUNK] = act.astype(bf16)
+    for f in range(FF // FF_CHUNK):
+        cols = slice(f * FF_CHUNK, (f + 1) * FF_CHUNK)
+        g = mm(x[...], gate_ref[0, :, cols])
+        u = mm(x[...], up_ref[0, :, cols])
+        hidden[:, cols] = (g / (1.0 + jnp.exp(-g)) * u).astype(bf16)
     down_copy.wait()
     for half in range(2):
         cols = slice(half * HALF, (half + 1) * HALF)
@@ -226,6 +220,10 @@
             out_ref[:, at : at + QUARTER] = parts[half, 4 * quarter : 4 * quarter + 4]
 
 
+def in_hbm(array):
+    return pltpu.with_memory_space_constraint(array, pltpu.HBM)
+
+
 def shape(dims, dtype):
     return jax.ShapeDtypeStruct(dims, dtype)
 
@@ -238,8 +236,16 @@
 
 def borders(rank, flows, rollout):
     return call(
-        border_kernel, [shape((MOVE, D), bf16)] * 2, [SMEM, SMEM, VMEM], 25_000_000
-    )(rank, flows, rollout)
+        border_kernel,
+        [shape((MOVE, D), bf16)] * 2,
+        [SMEM, HBM, HBM],
+        25_000_000,
+        [
+            pltpu.SMEM((1, 24), i32),
+            pltpu.VMEM((NEAR, D), bf16),
+            pltpu.SemaphoreType.DMA((3,)),
+        ],
+    )(rank, in_hbm(flows), in_hbm(rollout))
 
 
 def routes(ids, logits):
@@ -266,22 +272,18 @@
 
 
 def ffn(rows, w_gate, w_up, w_down):
-    parts = FF // FF_CHUNK
     return call(
         ffn_kernel,
         shape((ROWS, HALF), bf16),
-        [VMEM, ANY, ANY, ANY],
+        [VMEM, VMEM, VMEM, HBM],
         3_700_000_000,
         [
-            pltpu.VMEM((parts, D, FF_CHUNK), bf16),
-            pltpu.VMEM((parts, D, FF_CHUNK), bf16),
             pltpu.VMEM((FF, D), bf16),
             pltpu.VMEM((SLOTS, D), bf16),
             pltpu.VMEM((SLOTS, FF), bf16),
-            pltpu.SemaphoreType.DMA((2 * parts + 1,)),
+            pltpu.SemaphoreType.DMA,
         ],
-        limit=40 << 20,
-    )(rows, w_gate, w_up, w_down)
+    )(rows, w_gate, w_up, in_hbm(w_down))
 
 
 def router_terms(rows, grad_out, balanced, place, weight):

time: 180 us -> 175 us (0.972)
  local copies, waits for them, and re-layouts: 5.06 us -> 1.39 us
    unnamed x20 -> x14, local copies, waits for them, and re-layouts: 5.06 us -> 1.39 us
  transfers between devices with their start and end apart: 3 -> 3, of which waited for: 2 -> 2; matrix products, arithmetic and copies ran while one was open for 0% -> 0% of each run, Pallas kernels for 1% -> 2%
where the time goes in v3:
time: 175 us; the launch traced here: 174 us
  blocking collectives  120 us (69%)
  starting transfers between devices  25.8 us (15%)
  Pallas kernels  15.9 us (9%)
  waiting for transfers between devices  10.7 us (6%)
    all_to_all x3, blocking collectives, exchange(): lax.all_to_all(apart, axes, split_axis=0, concat_axis=0, tiled=True)  120 us
    ppermute x1, starting transfers between devices, shards(): right = lax.ppermute(head, DP, [((i + 1) % ranks, i) for i in range(ranks)])  12.1 us
    all_to_all x1, waiting for transfers between devices, exchange(): lax.all_to_all(apart, axes, split_axis=0, concat_axis=0, tiled=True)  10.2 us
    all_to_all x1, starting transfers between devices, exchange(): lax.all_to_all(apart, axes, split_axis=0, concat_axis=0, tiled=True)  9.41 us
    pallas_call x1, Pallas kernels, ffn(): call(ffn_kernel, shape((ROWS, HALF), bf16), [VMEM, VMEM, VMEM, HBM], 3700...  6.48 us
    ppermute x1, starting transfers between devices, shards(): left = lax.ppermute(tail, DP, [(i, (i + 1) % ranks) for i in range(ranks)])  4.28 us
  transfers between devices with their start and end apart: 3, of which 2 were waited for; matrix products, arithmetic and copies ran while one was open for 0% of the time, Pallas kernels for 2%

profile of v3, /device:TPU:8, one launch (start us, length us, event | category | flops | bytes accessed | tf_op | source)
XLA Modules:
  0.0 174.4 jit_solution(16353540933269344074)
XLA Ops:
  0.6 0.0 copy-start
  0.6 0.0 copy-start.2
  0.7 1.9 %shard_map.95 = (bf16[32,2048]{1,0:T(8,128)(2,1)S(1)}, bf16[32,2048]{1,0:T(8,128)(2,1)S(1)}) custom-call(s32[1]{0:T(128)} %bitcast.rank_ref, s32[1,24]{1,0:T(1,128)} %bitcast.20, bf16[192,2048]{1,0:T(8,128)(2,1)} %rollout_ref.1), custom_call_target="tpu_custom_call" | custom-call | flops 25000000 | bytes 524288 | tf_op jit(solution)/shard_map/pallas_call | solution.py:238
  2.6 4.3 %collective-permute-start = (bf16[32,2048]{1,0:T(8,128)(2,1)S(1)}, bf16[32,2048]{1,0:T(8,128)(2,1)S(1)}, u32[]{:S(2)}, u32[]{:S(2)}) collective-permute-start(bf16[32,2048]{1,0:T(8,128)(2,1)S(1)} %get-tuple-element.10), channel_id=1, source_target_pairs={{0,32},{32,64},{64,96},{96,128},{128,160},{160,192},{192,224},{224... | collective-permute-start | bytes 393224 | tf_op jit(solution)/shard_map/ppermute | solution.py:314
  6.9 12.1 %collective-permute-start.1 = (bf16[32,2048]{1,0:T(8,128)(2,1)S(1)}, bf16[32,2048]{1,0:T(8,128)(2,1)S(1)}, u32[]{:S(2)}, u32[]{:S(2)}) collective-permute-start(bf16[32,2048]{1,0:T(8,128)(2,1)S(1)} %get-tuple-element.11), channel_id=1, source_target_pairs={{32,0},{64,32},{96,64},{128,96},{160,128},{192,160},{224,192},{256... | collective-permute-start | bytes 393224 | tf_op jit(solution)/shard_map/ppermute | solution.py:315
  19.0 0.0 copy-start.5
  19.0 0.7 copy-done.5
  19.7 0.0 copy-start.6
  19.7 0.7 copy-done.6
  20.4 0.0 copy-start.4
  20.4 0.9 shard_map.96
  21.3 0.0 collective-permute-done.left_ref
  21.3 0.4 collective-permute-done.1.right_ref
  21.8 0.0 copy-done
  21.8 0.0 copy-done.2
  21.8 1.4 shard_map.97
  23.1 0.0 copy-start.3
  23.1 51.2 %all_to_all.20 = bf16[32,24,1024]{2,1,0:T(8,128)(2,1)S(1)} all-to-all(bf16[32,24,1024]{2,1,0:T(8,128)(2,1)S(1)} %bitcast.16), channel_id=1, replica_groups=mesh['yl'=2,'z'=12,'fsdp'=32] {'fsdp'}, dimensions={0} | all-to-all | bytes 3145728 | tf_op jit(solution)/shard_map/all_to_all | solution.py:234
  74.4 0.0 copy-done.4
  74.4 0.0 copy-done.3
  74.4 6.5 %shard_map.98 = bf16[768,1024]{1,0:T(8,128)(2,1)S(1)} custom-call(bf16[768,1024]{1,0:T(8,128)(2,1)S(1)} %bitcast.17, bf16[1,2048,768]{2,1,0:T(8,128)(2,1)S(1)} %copy-done.3, bf16[1,2048,768]{2,1,0:T(8,128)(2,1)S(1)} %copy-done.4, bf16[1,768,2048]{2,1,0:T(8,128)(2,1)} %down_hbm.1), custom_call_target="tpu_custom_call" | custom-call | flops 3700000000 | bytes 3145728 | tf_op jit(solution)/shard_map/pallas_call | solution.py:275
  80.9 0.0 copy-start.1
  80.9 45.1 %all_to_all.21 = bf16[32,24,1024]{2,1,0:T(8,128)(2,1)S(1)} all-to-all(bf16[32,24,1024]{2,1,0:T(8,128)(2,1)S(1)} %bitcast.18), channel_id=1, replica_groups=mesh['yl'=2,'z'=12,'fsdp'=32] {'fsdp'}, dimensions={0} | all-to-all | bytes 3145728 | tf_op jit(solution)/shard_map/all_to_all | solution.py:234
  126.0 0.0 copy-done.1
  126.0 2.1 %shard_map.100 = bf16[512,512]{1,0:T(8,128)(2,1)S(1)} custom-call(bf16[768,1024]{1,0:T(8,128)(2,1)S(1)} %bitcast.12, bf16[128,2048]{1,0:T(8,128)(2,1)S(1)} %copy-done.1, bf16[256,1024]{1,0:T(8,128)(2,1)S(1)} %get-tuple-element.16.bal_ref, bf16[768,256]{1,0:T(8,128)(2,1)S(1)} %get-tuple-element.12.place_ref, f32[128,128]{1,0:T(8,128)S(1)} %get-tuple-element.17.weight_ref), custom_call_target="tpu_custom_call" | custom-call | flops 700000000 | bytes 1048576 | tf_op jit(solution)/shard_map/pallas_call | solution.py:290
  128.1 23.4 %all_to_all.22 = bf16[64,8,512]{2,1,0:T(8,128)(2,1)S(1)} all-to-all(bf16[64,8,512]{2,1,0:T(8,128)(2,1)S(1)} %bitcast.14), channel_id=1, replica_groups=mesh['yl'=2,'z'=12,'fsdp'=32] {'yl','fsdp'}, dimensions={0} | all-to-all | bytes 1048576 | tf_op jit(solution)/shard_map/all_to_all | solution.py:234
  151.5 0.8 shard_map.101
  152.3 9.4 %all-to-all-start.3 = ((bf16[24,8,512]{2,1,0:T(8,128)(2,1)}), bf16[24,8,512]{2,1,0:T(8,128)(2,1)S(1)}, u32[]{:S(2)}, u32[]{:S(2)}) async-start(bf16[24,8,512]{2,1,0:T(8,128)(2,1)} %bitcast.10), calls=%async_computation.3 | async-start | bytes 393216 | tf_op jit(solution)/shard_map/all_to_all | solution.py:234
  161.7 1.8 %shard_map.99 = bf16[128,2048]{1,0:T(8,128)(2,1)} custom-call(bf16[768,1024]{1,0:T(8,128)(2,1)S(1)} %bitcast.13, bf16[256,768]{1,0:T(8,128)(2,1)S(1)} %get-tuple-element.14.high_ref, bf16[256,768]{1,0:T(8,128)(2,1)S(1)} %get-tuple-element.15.low_ref), custom_call_target="tpu_custom_call" | custom-call | flops 4000000000 | bytes 1048576 | tf_op jit(solution)/shard_map/pallas_call | solution.py:296
  163.5 10.2 %all-to-all-done.3 = bf16[24,8,512]{2,1,0:T(8,128)(2,1)S(1)} async-done(((bf16[24,8,512]{2,1,0:T(8,128)(2,1)}), bf16[24,8,512]{2,1,0:T(8,128)(2,1)S(1)}, u32[]{:S(2)}, u32[]{:S(2)}) %all-to-all-start.3) | async-done | bytes 196640 | tf_op jit(solution)/shard_map/all_to_all | solution.py:234
  173.7 0.6 shard_map.102
Async XLA Ops:
  0.6 21.1 %copy-start = (bf16[192,2048]{1,0:T(8,128)(2,1)S(1)}, bf16[192,2048]{1,0:T(8,128)(2,1)}, u32[]{:S(2)}) copy-start(bf16[192,2048]{1,0:T(8,128)(2,1)} %rollout_ref.1) | copy-start | bytes 2359300
  0.6 21.1 %copy-start.2 = (s32[24,1]{0,1:T(1,128)S(1)}, s32[24,1]{0,1:T(1,128)}, u32[]{:S(2)}) copy-start(s32[24,1]{0,1:T(1,128)} %param.9) | copy-start | bytes 292
  2.6 18.7 %collective-permute-start = (bf16[32,2048]{1,0:T(8,128)(2,1)S(1)}, bf16[32,2048]{1,0:T(8,128)(2,1)S(1)}, u32[]{:S(2)}, u32[]{:S(2)}) collective-permute-start(bf16[32,2048]{1,0:T(8,128)(2,1)S(1)} %get-tuple-element.10), channel_id=1, source_target_pairs={{0,32},{32,64},{64,96},{96,128},{128,160},{160,192},{192,224},{224... | collective-permute-start | bytes 393224 | tf_op jit(solution)/shard_map/ppermute | solution.py:314
  6.9 14.9 %collective-permute-start.1 = (bf16[32,2048]{1,0:T(8,128)(2,1)S(1)}, bf16[32,2048]{1,0:T(8,128)(2,1)S(1)}, u32[]{:S(2)}, u32[]{:S(2)}) collective-permute-start(bf16[32,2048]{1,0:T(8,128)(2,1)S(1)} %get-tuple-element.11), channel_id=1, source_target_pairs={{32,0},{64,32},{96,64},{128,96},{160,128},{192,160},{224,192},{256... | collective-permute-start | bytes 393224 | tf_op jit(solution)/shard_map/ppermute | solution.py:315
  19.0 0.7 copy-start.5
  19.7 0.7 copy-start.6
  20.4 54.0 %copy-start.4 = (bf16[1,2048,768]{2,1,0:T(8,128)(2,1)S(1)}, bf16[1,2048,768]{2,1,0:T(8,128)(2,1)}, u32[]{:S(2)}) copy-start(bf16[1,2048,768]{2,1,0:T(8,128)(2,1)} %up_ref.1) | copy-start | bytes 9437188
  23.1 51.2 %copy-start.3 = (bf16[1,2048,768]{2,1,0:T(8,128)(2,1)S(1)}, bf16[1,2048,768]{2,1,0:T(8,128)(2,1)}, u32[]{:S(2)}) copy-start(bf16[1,2048,768]{2,1,0:T(8,128)(2,1)} %gate_ref.1) | copy-start | bytes 9437188
  80.9 45.1 %copy-start.1 = (bf16[128,2048]{1,0:T(8,128)(2,1)S(1)}, bf16[128,2048]{1,0:T(8,128)(2,1)}, u32[]{:S(2)}) copy-start(bf16[128,2048]{1,0:T(8,128)(2,1)} %grad_ref.1) | copy-start | bytes 1572868
  152.3 21.4 %all-to-all-start.3 = ((bf16[24,8,512]{2,1,0:T(8,128)(2,1)}), bf16[24,8,512]{2,1,0:T(8,128)(2,1)S(1)}, u32[]{:S(2)}, u32[]{:S(2)}) async-start(bf16[24,8,512]{2,1,0:T(8,128)(2,1)} %bitcast.10), calls=%async_computation.3 | async-start | bytes 393216 | tf_op jit(solution)/shard_map/all_to_all | solution.py:234

commit v4 on v3

v4 whole, which is shorter than its diff:
```python
import jax
import jax.numpy as jnp
from jax import lax
from jax.experimental import pallas as pl
from jax.experimental.pallas import tpu as pltpu
from jax.sharding import Mesh
from jax.sharding import PartitionSpec as P

D = 2048
HALF = D // 2
QUARTER = D // 4
FF = 768
EXPERTS = 128
WIN = 32
TOPK = 8
TOK_DEV = 128
SRC_DEV = 192
MOVE = 32
NEAR = 48
CAP = 12
WHOLE = 8
ROWS = WIN * WHOLE
WIDTH = D + HALF
SLOTS = WIN * CAP
BLOCK = 128
DP = ("yl", "z")
FF_CHUNK = 256
bf16, f32, i32 = jnp.bfloat16, jnp.float32, jnp.int32
VMEM = pl.BlockSpec(memory_space=pltpu.VMEM)
SMEM = pl.BlockSpec(memory_space=pltpu.SMEM)
HBM = pl.BlockSpec(memory_space=pltpu.HBM)


def iota(shape, dim):
    return lax.broadcasted_iota(i32, shape, dim)


def mm(a, b):
    return jnp.dot(a, b, preferred_element_type=f32)


def split2(v):
    high = v.astype(bf16)
    return high, (v - high.astype(f32)).astype(bf16)


def call(kernel, outs, in_specs, flops, scratch=(), limit=24 << 20):
    many = isinstance(outs, list)
    nbytes = sum(o.size * o.dtype.itemsize for o in (outs if many else [outs]))
    return pl.pallas_call(
        kernel,
        out_shape=outs,
        in_specs=in_specs,
        out_specs=[VMEM] * len(outs) if many else VMEM,
        scratch_shapes=list(scratch),
        cost_estimate=pl.CostEstimate(
            flops=flops, bytes_accessed=2 * nbytes, transcendentals=0
        ),
        compiler_params=pltpu.CompilerParams(vmem_limit_bytes=limit),
    )


def live_of(rank_ref, flows_ref):
    rank = rank_ref[0]
    own = flows_ref[0, rank]
    left = flows_ref[0, jnp.where(rank == 0, 23, rank - 1)]
    return left, TOK_DEV + own - left


def border_kernel(
    rank_ref,
    flows_hbm,
    rollout_hbm,
    ids_hbm,
    logits_hbm,
    head_ref,
    tail_ref,
    place_ref,
    late_ref,
    weight_ref,
    high_ref,
    low_ref,
    late_high_ref,
    late_low_ref,
    flows,
    near,
    ids,
    logits,
    sems,
):
    flow_copy = pltpu.make_async_copy(flows_hbm, flows, sems.at[0])
    ids_copy = pltpu.make_async_copy(ids_hbm, ids, sems.at[1])
    logits_copy = pltpu.make_async_copy(logits_hbm, logits, sems.at[2])
    head_copy = pltpu.make_async_copy(rollout_hbm.at[pl.ds(0, MOVE)], head_ref, sems.at[3])
    flow_copy.start()
    ids_copy.start()
    logits_copy.start()
    head_copy.start()
    flow_copy.wait()
    _, live = live_of(rank_ref, flows)
    begin = pl.multiple_of(jnp.minimum((live - MOVE) >> 4, (SRC_DEV - NEAR) >> 4) * 16, 16)
    near_copy = pltpu.make_async_copy(rollout_hbm.at[pl.ds(begin, NEAR)], near, sems.at[4])
    near_copy.start()
    ids_copy.wait()
    logits_copy.wait()
    route(
        ids,
        logits[...],
        place_ref,
        late_ref,
        weight_ref,
        (high_ref, low_ref),
        (late_high_ref, late_low_ref),
    )
    at = iota((MOVE, NEAR), 0) + (live - MOVE - begin)
    pick = (iota((MOVE, NEAR), 1) == at).astype(bf16)
    near_copy.wait()
    tail_ref[...] = mm(pick, near[...]).astype(bf16)
    head_copy.wait()


def route(ids, logits, place_ref, late_ref, weight_ref, parts_refs, late_parts_refs):
    raised = jnp.exp(logits - jnp.max(logits, axis=0, keepdims=True))
    share = raised / jnp.sum(raised, axis=0, keepdims=True)
    expert = iota((EXPERTS, TOK_DEV), 0)
    weight = jnp.zeros((EXPERTS, TOK_DEV), f32)
    named = jnp.zeros((EXPERTS, TOK_DEV), f32)
    for k in range(TOPK):
        hit = ids[k : k + 1, :] == expert
        weight = jnp.where(hit, share[k : k + 1, :], weight)
        named = jnp.where(hit, 1.0, named)
    weight_ref[...] = weight
    upto = (iota((TOK_DEV, TOK_DEV), 0) <= iota((TOK_DEV, TOK_DEV), 1)).astype(bf16)
    count = mm(named[:WIN].astype(bf16), upto)
    code = jnp.where(named[:WIN] > 0.0, count, 0.0).astype(bf16)
    spread = ((iota((ROWS, WIN), 0) >> 3) == iota((ROWS, WIN), 1)).astype(bf16)
    row = iota((ROWS, TOK_DEV), 0)
    codes = mm(spread, code).astype(i32)
    whole = codes == (row & 7) + 1
    late = codes == (row & 3) + (WHOLE + 1)
    second = (row & 4) == 4
    place_ref[...] = whole.astype(bf16)
    for half in range(2):
        cols = slice(half * TOK_DEV, (half + 1) * TOK_DEV)
        late_ref[:, cols] = (late & (second == (half == 1))).astype(bf16)
    for part, out, late_out in zip(split2(weight[:WIN]), parts_refs, late_parts_refs):
        spreads = mm(spread, part)
        out[...] = jnp.where(whole, spreads, 0.0).T.astype(bf16)
        for half in range(2):
            mine = late & (second == (half == 1))
            late_out[half * TOK_DEV : (half + 1) * TOK_DEV, :] = (
                jnp.where(mine, spreads, 0.0).T.astype(bf16)
            )


def halves(wide):
    return jnp.concatenate([wide[:, :HALF], wide[:, HALF:]], axis=0)


def dispatch_kernel(
    rank_ref,
    flows_ref,
    left_ref,
    right_ref,
    rollout_ref,
    place_ref,
    late_ref,
    out_ref,
    bal_ref,
):
    left, live = live_of(rank_ref, flows_ref)
    span = SRC_DEV + 2 * MOVE
    at = iota((TOK_DEV, span), 0) + (MOVE - left)
    at = jnp.where(at < MOVE + live, at, at + (SRC_DEV - live))
    settle = (iota((TOK_DEV, span), 1) == at).astype(bf16)
    rows = jnp.concatenate([left_ref[...], rollout_ref[...], right_ref[...]], axis=0)
    balanced = mm(settle, rows).astype(bf16)
    bal_ref[...] = balanced
    out_ref[:, :D] = mm(place_ref[...], balanced).astype(bf16)
    out_ref[:, D:] = mm(late_ref[...], halves(balanced)).astype(bf16)


def block_source(dim):
    row = iota((BLOCK, BLOCK), dim)
    return ((row >> 2) & 15) * 8 + (row >> 6) * 4 + (row & 3)


def ffn_kernel(rows_ref, gate_ref, up_ref, down_hbm, out_ref, down, x, hidden, sem):
    down_copy = pltpu.make_async_copy(down_hbm.at[0], down, sem)
    down_copy.start()
    ordered = (iota((BLOCK, BLOCK), 1) == block_source(0)).astype(bf16)
    back = (iota((BLOCK, BLOCK), 0) == block_source(1)).astype(bf16)
    part_rows = BLOCK // 2
    x[:ROWS, :] = rows_ref[:, :D]
    for b in range(ROWS // BLOCK):
        y = mm(ordered, rows_ref[b * BLOCK : (b + 1) * BLOCK, D:]).astype(bf16)
        mine = slice(ROWS + b * part_rows, ROWS + (b + 1) * part_rows)
        x[mine, :HALF] = y[:part_rows]
        x[mine, HALF:] = y[part_rows:]
    for f in range(FF // FF_CHUNK):
        cols = slice(f * FF_CHUNK, (f + 1) * FF_CHUNK)
        g = mm(x[...], gate_ref[0, :, cols])
        u = mm(x[...], up_ref[0, :, cols])
        hidden[:, cols] = (g / (1.0 + jnp.exp(-g)) * u).astype(bf16)
    down_copy.wait()
    late = []
    for half in range(2):
        cols = slice(half * HALF, (half + 1) * HALF)
        y = mm(hidden[...], down[:, cols]).astype(bf16)
        out_ref[:, cols] = y[:ROWS]
        late.append(y[ROWS:])
    for b in range(ROWS // BLOCK):
        mine = slice(b * part_rows, (b + 1) * part_rows)
        y = jnp.concatenate([late[0][mine], late[1][mine]], axis=0)
        out_ref[b * BLOCK : (b + 1) * BLOCK, D:] = mm(back, y).astype(bf16)


def against(a, b):
    return lax.dot_general(a, b, (((1,), (1,)), ((), ())), preferred_element_type=f32)


def terms_kernel(rows_ref, grad_ref, bal_ref, place_ref, late_ref, weight_ref, out_ref):
    cotangent = grad_ref[...]
    scores = against(rows_ref[:, :D], cotangent) * place_ref[...].astype(f32)
    late = against(rows_ref[:, D:], halves(cotangent)) * late_ref[...].astype(f32)
    scores = scores + late[:, :TOK_DEV] + late[:, TOK_DEV:]
    score = jnp.sum(scores.reshape(WIN, WHOLE, TOK_DEV), axis=1)
    weight = weight_ref[...]
    total = jnp.sum(weight[:WIN] * score, axis=0, keepdims=True)
    grad = jnp.concatenate(
        [weight[:WIN] * (score - total), weight[WIN:] * (0.0 - total)], axis=0
    )
    high, low = split2(grad)
    line = iota((2 * EXPERTS, EXPERTS), 0)
    order = (iota((2 * EXPERTS, EXPERTS), 1) == (line >> 3) * 4 + (line & 3)).astype(bf16)
    factor = jnp.concatenate(
        [mm(order, high).astype(bf16), mm(order, low).astype(bf16)], axis=1
    )
    first = (iota((2 * EXPERTS, QUARTER), 0) & 4) == 0
    for half in range(2):
        tokens = bal_ref[:, half * HALF : (half + 1) * HALF]
        term = mm(factor, jnp.concatenate([tokens, tokens], axis=0))
        out_ref[half * 2 * EXPERTS : (half + 1) * 2 * EXPERTS, :] = jnp.where(
            first, term[:, :QUARTER], term[:, QUARTER:]
        ).astype(bf16)


def output_kernel(rows_ref, high_ref, low_ref, late_high_ref, late_low_ref, out_ref):
    rows, ends = rows_ref[:, :D], rows_ref[:, D:]
    late = mm(late_high_ref[...], ends) + mm(late_low_ref[...], ends)
    both = mm(high_ref[...], rows) + mm(low_ref[...], rows)
    out_ref[:, :HALF] = (both[:, :HALF] + late[:TOK_DEV]).astype(bf16)
    out_ref[:, HALF:] = (both[:, HALF:] + late[TOK_DEV:]).astype(bf16)


def part_kernel(terms_ref, out_ref):
    part = jnp.sum(terms_ref[...].astype(f32).reshape(64, 8, QUARTER), axis=0)
    two = jnp.concatenate([part, part], axis=0).astype(bf16)
    for i in range(12):
        out_ref[16 * i : 16 * (i + 1), :] = two


def last_kernel(parts_ref, out_ref):
    parts = jnp.sum(parts_ref[...].astype(f32).reshape(2, 12, 8, QUARTER), axis=1)
    for half in range(2):
        for quarter in range(2):
            at = half * HALF + quarter * QUARTER
            out_ref[:, at : at + QUARTER] = parts[half, 4 * quarter : 4 * quarter + 4]


def in_hbm(array):
    return pltpu.with_memory_space_constraint(array, pltpu.HBM)


def shape(dims, dtype):
    return jax.ShapeDtypeStruct(dims, dtype)


def exchange(blocks, axes, peers):
    rows, cols = blocks.shape
    apart = blocks.reshape(peers, rows // peers, cols)
    return lax.all_to_all(apart, axes, split_axis=0, concat_axis=0, tiled=True).reshape(rows, cols)


def borders(rank, flows, rollout, ids, logits):
    return call(
        border_kernel,
        [
            shape((MOVE, D), bf16),
            shape((MOVE, D), bf16),
            shape((ROWS, TOK_DEV), bf16),
            shape((ROWS, 2 * TOK_DEV), bf16),
            shape((EXPERTS, TOK_DEV), f32),
            shape((TOK_DEV, ROWS), bf16),
            shape((TOK_DEV, ROWS), bf16),
            shape((2 * TOK_DEV, ROWS), bf16),
            shape((2 * TOK_DEV, ROWS), bf16),
        ],
        [SMEM] + [HBM] * 4,
        25_000_000,
        [
            pltpu.SMEM((1, 24), i32),
            pltpu.VMEM((NEAR, D), bf16),
            pltpu.VMEM((TOPK, TOK_DEV), i32),
            pltpu.VMEM((TOPK, TOK_DEV), f32),
            pltpu.SemaphoreType.DMA((5,)),
        ],
    )(rank, *[in_hbm(v) for v in (flows, rollout, ids, logits)])


def dispatch(rank, flows, left, right, rollout, place, late):
    return call(
        dispatch_kernel,
        [shape((ROWS, WIDTH), bf16), shape((TOK_DEV, D), bf16)],
        [SMEM, SMEM] + [VMEM] * 5,
        550_000_000,
    )(rank, flows, left, right, rollout, place, late)


def ffn(rows, w_gate, w_up, w_down):
    return call(
        ffn_kernel,
        shape((ROWS, WIDTH), bf16),
        [VMEM, VMEM, VMEM, HBM],
        3_700_000_000,
        [
            pltpu.VMEM((FF, D), bf16),
            pltpu.VMEM((SLOTS, D), bf16),
            pltpu.VMEM((SLOTS, FF), bf16),
            pltpu.SemaphoreType.DMA,
        ],
    )(rows, w_gate, w_up, in_hbm(w_down))


def router_terms(rows, grad_out, balanced, place, late, weight):
    return call(terms_kernel, shape((4 * EXPERTS, QUARTER), bf16), [VMEM] * 6, 700_000_000)(
        rows, grad_out, balanced, place, late, weight
    )


def layer_output(rows, high, low, late_high, late_low):
    return call(output_kernel, shape((TOK_DEV, D), bf16), [VMEM] * 5, 4_000_000_000)(
        rows, high, low, late_high, late_low
    )


def partial_sum(terms):
    return call(part_kernel, shape((192, QUARTER), bf16), [VMEM], 1_000_000)(terms)


def last_sum(parts):
    return call(last_kernel, shape((4, D), f32), [VMEM], 1_000_000)(parts)


def shards(rollout, flows, route_ids, route_logits, grad_out, w_gate, w_up, w_down):
    ranks = lax.axis_size(DP)
    rank = lax.axis_index(DP).reshape(1)
    flows = flows.T
    head, tail, place, late, weight, *shares = borders(
        rank, flows, rollout, route_ids.T, route_logits.T
    )
    left = lax.ppermute(tail, DP, [(i, (i + 1) % ranks) for i in range(ranks)])
    right = lax.ppermute(head, DP, [((i + 1) % ranks, i) for i in range(ranks)])
    outgoing, balanced = dispatch(rank, flows, left, right, rollout, place, late)
    rows = exchange(outgoing, "fsdp", WIN)
    computed = ffn(rows, w_gate, w_up, w_down)
    returned = exchange(computed, "fsdp", WIN)
    terms = router_terms(returned, grad_out, balanced, place, late, weight)
    terms = exchange(terms, ("yl", "fsdp"), 64)
    layer_out = layer_output(returned, *shares)
    parts = exchange(partial_sum(terms), DP, 24)
    return (layer_out, last_sum(parts))


def solution(mesh):
    fine = Mesh(mesh.devices.reshape(2, 12, 32), ("yl", "z", "fsdp"))
    rows = P(("yl", "z", "fsdp"), None)
    expert = P("fsdp", None, None)
    return jax.shard_map(
        shards,
        mesh=fine,
        in_specs=(rows, P(None, "fsdp"), rows, rows, rows, expert, expert, expert),
        out_specs=(rows, P("fsdp", None)),
        check_vma=False,
    )
```

time: 175 us -> 177 us (1.011)
  Pallas kernels: 15.9 us -> 13.3 us
  waiting for transfers between devices: 10.7 us -> 13.2 us
  local copies, waits for them, and re-layouts: 1.39 us -> 3.69 us
    pallas_call x6 -> x5, Pallas kernels: 14.5 us -> 11.9 us  [the longest x1 5.93 us: ffn(): call(ffn_kernel, shape((ROWS, WIDTH), bf16), [VMEM, VMEM, VMEM, HBM], 370...]
    unnamed x14 -> x10, local copies, waits for them, and re-layouts: 1.39 us -> 3.69 us
  transfers between devices with their start and end apart: 3 -> 3, of which waited for: 2 -> 3; matrix products, arithmetic and copies ran while one was open for 0% -> 0% of each run, Pallas kernels for 2% -> 1%
where the time goes in v4:
time: 177 us
  blocking collectives  120 us (68%)
  starting transfers between devices  25.8 us (15%)
  Pallas kernels  13.3 us (8%)
  waiting for transfers between devices  13.2 us (7%)
  local copies, waits for them, and re-layouts  3.69 us (2%)
    all_to_all x3, blocking collectives, exchange(): lax.all_to_all(apart, axes, split_axis=0, concat_axis=0, tiled=True)  120 us
    ppermute x1, starting transfers between devices, shards(): right = lax.ppermute(head, DP, [((i + 1) % ranks, i) for i in range(ranks)])  12.1 us
    all_to_all x1, waiting for transfers between devices, exchange(): lax.all_to_all(apart, axes, split_axis=0, concat_axis=0, tiled=True)  10.5 us
    all_to_all x1, starting transfers between devices, exchange(): lax.all_to_all(apart, axes, split_axis=0, concat_axis=0, tiled=True)  9.41 us
    pallas_call x1, Pallas kernels, ffn(): call(ffn_kernel, shape((ROWS, WIDTH), bf16), [VMEM, VMEM, VMEM, HBM], 370...  5.93 us
    ppermute x1, starting transfers between devices, shards(): left = lax.ppermute(tail, DP, [(i, (i + 1) % ranks) for i in range(ranks)])  4.28 us
    unnamed x10, local copies, waits for them, and re-layouts  3.69 us
  transfers between devices with their start and end apart: 3, of which 3 were waited for; matrix products, arithmetic and copies ran while one was open for 0% of the time, Pallas kernels for 1%

profile of v4, /device:TPU:8, one launch (start us, length us, event | category | flops | bytes accessed | tf_op | source)
XLA Modules:
  0.0 176.6 jit_solution(9528055334888555875)
XLA Ops:
  0.6 1.8 %shard_map.95 = (bf16[32,2048]{1,0:T(8,128)(2,1)S(1)}, bf16[32,2048]{1,0:T(8,128)(2,1)S(1)}, bf16[256,128]{1,0:T(8,128)(2,1)S(1)}, bf16[256,256]{1,0:T(8,128)(2,...) custom-call(s32[1]{0:T(128)} %bitcast.rank_ref, ...), custom_call_target="tpu_custom_call" | custom-call | flops 25000000 | bytes 1835008 | tf_op jit(solution)/shard_map/pallas_call | solution.py:286
  2.5 4.3 %collective-permute-start = (bf16[32,2048]{1,0:T(8,128)(2,1)S(1)}, bf16[32,2048]{1,0:T(8,128)(2,1)S(1)}, u32[]{:S(2)}, u32[]{:S(2)}) collective-permute-start(bf16[32,2048]{1,0:T(8,128)(2,1)S(1)} %get-tuple-element.13), channel_id=1, source_target_pairs={{0,32},{32,64},{64,96},{96,128},{128,160},{160,192},{192,224},{224... | collective-permute-start | bytes 393224 | tf_op jit(solution)/shard_map/ppermute | solution.py:362
  6.8 12.1 %collective-permute-start.1 = (bf16[32,2048]{1,0:T(8,128)(2,1)S(1)}, bf16[32,2048]{1,0:T(8,128)(2,1)S(1)}, u32[]{:S(2)}, u32[]{:S(2)}) collective-permute-start(bf16[32,2048]{1,0:T(8,128)(2,1)S(1)} %get-tuple-element.14), channel_id=1, source_target_pairs={{32,0},{64,32},{96,64},{128,96},{160,128},{192,160},{224,192},{256... | collective-permute-start | bytes 393224 | tf_op jit(solution)/shard_map/ppermute | solution.py:363
  18.9 1.6 collective-permute-done.left_ref
  20.5 1.2 collective-permute-done.1.right_ref
  21.6 0.0 copy-start
  21.6 1.1 copy-done
  22.8 0.0 copy-start.2
  22.8 0.7 copy-done.2
  23.4 1.3 shard_map.96
  24.7 0.0 copy-start.3
  24.7 51.2 %all_to_all.20 = bf16[32,8,3072]{2,1,0:T(8,128)(2,1)S(1)} all-to-all(bf16[32,8,3072]{2,1,0:T(8,128)(2,1)S(1)} %bitcast.16), channel_id=1, replica_groups=mesh['yl'=2,'z'=12,'fsdp'=32] {'fsdp'}, dimensions={0} | all-to-all | bytes 3145728 | tf_op jit(solution)/shard_map/all_to_all | solution.py:282
  76.0 0.0 copy-done.3
  76.0 0.0 copy-start.4
  76.0 1.9 %copy-done.4 = bf16[1,2048,768]{2,1,0:T(8,128)(2,1)S(1)} copy-done((bf16[1,2048,768]{2,1,0:T(8,128)(2,1)S(1)}, bf16[1,2048,768]{2,1,0:T(8,128)(2,1)}, u32[]{:S(2)}) %copy-start.4) | copy-done | bytes 3145752
  77.9 5.9 %shard_map.97 = bf16[256,3072]{1,0:T(8,128)(2,1)S(1)} custom-call(bf16[256,3072]{1,0:T(8,128)(2,1)S(1)} %bitcast.17, bf16[1,2048,768]{2,1,0:T(8,128)(2,1)S(1)} %copy-done.3, bf16[1,2048,768]{2,1,0:T(8,128)(2,1)S(1)} %copy-done.4, bf16[1,768,2048]{2,1,0:T(8,128)(2,1)} %down_hbm.1), custom_call_target="tpu_custom_call" | custom-call | flops 3700000000 | bytes 3145728 | tf_op jit(solution)/shard_map/pallas_call | solution.py:321
  83.8 0.0 copy-start.1
  83.8 45.1 %all_to_all.21 = bf16[32,8,3072]{2,1,0:T(8,128)(2,1)S(1)} all-to-all(bf16[32,8,3072]{2,1,0:T(8,128)(2,1)S(1)} %bitcast.18), channel_id=1, replica_groups=mesh['yl'=2,'z'=12,'fsdp'=32] {'fsdp'}, dimensions={0} | all-to-all | bytes 3145728 | tf_op jit(solution)/shard_map/all_to_all | solution.py:282
  128.9 0.0 copy-done.1
  129.0 1.4 shard_map.99
  130.3 23.4 %all_to_all.22 = bf16[64,8,512]{2,1,0:T(8,128)(2,1)S(1)} all-to-all(bf16[64,8,512]{2,1,0:T(8,128)(2,1)S(1)} %bitcast.15), channel_id=1, replica_groups=mesh['yl'=2,'z'=12,'fsdp'=32] {'yl','fsdp'}, dimensions={0} | all-to-all | bytes 1048576 | tf_op jit(solution)/shard_map/all_to_all | solution.py:282
  153.7 0.8 shard_map.100
  154.5 9.4 %all-to-all-start.3 = ((bf16[24,8,512]{2,1,0:T(8,128)(2,1)}), bf16[24,8,512]{2,1,0:T(8,128)(2,1)S(1)}, u32[]{:S(2)}, u32[]{:S(2)}) async-start(bf16[24,8,512]{2,1,0:T(8,128)(2,1)} %bitcast.10), calls=%async_computation.3 | async-start | bytes 393216 | tf_op jit(solution)/shard_map/all_to_all | solution.py:282
  163.9 1.5 shard_map.98
  165.4 10.5 %all-to-all-done.3 = bf16[24,8,512]{2,1,0:T(8,128)(2,1)S(1)} async-done(((bf16[24,8,512]{2,1,0:T(8,128)(2,1)}), bf16[24,8,512]{2,1,0:T(8,128)(2,1)S(1)}, u32[]{:S(2)}, u32[]{:S(2)}) %all-to-all-start.3) | async-done | bytes 196640 | tf_op jit(solution)/shard_map/all_to_all | solution.py:282
  176.0 0.6 shard_map.101
Async XLA Ops:
  2.5 18.0 %collective-permute-start = (bf16[32,2048]{1,0:T(8,128)(2,1)S(1)}, bf16[32,2048]{1,0:T(8,128)(2,1)S(1)}, u32[]{:S(2)}, u32[]{:S(2)}) collective-permute-start(bf16[32,2048]{1,0:T(8,128)(2,1)S(1)} %get-tuple-element.13), channel_id=1, source_target_pairs={{0,32},{32,64},{64,96},{96,128},{128,160},{160,192},{192,224},{224... | collective-permute-start | bytes 393224 | tf_op jit(solution)/shard_map/ppermute | solution.py:362
  6.8 14.9 %collective-permute-start.1 = (bf16[32,2048]{1,0:T(8,128)(2,1)S(1)}, bf16[32,2048]{1,0:T(8,128)(2,1)S(1)}, u32[]{:S(2)}, u32[]{:S(2)}) collective-permute-start(bf16[32,2048]{1,0:T(8,128)(2,1)S(1)} %get-tuple-element.14), channel_id=1, source_target_pairs={{32,0},{64,32},{96,64},{128,96},{160,128},{192,160},{224,192},{256... | collective-permute-start | bytes 393224 | tf_op jit(solution)/shard_map/ppermute | solution.py:363
  21.6 1.1 copy-start
  22.8 0.7 copy-start.2
  24.7 51.2 %copy-start.3 = (bf16[1,2048,768]{2,1,0:T(8,128)(2,1)S(1)}, bf16[1,2048,768]{2,1,0:T(8,128)(2,1)}, u32[]{:S(2)}) copy-start(bf16[1,2048,768]{2,1,0:T(8,128)(2,1)} %gate_ref.1) | copy-start | bytes 9437188
  76.0 1.9 %copy-start.4 = (bf16[1,2048,768]{2,1,0:T(8,128)(2,1)S(1)}, bf16[1,2048,768]{2,1,0:T(8,128)(2,1)}, u32[]{:S(2)}) copy-start(bf16[1,2048,768]{2,1,0:T(8,128)(2,1)} %up_ref.1) | copy-start | bytes 9437188
  83.8 45.2 %copy-start.1 = (bf16[128,2048]{1,0:T(8,128)(2,1)S(1)}, bf16[128,2048]{1,0:T(8,128)(2,1)}, u32[]{:S(2)}) copy-start(bf16[128,2048]{1,0:T(8,128)(2,1)} %grad_ref.1) | copy-start | bytes 1572868
  154.5 21.4 %all-to-all-start.3 = ((bf16[24,8,512]{2,1,0:T(8,128)(2,1)}), bf16[24,8,512]{2,1,0:T(8,128)(2,1)S(1)}, u32[]{:S(2)}, u32[]{:S(2)}) async-start(bf16[24,8,512]{2,1,0:T(8,128)(2,1)} %bitcast.10), calls=%async_computation.3 | async-start | bytes 393216 | tf_op jit(solution)/shard_map/all_to_all | solution.py:282

commit v5 on v4

--- a/solution.py
+++ b/solution.py
@@ -16,8 +16,8 @@
 TOK_DEV = 128
 SRC_DEV = 192
 MOVE = 32
-NEAR = 48
 CAP = 12
+SPAN = SRC_DEV + 2 * MOVE
 WHOLE = 8
 ROWS = WIN * WHOLE
 WIDTH = D + HALF
@@ -60,13 +60,6 @@
     )
 
 
-def live_of(rank_ref, flows_ref):
-    rank = rank_ref[0]
-    own = flows_ref[0, rank]
-    left = flows_ref[0, jnp.where(rank == 0, 23, rank - 1)]
-    return left, TOK_DEV + own - left
-
-
 def border_kernel(
     rank_ref,
     flows_hbm,
@@ -75,6 +68,8 @@
     logits_hbm,
     head_ref,
     tail_ref,
+    held_ref,
+    settle_ref,
     place_ref,
     late_ref,
     weight_ref,
@@ -83,7 +78,6 @@
     late_high_ref,
     late_low_ref,
     flows,
-    near,
     ids,
     logits,
     sems,
@@ -91,16 +85,11 @@
     flow_copy = pltpu.make_async_copy(flows_hbm, flows, sems.at[0])
     ids_copy = pltpu.make_async_copy(ids_hbm, ids, sems.at[1])
     logits_copy = pltpu.make_async_copy(logits_hbm, logits, sems.at[2])
-    head_copy = pltpu.make_async_copy(rollout_hbm.at[pl.ds(0, MOVE)], head_ref, sems.at[3])
+    held_copy = pltpu.make_async_copy(rollout_hbm, held_ref, sems.at[3])
     flow_copy.start()
     ids_copy.start()
     logits_copy.start()
-    head_copy.start()
-    flow_copy.wait()
-    _, live = live_of(rank_ref, flows)
-    begin = pl.multiple_of(jnp.minimum((live - MOVE) >> 4, (SRC_DEV - NEAR) >> 4) * 16, 16)
-    near_copy = pltpu.make_async_copy(rollout_hbm.at[pl.ds(begin, NEAR)], near, sems.at[4])
-    near_copy.start()
+    held_copy.start()
     ids_copy.wait()
     logits_copy.wait()
     route(
@@ -112,11 +101,18 @@
         (high_ref, low_ref),
         (late_high_ref, late_low_ref),
     )
-    at = iota((MOVE, NEAR), 0) + (live - MOVE - begin)
-    pick = (iota((MOVE, NEAR), 1) == at).astype(bf16)
-    near_copy.wait()
-    tail_ref[...] = mm(pick, near[...]).astype(bf16)
-    head_copy.wait()
+    flow_copy.wait()
+    rank = rank_ref[0]
+    left = flows[0, jnp.where(rank == 0, 23, rank - 1)]
+    live = TOK_DEV + flows[0, rank] - left
+    at = iota((TOK_DEV, SPAN), 0) + (MOVE - left)
+    at = jnp.where(at < MOVE + live, at, at + (SRC_DEV - live))
+    settle_ref[...] = (iota((TOK_DEV, SPAN), 1) == at).astype(bf16)
+    at = iota((MOVE, SRC_DEV), 0) + (live - MOVE)
+    pick = (iota((MOVE, SRC_DEV), 1) == at).astype(bf16)
+    held_copy.wait()
+    head_ref[...] = held_ref[:MOVE, :]
+    tail_ref[...] = mm(pick, held_ref[...]).astype(bf16)
 
 
 def route(ids, logits, place_ref, late_ref, weight_ref, parts_refs, late_parts_refs):
@@ -158,23 +154,10 @@
 
 
 def dispatch_kernel(
-    rank_ref,
-    flows_ref,
-    left_ref,
-    right_ref,
-    rollout_ref,
-    place_ref,
-    late_ref,
-    out_ref,
-    bal_ref,
+    left_ref, right_ref, held_ref, settle_ref, place_ref, late_ref, out_ref, bal_ref
 ):
-    left, live = live_of(rank_ref, flows_ref)
-    span = SRC_DEV + 2 * MOVE
-    at = iota((TOK_DEV, span), 0) + (MOVE - left)
-    at = jnp.where(at < MOVE + live, at, at + (SRC_DEV - live))
-    settle = (iota((TOK_DEV, span), 1) == at).astype(bf16)
-    rows = jnp.concatenate([left_ref[...], rollout_ref[...], right_ref[...]], axis=0)
-    balanced = mm(settle, rows).astype(bf16)
+    rows = jnp.concatenate([left_ref[...], held_ref[...], right_ref[...]], axis=0)
+    balanced = mm(settle_ref[...], rows).astype(bf16)
     bal_ref[...] = balanced
     out_ref[:, :D] = mm(place_ref[...], balanced).astype(bf16)
     out_ref[:, D:] = mm(late_ref[...], halves(balanced)).astype(bf16)
@@ -185,8 +168,14 @@
     return ((row >> 2) & 15) * 8 + (row >> 6) * 4 + (row & 3)
 
 
-def ffn_kernel(rows_ref, gate_ref, up_ref, down_hbm, out_ref, down, x, hidden, sem):
-    down_copy = pltpu.make_async_copy(down_hbm.at[0], down, sem)
+def ffn_kernel(rows_ref, gate_ref, up_hbm, down_hbm, out_ref, up, down, x, hidden, sems):
+    parts = FF // FF_CHUNK
+    up_copies = []
+    for f in range(parts):
+        cols = pl.ds(f * FF_CHUNK, FF_CHUNK)
+        up_copies.append(pltpu.make_async_copy(up_hbm.at[0, :, cols], up.at[f], sems.at[f]))
+        up_copies[f].start()
+    down_copy = pltpu.make_async_copy(down_hbm.at[0], down, sems.at[parts])
     down_copy.start()
     ordered = (iota((BLOCK, BLOCK), 1) == block_source(0)).astype(bf16)
     back = (iota((BLOCK, BLOCK), 0) == block_source(1)).astype(bf16)
@@ -197,10 +186,13 @@
         mine = slice(ROWS + b * part_rows, ROWS + (b + 1) * part_rows)
         x[mine, :HALF] = y[:part_rows]
         x[mine, HALF:] = y[part_rows:]
-    for f in range(FF // FF_CHUNK):
+    gates = [
+        mm(x[...], gate_ref[0, :, f * FF_CHUNK : (f + 1) * FF_CHUNK]) for f in range(parts)
+    ]
+    for f, g in enumerate(gates):
+        up_copies[f].wait()
+        u = mm(x[...], up[f])
         cols = slice(f * FF_CHUNK, (f + 1) * FF_CHUNK)
-        g = mm(x[...], gate_ref[0, :, cols])
-        u = mm(x[...], up_ref[0, :, cols])
         hidden[:, cols] = (g / (1.0 + jnp.exp(-g)) * u).astype(bf16)
     down_copy.wait()
     late = []
@@ -288,6 +280,8 @@
         [
             shape((MOVE, D), bf16),
             shape((MOVE, D), bf16),
+            shape((SRC_DEV, D), bf16),
+            shape((TOK_DEV, SPAN), bf16),
             shape((ROWS, TOK_DEV), bf16),
             shape((ROWS, 2 * TOK_DEV), bf16),
             shape((EXPERTS, TOK_DEV), f32),
@@ -300,36 +294,36 @@
         25_000_000,
         [
             pltpu.SMEM((1, 24), i32),
-            pltpu.VMEM((NEAR, D), bf16),
             pltpu.VMEM((TOPK, TOK_DEV), i32),
             pltpu.VMEM((TOPK, TOK_DEV), f32),
-            pltpu.SemaphoreType.DMA((5,)),
+            pltpu.SemaphoreType.DMA((4,)),
         ],
     )(rank, *[in_hbm(v) for v in (flows, rollout, ids, logits)])
 
 
-def dispatch(rank, flows, left, right, rollout, place, late):
+def dispatch(left, right, held, settle, place, late):
     return call(
         dispatch_kernel,
         [shape((ROWS, WIDTH), bf16), shape((TOK_DEV, D), bf16)],
-        [SMEM, SMEM] + [VMEM] * 5,
+        [VMEM] * 6,
         550_000_000,
-    )(rank, flows, left, right, rollout, place, late)
+    )(left, right, held, settle, place, late)
 
 
 def ffn(rows, w_gate, w_up, w_down):
     return call(
         ffn_kernel,
         shape((ROWS, WIDTH), bf16),
-        [VMEM, VMEM, VMEM, HBM],
+        [VMEM, VMEM, HBM, HBM],
         3_700_000_000,
         [
+            pltpu.VMEM((FF // FF_CHUNK, D, FF_CHUNK), bf16),
             pltpu.VMEM((FF, D), bf16),
             pltpu.VMEM((SLOTS, D), bf16),
             pltpu.VMEM((SLOTS, FF), bf16),
-            pltpu.SemaphoreType.DMA,
+            pltpu.SemaphoreType.DMA((FF // FF_CHUNK + 1,)),
         ],
-    )(rows, w_gate, w_up, in_hbm(w_down))
+    )(rows, w_gate, in_hbm(w_up), in_hbm(w_down))
 
 
 def router_terms(rows, grad_out, balanced, place, late, weight):
@@ -356,12 +350,12 @@
     ranks = lax.axis_size(DP)
     rank = lax.axis_index(DP).reshape(1)
     flows = flows.T
-    head, tail, place, late, weight, *shares = borders(
+    head, tail, held, settle, place, late, weight, *shares = borders(
         rank, flows, rollout, route_ids.T, route_logits.T
     )
     left = lax.ppermute(tail, DP, [(i, (i + 1) % ranks) for i in range(ranks)])
     right = lax.ppermute(head, DP, [((i + 1) % ranks, i) for i in range(ranks)])
-    outgoing, balanced = dispatch(rank, flows, left, right, rollout, place, late)
+    outgoing, balanced = dispatch(left, right, held, settle, place, late)
     rows = exchange(outgoing, "fsdp", WIN)
     computed = ffn(rows, w_gate, w_up, w_down)
     returned = exchange(computed, "fsdp", WIN)

time: 177 us -> 174 us (0.983)
  local copies, waits for them, and re-layouts: 3.69 us -> 0.01 us
    unnamed x10 -> x4, local copies, waits for them, and re-layouts: 3.69 us -> 0.01 us
where the time goes in v5:
time: 174 us
  blocking collectives  120 us (69%)
  starting transfers between devices  25.8 us (15%)
  Pallas kernels  14 us (8%)
  waiting for transfers between devices  13.2 us (8%)
    all_to_all x3, blocking collectives, exchange(): lax.all_to_all(apart, axes, split_axis=0, concat_axis=0, tiled=True)  120 us
    ppermute x1, starting transfers between devices, shards(): right = lax.ppermute(head, DP, [((i + 1) % ranks, i) for i in range(ranks)])  12.1 us
    all_to_all x1, waiting for transfers between devices, exchange(): lax.all_to_all(apart, axes, split_axis=0, concat_axis=0, tiled=True)  10.5 us
    all_to_all x1, starting transfers between devices, exchange(): lax.all_to_all(apart, axes, split_axis=0, concat_axis=0, tiled=True)  9.37 us
    pallas_call x1, Pallas kernels, ffn(): call(ffn_kernel, shape((ROWS, WIDTH), bf16), [VMEM, VMEM, HBM, HBM], 3700...  7.37 us
    ppermute x1, starting transfers between devices, shards(): left = lax.ppermute(tail, DP, [(i, (i + 1) % ranks) for i in range(ranks)])  4.28 us
  transfers between devices with their start and end apart: 3, of which 3 were waited for; matrix products, arithmetic and copies ran while one was open for 0% of the time, Pallas kernels for 1%

profile of v5, /device:TPU:8, one launch (start us, length us, event | category | flops | bytes accessed | tf_op | source)
XLA Modules:
  0.0 173.6 jit_solution(11640834746841652841)
XLA Ops:
  0.6 1.6 shard_map.95
  2.2 4.3 %collective-permute-start = (bf16[32,2048]{1,0:T(8,128)(2,1)S(1)}, bf16[32,2048]{1,0:T(8,128)(2,1)S(1)}, u32[]{:S(2)}, u32[]{:S(2)}) collective-permute-start(bf16[32,2048]{1,0:T(8,128)(2,1)S(1)} %get-tuple-element.15), channel_id=1, source_target_pairs={{0,32},{32,64},{64,96},{96,128},{128,160},{160,192},{192,224},{224... | collective-permute-start | bytes 393224 | tf_op jit(solution)/shard_map/ppermute | solution.py:356
  6.5 12.1 %collective-permute-start.1 = (bf16[32,2048]{1,0:T(8,128)(2,1)S(1)}, bf16[32,2048]{1,0:T(8,128)(2,1)S(1)}, u32[]{:S(2)}, u32[]{:S(2)}) collective-permute-start(bf16[32,2048]{1,0:T(8,128)(2,1)S(1)} %get-tuple-element.16), channel_id=1, source_target_pairs={{32,0},{64,32},{96,64},{128,96},{160,128},{192,160},{224,192},{256... | collective-permute-start | bytes 393224 | tf_op jit(solution)/shard_map/ppermute | solution.py:357
  18.7 1.6 collective-permute-done.left_ref
  20.2 1.2 collective-permute-done.1.right_ref
  21.4 0.7 shard_map.96
  22.1 0.0 copy-start.1
  22.2 51.2 %all_to_all.20 = bf16[32,8,3072]{2,1,0:T(8,128)(2,1)S(1)} all-to-all(bf16[32,8,3072]{2,1,0:T(8,128)(2,1)S(1)} %bitcast.16), channel_id=1, replica_groups=mesh['yl'=2,'z'=12,'fsdp'=32] {'fsdp'}, dimensions={0} | all-to-all | bytes 3145728 | tf_op jit(solution)/shard_map/all_to_all | solution.py:274
  73.3 0.0 copy-done.1
  73.3 7.4 %shard_map.97 = bf16[256,3072]{1,0:T(8,128)(2,1)S(1)} custom-call(bf16[256,3072]{1,0:T(8,128)(2,1)S(1)} %bitcast.17, bf16[1,2048,768]{2,1,0:T(8,128)(2,1)S(1)} %copy-done.1, bf16[1,2048,768]{2,1,0:T(8,128)(2,1)} %up_hbm.1, bf16[1,768,2048]{2,1,0:T(8,128)(2,1)} %down_hbm.1), custom_call_target="tpu_custom_call" | custom-call | flops 3700000000 | bytes 3145728 | tf_op jit(solution)/shard_map/pallas_call | solution.py:314
  80.7 0.0 copy-start
  80.7 45.2 %all_to_all.21 = bf16[32,8,3072]{2,1,0:T(8,128)(2,1)S(1)} all-to-all(bf16[32,8,3072]{2,1,0:T(8,128)(2,1)S(1)} %bitcast.18), channel_id=1, replica_groups=mesh['yl'=2,'z'=12,'fsdp'=32] {'fsdp'}, dimensions={0} | all-to-all | bytes 3145728 | tf_op jit(solution)/shard_map/all_to_all | solution.py:274
  125.9 0.0 copy-done
  125.9 1.4 shard_map.99
  127.3 23.5 %all_to_all.22 = bf16[64,8,512]{2,1,0:T(8,128)(2,1)S(1)} all-to-all(bf16[64,8,512]{2,1,0:T(8,128)(2,1)S(1)} %bitcast.15), channel_id=1, replica_groups=mesh['yl'=2,'z'=12,'fsdp'=32] {'yl','fsdp'}, dimensions={0} | all-to-all | bytes 1048576 | tf_op jit(solution)/shard_map/all_to_all | solution.py:274
  150.8 0.8 shard_map.100
  151.5 9.4 %all-to-all-start.3 = ((bf16[24,8,512]{2,1,0:T(8,128)(2,1)}), bf16[24,8,512]{2,1,0:T(8,128)(2,1)S(1)}, u32[]{:S(2)}, u32[]{:S(2)}) async-start(bf16[24,8,512]{2,1,0:T(8,128)(2,1)} %bitcast.10), calls=%async_computation.3 | async-start | bytes 393216 | tf_op jit(solution)/shard_map/all_to_all | solution.py:274
  160.9 1.5 shard_map.98
  162.4 10.5 %all-to-all-done.3 = bf16[24,8,512]{2,1,0:T(8,128)(2,1)S(1)} async-done(((bf16[24,8,512]{2,1,0:T(8,128)(2,1)}), bf16[24,8,512]{2,1,0:T(8,128)(2,1)S(1)}, u32[]{:S(2)}, u32[]{:S(2)}) %all-to-all-start.3) | async-done | bytes 196640 | tf_op jit(solution)/shard_map/all_to_all | solution.py:274
  172.9 0.6 shard_map.101
Async XLA Ops:
  2.2 18.0 %collective-permute-start = (bf16[32,2048]{1,0:T(8,128)(2,1)S(1)}, bf16[32,2048]{1,0:T(8,128)(2,1)S(1)}, u32[]{:S(2)}, u32[]{:S(2)}) collective-permute-start(bf16[32,2048]{1,0:T(8,128)(2,1)S(1)} %get-tuple-element.15), channel_id=1, source_target_pairs={{0,32},{32,64},{64,96},{96,128},{128,160},{160,192},{192,224},{224... | collective-permute-start | bytes 393224 | tf_op jit(solution)/shard_map/ppermute | solution.py:356
  6.5 14.9 %collective-permute-start.1 = (bf16[32,2048]{1,0:T(8,128)(2,1)S(1)}, bf16[32,2048]{1,0:T(8,128)(2,1)S(1)}, u32[]{:S(2)}, u32[]{:S(2)}) collective-permute-start(bf16[32,2048]{1,0:T(8,128)(2,1)S(1)} %get-tuple-element.16), channel_id=1, source_target_pairs={{32,0},{64,32},{96,64},{128,96},{160,128},{192,160},{224,192},{256... | collective-permute-start | bytes 393224 | tf_op jit(solution)/shard_map/ppermute | solution.py:357
  22.1 51.2 %copy-start.1 = (bf16[1,2048,768]{2,1,0:T(8,128)(2,1)S(1)}, bf16[1,2048,768]{2,1,0:T(8,128)(2,1)}, u32[]{:S(2)}) copy-start(bf16[1,2048,768]{2,1,0:T(8,128)(2,1)} %gate_ref.1) | copy-start | bytes 9437188
  80.7 45.2 %copy-start = (bf16[128,2048]{1,0:T(8,128)(2,1)S(1)}, bf16[128,2048]{1,0:T(8,128)(2,1)}, u32[]{:S(2)}) copy-start(bf16[128,2048]{1,0:T(8,128)(2,1)} %grad_ref.1) | copy-start | bytes 1572868
  151.5 21.4 %all-to-all-start.3 = ((bf16[24,8,512]{2,1,0:T(8,128)(2,1)}), bf16[24,8,512]{2,1,0:T(8,128)(2,1)S(1)}, u32[]{:S(2)}, u32[]{:S(2)}) async-start(bf16[24,8,512]{2,1,0:T(8,128)(2,1)} %bitcast.10), calls=%async_computation.3 | async-start | bytes 393216 | tf_op jit(solution)/shard_map/all_to_all | solution.py:274

commit v6 on v5

--- a/solution.py
+++ b/solution.py
@@ -168,15 +168,7 @@
     return ((row >> 2) & 15) * 8 + (row >> 6) * 4 + (row & 3)
 
 
-def ffn_kernel(rows_ref, gate_ref, up_hbm, down_hbm, out_ref, up, down, x, hidden, sems):
-    parts = FF // FF_CHUNK
-    up_copies = []
-    for f in range(parts):
-        cols = pl.ds(f * FF_CHUNK, FF_CHUNK)
-        up_copies.append(pltpu.make_async_copy(up_hbm.at[0, :, cols], up.at[f], sems.at[f]))
-        up_copies[f].start()
-    down_copy = pltpu.make_async_copy(down_hbm.at[0], down, sems.at[parts])
-    down_copy.start()
+def ffn_kernel(rows_ref, gate_ref, up_ref, down_ref, out_ref, x, hidden):
     ordered = (iota((BLOCK, BLOCK), 1) == block_source(0)).astype(bf16)
     back = (iota((BLOCK, BLOCK), 0) == block_source(1)).astype(bf16)
     part_rows = BLOCK // 2
@@ -186,19 +178,15 @@
         mine = slice(ROWS + b * part_rows, ROWS + (b + 1) * part_rows)
         x[mine, :HALF] = y[:part_rows]
         x[mine, HALF:] = y[part_rows:]
-    gates = [
-        mm(x[...], gate_ref[0, :, f * FF_CHUNK : (f + 1) * FF_CHUNK]) for f in range(parts)
-    ]
-    for f, g in enumerate(gates):
-        up_copies[f].wait()
-        u = mm(x[...], up[f])
+    for f in range(FF // FF_CHUNK):
         cols = slice(f * FF_CHUNK, (f + 1) * FF_CHUNK)
+        g = mm(x[...], gate_ref[0, :, cols])
+        u = mm(x[...], up_ref[0, :, cols])
         hidden[:, cols] = (g / (1.0 + jnp.exp(-g)) * u).astype(bf16)
-    down_copy.wait()
     late = []
     for half in range(2):
         cols = slice(half * HALF, (half + 1) * HALF)
-        y = mm(hidden[...], down[:, cols]).astype(bf16)
+        y = mm(hidden[...], down_ref[0, :, cols]).astype(bf16)
         out_ref[:, cols] = y[:ROWS]
         late.append(y[ROWS:])
     for b in range(ROWS // BLOCK):
@@ -306,7 +294,7 @@
         dispatch_kernel,
         [shape((ROWS, WIDTH), bf16), shape((TOK_DEV, D), bf16)],
         [VMEM] * 6,
-        550_000_000,
+        12_000_000_000,
     )(left, right, held, settle, place, late)
 
 
@@ -314,16 +302,10 @@
     return call(
         ffn_kernel,
         shape((ROWS, WIDTH), bf16),
-        [VMEM, VMEM, HBM, HBM],
+        [VMEM] * 4,
         3_700_000_000,
-        [
-            pltpu.VMEM((FF // FF_CHUNK, D, FF_CHUNK), bf16),
-            pltpu.VMEM((FF, D), bf16),
-            pltpu.VMEM((SLOTS, D), bf16),
-            pltpu.VMEM((SLOTS, FF), bf16),
-            pltpu.SemaphoreType.DMA((FF // FF_CHUNK + 1,)),
-        ],
-    )(rows, w_gate, in_hbm(w_up), in_hbm(w_down))
+        [pltpu.VMEM((SLOTS, D), bf16), pltpu.VMEM((SLOTS, FF), bf16)],
+    )(rows, w_gate, w_up, w_down)
 
 
 def router_terms(rows, grad_out, balanced, place, late, weight):

time: 174 us -> 171 us (0.983)
  Pallas kernels: 14 us -> 10.8 us
    pallas_call x1, Pallas kernels: 7.37 us -> 4.16 us  [ffn(): call(ffn_kernel, shape((ROWS, WIDTH), bf16), [VMEM] * 4, 3700000000, [plt...]
where the time goes in v6:
time: 171 us; the launch traced here: 170 us
  blocking collectives  120 us (70%)
  starting transfers between devices  25.8 us (15%)
  waiting for transfers between devices  13.2 us (8%)
  Pallas kernels  10.8 us (6%)
    all_to_all x3, blocking collectives, exchange(): lax.all_to_all(apart, axes, split_axis=0, concat_axis=0, tiled=True)  120 us
    ppermute x1, starting transfers between devices, shards(): right = lax.ppermute(head, DP, [((i + 1) % ranks, i) for i in range(ranks)])  12.1 us
    all_to_all x1, waiting for transfers between devices, exchange(): lax.all_to_all(apart, axes, split_axis=0, concat_axis=0, tiled=True)  10.5 us
    all_to_all x1, starting transfers between devices, exchange(): lax.all_to_all(apart, axes, split_axis=0, concat_axis=0, tiled=True)  9.39 us
    ppermute x1, starting transfers between devices, shards(): left = lax.ppermute(tail, DP, [(i, (i + 1) % ranks) for i in range(ranks)])  4.28 us
    pallas_call x1, Pallas kernels, ffn(): call(ffn_kernel, shape((ROWS, WIDTH), bf16), [VMEM] * 4, 3700000000, [plt...  4.16 us
  transfers between devices with their start and end apart: 3, of which 3 were waited for; matrix products, arithmetic and copies ran while one was open for 0% of the time, Pallas kernels for 1%

profile of v6, /device:TPU:8, one launch (start us, length us, event | category | flops | bytes accessed | tf_op | source)
XLA Modules:
  0.0 170.4 jit_solution(14153425078017127221)
XLA Ops:
  0.6 1.6 shard_map.95
  2.2 4.3 %collective-permute-start = (bf16[32,2048]{1,0:T(8,128)(2,1)S(1)}, bf16[32,2048]{1,0:T(8,128)(2,1)S(1)}, u32[]{:S(2)}, u32[]{:S(2)}) collective-permute-start(bf16[32,2048]{1,0:T(8,128)(2,1)S(1)} %get-tuple-element.15), channel_id=1, source_target_pairs={{0,32},{32,64},{64,96},{96,128},{128,160},{160,192},{192,224},{224... | collective-permute-start | bytes 393224 | tf_op jit(solution)/shard_map/ppermute | solution.py:338
  6.5 12.1 %collective-permute-start.1 = (bf16[32,2048]{1,0:T(8,128)(2,1)S(1)}, bf16[32,2048]{1,0:T(8,128)(2,1)S(1)}, u32[]{:S(2)}, u32[]{:S(2)}) collective-permute-start(bf16[32,2048]{1,0:T(8,128)(2,1)S(1)} %get-tuple-element.16), channel_id=1, source_target_pairs={{32,0},{64,32},{96,64},{128,96},{160,128},{192,160},{224,192},{256... | collective-permute-start | bytes 393224 | tf_op jit(solution)/shard_map/ppermute | solution.py:339
  18.7 1.6 collective-permute-done.left_ref
  20.2 1.2 collective-permute-done.1.right_ref
  21.4 0.0 copy-start.2
  21.4 0.0 copy-start.3
  21.4 0.7 shard_map.96
  22.1 0.0 copy-start.1
  22.2 51.2 %all_to_all.20 = bf16[32,8,3072]{2,1,0:T(8,128)(2,1)S(1)} all-to-all(bf16[32,8,3072]{2,1,0:T(8,128)(2,1)S(1)} %bitcast.16), channel_id=1, replica_groups=mesh['yl'=2,'z'=12,'fsdp'=32] {'fsdp'}, dimensions={0} | all-to-all | bytes 3145728 | tf_op jit(solution)/shard_map/all_to_all | solution.py:262
  73.4 0.0 copy-done.2
  73.4 0.0 copy-done.3
  73.4 0.0 copy-done.1
  73.4 4.2 %shard_map.97 = bf16[256,3072]{1,0:T(8,128)(2,1)S(1)} custom-call(bf16[256,3072]{1,0:T(8,128)(2,1)S(1)} %bitcast.17, bf16[1,2048,768]{2,1,0:T(8,128)(2,1)S(1)} %copy-done.1, bf16[1,2048,768]{2,1,0:T(8,128)(2,1)S(1)} %copy-done.2, bf16[1,768,2048]{2,1,0:T(8,128)(2,1)S(1)} %copy-done.3), custom_call_target="tpu_custom_call" | custom-call | flops 3700000000 | bytes 3145728 | tf_op jit(solution)/shard_map/pallas_call | solution.py:302
  77.6 0.0 copy-start
  77.6 45.1 %all_to_all.21 = bf16[32,8,3072]{2,1,0:T(8,128)(2,1)S(1)} all-to-all(bf16[32,8,3072]{2,1,0:T(8,128)(2,1)S(1)} %bitcast.18), channel_id=1, replica_groups=mesh['yl'=2,'z'=12,'fsdp'=32] {'fsdp'}, dimensions={0} | all-to-all | bytes 3145728 | tf_op jit(solution)/shard_map/all_to_all | solution.py:262
  122.7 0.0 copy-done
  122.7 1.4 shard_map.99
  124.1 23.4 %all_to_all.22 = bf16[64,8,512]{2,1,0:T(8,128)(2,1)S(1)} all-to-all(bf16[64,8,512]{2,1,0:T(8,128)(2,1)S(1)} %bitcast.15), channel_id=1, replica_groups=mesh['yl'=2,'z'=12,'fsdp'=32] {'yl','fsdp'}, dimensions={0} | all-to-all | bytes 1048576 | tf_op jit(solution)/shard_map/all_to_all | solution.py:262
  147.5 0.8 shard_map.100
  148.3 9.4 %all-to-all-start.3 = ((bf16[24,8,512]{2,1,0:T(8,128)(2,1)}), bf16[24,8,512]{2,1,0:T(8,128)(2,1)S(1)}, u32[]{:S(2)}, u32[]{:S(2)}) async-start(bf16[24,8,512]{2,1,0:T(8,128)(2,1)} %bitcast.10), calls=%async_computation.3 | async-start | bytes 393216 | tf_op jit(solution)/shard_map/all_to_all | solution.py:262
  157.7 1.5 shard_map.98
  159.2 10.5 %all-to-all-done.3 = bf16[24,8,512]{2,1,0:T(8,128)(2,1)S(1)} async-done(((bf16[24,8,512]{2,1,0:T(8,128)(2,1)}), bf16[24,8,512]{2,1,0:T(8,128)(2,1)S(1)}, u32[]{:S(2)}, u32[]{:S(2)}) %all-to-all-start.3) | async-done | bytes 196640 | tf_op jit(solution)/shard_map/all_to_all | solution.py:262
  169.7 0.6 shard_map.101
Async XLA Ops:
  2.2 18.0 %collective-permute-start = (bf16[32,2048]{1,0:T(8,128)(2,1)S(1)}, bf16[32,2048]{1,0:T(8,128)(2,1)S(1)}, u32[]{:S(2)}, u32[]{:S(2)}) collective-permute-start(bf16[32,2048]{1,0:T(8,128)(2,1)S(1)} %get-tuple-element.15), channel_id=1, source_target_pairs={{0,32},{32,64},{64,96},{96,128},{128,160},{160,192},{192,224},{224... | collective-permute-start | bytes 393224 | tf_op jit(solution)/shard_map/ppermute | solution.py:338
  6.5 14.9 %collective-permute-start.1 = (bf16[32,2048]{1,0:T(8,128)(2,1)S(1)}, bf16[32,2048]{1,0:T(8,128)(2,1)S(1)}, u32[]{:S(2)}, u32[]{:S(2)}) collective-permute-start(bf16[32,2048]{1,0:T(8,128)(2,1)S(1)} %get-tuple-element.16), channel_id=1, source_target_pairs={{32,0},{64,32},{96,64},{128,96},{160,128},{192,160},{224,192},{256... | collective-permute-start | bytes 393224 | tf_op jit(solution)/shard_map/ppermute | solution.py:339
  21.4 52.0 %copy-start.2 = (bf16[1,2048,768]{2,1,0:T(8,128)(2,1)S(1)}, bf16[1,2048,768]{2,1,0:T(8,128)(2,1)}, u32[]{:S(2)}) copy-start(bf16[1,2048,768]{2,1,0:T(8,128)(2,1)} %up_ref.1) | copy-start | bytes 9437188
  21.4 52.0 %copy-start.3 = (bf16[1,768,2048]{2,1,0:T(8,128)(2,1)S(1)}, bf16[1,768,2048]{2,1,0:T(8,128)(2,1)}, u32[]{:S(2)}) copy-start(bf16[1,768,2048]{2,1,0:T(8,128)(2,1)} %down_ref.1) | copy-start | bytes 9437188
  22.1 51.3 %copy-start.1 = (bf16[1,2048,768]{2,1,0:T(8,128)(2,1)S(1)}, bf16[1,2048,768]{2,1,0:T(8,128)(2,1)}, u32[]{:S(2)}) copy-start(bf16[1,2048,768]{2,1,0:T(8,128)(2,1)} %gate_ref.1) | copy-start | bytes 9437188
  77.6 45.1 %copy-start = (bf16[128,2048]{1,0:T(8,128)(2,1)S(1)}, bf16[128,2048]{1,0:T(8,128)(2,1)}, u32[]{:S(2)}) copy-start(bf16[128,2048]{1,0:T(8,128)(2,1)} %grad_ref.1) | copy-start | bytes 1572868
  148.3 21.4 %all-to-all-start.3 = ((bf16[24,8,512]{2,1,0:T(8,128)(2,1)}), bf16[24,8,512]{2,1,0:T(8,128)(2,1)S(1)}, u32[]{:S(2)}, u32[]{:S(2)}) async-start(bf16[24,8,512]{2,1,0:T(8,128)(2,1)} %bitcast.10), calls=%async_computation.3 | async-start | bytes 393216 | tf_op jit(solution)/shard_map/all_to_all | solution.py:262

commit v7 on v6

--- a/solution.py
+++ b/solution.py
@@ -24,6 +24,8 @@
 SLOTS = WIN * CAP
 BLOCK = 128
 DP = ("yl", "z")
+FSDP = ("chip", "core")
+CHIPS = 16
 FF_CHUNK = 256
 bf16, f32, i32 = jnp.bfloat16, jnp.float32, jnp.int32
 VMEM = pl.BlockSpec(memory_space=pltpu.VMEM)
@@ -62,6 +64,7 @@
 
 def border_kernel(
     rank_ref,
+    core_ref,
     flows_hbm,
     rollout_hbm,
     ids_hbm,
@@ -70,6 +73,7 @@
     tail_ref,
     held_ref,
     settle_ref,
+    order_ref,
     place_ref,
     late_ref,
     weight_ref,
@@ -101,6 +105,10 @@
         (high_ref, low_ref),
         (late_high_ref, late_low_ref),
     )
+    line = iota((2 * EXPERTS, EXPERTS), 0)
+    core = jnp.where(line < EXPERTS, core_ref[0], 1 - core_ref[0])
+    expert = ((line >> 3) & 15) * 8 + 4 * core + (line & 3)
+    order_ref[...] = (iota((2 * EXPERTS, EXPERTS), 1) == expert).astype(bf16)
     flow_copy.wait()
     rank = rank_ref[0]
     left = flows[0, jnp.where(rank == 0, 23, rank - 1)]
@@ -199,7 +207,17 @@
     return lax.dot_general(a, b, (((1,), (1,)), ((), ())), preferred_element_type=f32)
 
 
-def terms_kernel(rows_ref, grad_ref, bal_ref, place_ref, late_ref, weight_ref, out_ref):
+def terms_kernel(
+    rows_ref,
+    grad_ref,
+    bal_ref,
+    order_ref,
+    place_ref,
+    late_ref,
+    weight_ref,
+    other_ref,
+    factor_ref,
+):
     cotangent = grad_ref[...]
     scores = against(rows_ref[:, :D], cotangent) * place_ref[...].astype(f32)
     late = against(rows_ref[:, D:], halves(cotangent)) * late_ref[...].astype(f32)
@@ -211,18 +229,28 @@
         [weight[:WIN] * (score - total), weight[WIN:] * (0.0 - total)], axis=0
     )
     high, low = split2(grad)
-    line = iota((2 * EXPERTS, EXPERTS), 0)
-    order = (iota((2 * EXPERTS, EXPERTS), 1) == (line >> 3) * 4 + (line & 3)).astype(bf16)
     factor = jnp.concatenate(
-        [mm(order, high).astype(bf16), mm(order, low).astype(bf16)], axis=1
-    )
-    first = (iota((2 * EXPERTS, QUARTER), 0) & 4) == 0
+        [mm(order_ref[...], high).astype(bf16), mm(order_ref[...], low).astype(bf16)], axis=1
+    )
+    factor_ref[...] = factor[:EXPERTS]
     for half in range(2):
-        tokens = bal_ref[:, half * HALF : (half + 1) * HALF]
-        term = mm(factor, jnp.concatenate([tokens, tokens], axis=0))
-        out_ref[half * 2 * EXPERTS : (half + 1) * 2 * EXPERTS, :] = jnp.where(
-            first, term[:, :QUARTER], term[:, QUARTER:]
+        other_ref[half * EXPERTS : (half + 1) * EXPERTS, :] = half_terms(
+            factor[EXPERTS:], bal_ref, half
         ).astype(bf16)
+
+
+def half_terms(factor, bal_ref, half):
+    tokens = bal_ref[:, half * HALF : (half + 1) * HALF]
+    term = mm(factor, jnp.concatenate([tokens, tokens], axis=0))
+    first = (iota((EXPERTS, QUARTER), 0) & 4) == 0
+    return jnp.where(first, term[:, :QUARTER], term[:, QUARTER:])
+
+
+def join_kernel(factor_ref, bal_ref, given_ref, out_ref):
+    for half in range(2):
+        rows = slice(half * EXPERTS, (half + 1) * EXPERTS)
+        own = half_terms(factor_ref[...], bal_ref, half)
+        out_ref[rows, :] = (own + given_ref[rows, :].astype(f32)).astype(bf16)
 
 
 def output_kernel(rows_ref, high_ref, low_ref, late_high_ref, late_low_ref, out_ref):
@@ -234,7 +262,7 @@
 
 
 def part_kernel(terms_ref, out_ref):
-    part = jnp.sum(terms_ref[...].astype(f32).reshape(64, 8, QUARTER), axis=0)
+    part = jnp.sum(terms_ref[...].astype(f32).reshape(2 * CHIPS, 8, QUARTER), axis=0)
     two = jnp.concatenate([part, part], axis=0).astype(bf16)
     for i in range(12):
         out_ref[16 * i : 16 * (i + 1), :] = two
@@ -262,7 +290,7 @@
     return lax.all_to_all(apart, axes, split_axis=0, concat_axis=0, tiled=True).reshape(rows, cols)
 
 
-def borders(rank, flows, rollout, ids, logits):
+def borders(rank, core, flows, rollout, ids, logits):
     return call(
         border_kernel,
         [
@@ -270,6 +298,7 @@
             shape((MOVE, D), bf16),
             shape((SRC_DEV, D), bf16),
             shape((TOK_DEV, SPAN), bf16),
+            shape((2 * EXPERTS, EXPERTS), bf16),
             shape((ROWS, TOK_DEV), bf16),
             shape((ROWS, 2 * TOK_DEV), bf16),
             shape((EXPERTS, TOK_DEV), f32),
@@ -278,7 +307,7 @@
             shape((2 * TOK_DEV, ROWS), bf16),
             shape((2 * TOK_DEV, ROWS), bf16),
         ],
-        [SMEM] + [HBM] * 4,
+        [SMEM] * 2 + [HBM] * 4,
         25_000_000,
         [
             pltpu.SMEM((1, 24), i32),
@@ -286,7 +315,7 @@
             pltpu.VMEM((TOPK, TOK_DEV), f32),
             pltpu.SemaphoreType.DMA((4,)),
         ],
-    )(rank, *[in_hbm(v) for v in (flows, rollout, ids, logits)])
+    )(rank, core, *[in_hbm(v) for v in (flows, rollout, ids, logits)])
 
 
 def dispatch(left, right, held, settle, place, late):
@@ -308,9 +337,18 @@
     )(rows, w_gate, w_up, w_down)
 
 
-def router_terms(rows, grad_out, balanced, place, late, weight):
-    return call(terms_kernel, shape((4 * EXPERTS, QUARTER), bf16), [VMEM] * 6, 700_000_000)(
-        rows, grad_out, balanced, place, late, weight
+def router_terms(rows, grad_out, balanced, order, place, late, weight):
+    return call(
+        terms_kernel,
+        [shape((2 * EXPERTS, QUARTER), bf16), shape((EXPERTS, 2 * TOK_DEV), bf16)],
+        [VMEM] * 7,
+        500_000_000,
+    )(rows, grad_out, balanced, order, place, late, weight)
+
+
+def join(factor, balanced, given):
+    return call(join_kernel, shape((2 * EXPERTS, QUARTER), bf16), [VMEM] * 3, 150_000_000)(
+        factor, balanced, given
     )
 
 
@@ -331,31 +369,33 @@
 def shards(rollout, flows, route_ids, route_logits, grad_out, w_gate, w_up, w_down):
     ranks = lax.axis_size(DP)
     rank = lax.axis_index(DP).reshape(1)
+    core = lax.axis_index("core").reshape(1)
     flows = flows.T
-    head, tail, held, settle, place, late, weight, *shares = borders(
-        rank, flows, rollout, route_ids.T, route_logits.T
+    head, tail, held, settle, order, place, late, weight, *shares = borders(
+        rank, core, flows, rollout, route_ids.T, route_logits.T
     )
     left = lax.ppermute(tail, DP, [(i, (i + 1) % ranks) for i in range(ranks)])
     right = lax.ppermute(head, DP, [((i + 1) % ranks, i) for i in range(ranks)])
     outgoing, balanced = dispatch(left, right, held, settle, place, late)
-    rows = exchange(outgoing, "fsdp", WIN)
+    rows = exchange(outgoing, FSDP, WIN)
     computed = ffn(rows, w_gate, w_up, w_down)
-    returned = exchange(computed, "fsdp", WIN)
-    terms = router_terms(returned, grad_out, balanced, place, late, weight)
-    terms = exchange(terms, ("yl", "fsdp"), 64)
+    returned = exchange(computed, FSDP, WIN)
+    other, factor = router_terms(returned, grad_out, balanced, order, place, late, weight)
+    given = lax.ppermute(other, "core", [(0, 1), (1, 0)])
+    terms = exchange(join(factor, balanced, given), ("yl", "chip"), 2 * CHIPS)
     layer_out = layer_output(returned, *shares)
     parts = exchange(partial_sum(terms), DP, 24)
     return (layer_out, last_sum(parts))
 
 
 def solution(mesh):
-    fine = Mesh(mesh.devices.reshape(2, 12, 32), ("yl", "z", "fsdp"))
-    rows = P(("yl", "z", "fsdp"), None)
-    expert = P("fsdp", None, None)
+    fine = Mesh(mesh.devices.reshape(2, 12, CHIPS, 2), DP + FSDP)
+    rows = P(DP + FSDP, None)
+    expert = P(FSDP, None, None)
     return jax.shard_map(
         shards,
         mesh=fine,
-        in_specs=(rows, P(None, "fsdp"), rows, rows, rows, expert, expert, expert),
-        out_specs=(rows, P("fsdp", None)),
+        in_specs=(rows, P(None, FSDP), rows, rows, rows, expert, expert, expert),
+        out_specs=(rows, P(FSDP, None)),
         check_vma=False,
     )

time: 171 us -> 167 us (0.977)
  blocking collectives: 120 us -> 113 us
  starting transfers between devices: 25.8 us -> 27.6 us
    all_to_all x3, blocking collectives: 120 us -> 113 us  [exchange(): lax.all_to_all(apart, axes, split_axis=0, concat_axis=0, tiled=True)]
    ppermute x0 -> x1, starting transfers between devices: none -> 1.92 us  [shards(): given = lax.ppermute(other, 'core', [(0, 1), (1, 0)])]
  transfers between devices with their start and end apart: 3 -> 4, of which waited for: 3 -> 4; matrix products, arithmetic and copies ran while one was open for 0% -> 0% of each run, Pallas kernels for 1% -> 1%
where the time goes in v7:
time: 167 us
  blocking collectives  113 us (68%)
  starting transfers between devices  27.6 us (17%)
  waiting for transfers between devices  14.2 us (9%)
  Pallas kernels  11 us (7%)
    all_to_all x3, blocking collectives, exchange(): lax.all_to_all(apart, axes, split_axis=0, concat_axis=0, tiled=True)  113 us
    ppermute x1, starting transfers between devices, shards(): right = lax.ppermute(head, DP, [((i + 1) % ranks, i) for i in range(ranks)])  12.1 us
    all_to_all x1, waiting for transfers between devices, exchange(): lax.all_to_all(apart, axes, split_axis=0, concat_axis=0, tiled=True)  9.99 us
    all_to_all x1, starting transfers between devices, exchange(): lax.all_to_all(apart, axes, split_axis=0, concat_axis=0, tiled=True)  9.32 us
    ppermute x1, starting transfers between devices, shards(): left = lax.ppermute(tail, DP, [(i, (i + 1) % ranks) for i in range(ranks)])  4.29 us
    pallas_call x1, Pallas kernels, ffn(): call(ffn_kernel, shape((ROWS, WIDTH), bf16), [VMEM] * 4, 3700000000, [plt...  4.16 us
  transfers between devices with their start and end apart: 4, of which 4 were waited for; matrix products, arithmetic and copies ran while one was open for 0% of the time, Pallas kernels for 1%

profile of v7, /device:TPU:8, one launch (start us, length us, event | category | flops | bytes accessed | tf_op | source)
XLA Modules:
  0.0 166.8 jit_solution(3786909680881902526)
XLA Ops:
  0.6 1.6 shard_map.95
  2.2 4.3 %collective-permute-start = (bf16[32,2048]{1,0:T(8,128)(2,1)S(1)}, bf16[32,2048]{1,0:T(8,128)(2,1)S(1)}, u32[]{:S(2)}, u32[]{:S(2)}) collective-permute-start(bf16[32,2048]{1,0:T(8,128)(2,1)S(1)} %get-tuple-element.18), channel_id=1, source_target_pairs={{0,32},{32,64},{64,96},{96,128},{128,160},{160,192},{192,224},{224... | collective-permute-start | bytes 393224 | tf_op jit(solution)/shard_map/ppermute | solution.py:377
  6.5 12.1 %collective-permute-start.1 = (bf16[32,2048]{1,0:T(8,128)(2,1)S(1)}, bf16[32,2048]{1,0:T(8,128)(2,1)S(1)}, u32[]{:S(2)}, u32[]{:S(2)}) collective-permute-start(bf16[32,2048]{1,0:T(8,128)(2,1)S(1)} %get-tuple-element.19), channel_id=1, source_target_pairs={{32,0},{64,32},{96,64},{128,96},{160,128},{192,160},{224,192},{256... | collective-permute-start | bytes 393224 | tf_op jit(solution)/shard_map/ppermute | solution.py:378
  18.7 1.6 collective-permute-done.left_ref
  20.2 1.2 collective-permute-done.1.right_ref
  21.4 0.0 copy-start.2
  21.4 0.0 copy-start.3
  21.4 0.7 shard_map.96
  22.2 0.0 copy-start.1
  22.2 51.2 %all_to_all.20 = bf16[32,8,3072]{2,1,0:T(8,128)(2,1)S(1)} all-to-all(bf16[32,8,3072]{2,1,0:T(8,128)(2,1)S(1)} %bitcast.15), channel_id=1, replica_groups=mesh['yl'=2,'z'=12,'chip'=16,'core'=2] {'chip','core'}, dimensions={0} | all-to-all | bytes 3145728 | tf_op jit(solution)/shard_map/all_to_all | solution.py:290
  73.4 0.0 copy-done.2
  73.4 0.0 copy-done.3
  73.4 0.0 copy-done.1
  73.4 4.2 %shard_map.97 = bf16[256,3072]{1,0:T(8,128)(2,1)S(1)} custom-call(bf16[256,3072]{1,0:T(8,128)(2,1)S(1)} %bitcast.16, bf16[1,2048,768]{2,1,0:T(8,128)(2,1)S(1)} %copy-done.1, bf16[1,2048,768]{2,1,0:T(8,128)(2,1)S(1)} %copy-done.2, bf16[1,768,2048]{2,1,0:T(8,128)(2,1)S(1)} %copy-done.3), custom_call_target="tpu_custom_call" | custom-call | flops 3700000000 | bytes 3145728 | tf_op jit(solution)/shard_map/pallas_call | solution.py:331
  77.5 0.0 copy-start
  77.6 45.2 %all_to_all.21 = bf16[32,8,3072]{2,1,0:T(8,128)(2,1)S(1)} all-to-all(bf16[32,8,3072]{2,1,0:T(8,128)(2,1)S(1)} %bitcast.17), channel_id=1, replica_groups=mesh['yl'=2,'z'=12,'chip'=16,'core'=2] {'chip','core'}, dimensions={0} | all-to-all | bytes 3145728 | tf_op jit(solution)/shard_map/all_to_all | solution.py:290
  122.7 0.0 copy-done
  122.7 1.3 shard_map.99
  124.0 1.9 %collective-permute-start.2 = (bf16[256,512]{1,0:T(8,128)(2,1)S(1)}, bf16[256,512]{1,0:T(8,128)(2,1)S(1)}, u32[]{:S(2)}, u32[]{:S(2)}) collective-permute-start(bf16[256,512]{1,0:T(8,128)(2,1)S(1)} %get-tuple-element.33), channel_id=1, source_target_pairs={{0,1},{1,0},{2,3},{3,2},{4,5},{5,4},{6,7},{7,6},{8,9},{9,8},{10,11... | collective-permute-start | bytes 786440 | tf_op jit(solution)/shard_map/ppermute | solution.py:384
  125.9 1.5 collective-permute-done.2.given_ref
  127.4 0.3 shard_map.100
  127.7 16.8 %all_to_all.22 = bf16[32,8,512]{2,1,0:T(8,128)(2,1)S(1)} all-to-all(bf16[32,8,512]{2,1,0:T(8,128)(2,1)S(1)} %bitcast.18), channel_id=1, replica_groups=mesh['yl'=2,'z'=12,'chip'=16,'core'=2] {'yl','chip'}, dimensions={0} | all-to-all | bytes 524288 | tf_op jit(solution)/shard_map/all_to_all | solution.py:290
  144.6 0.7 shard_map.101
  145.3 9.3 %all-to-all-start.3 = ((bf16[24,8,512]{2,1,0:T(8,128)(2,1)}), bf16[24,8,512]{2,1,0:T(8,128)(2,1)S(1)}, u32[]{:S(2)}, u32[]{:S(2)}) async-start(bf16[24,8,512]{2,1,0:T(8,128)(2,1)} %bitcast.11), calls=%async_computation.3 | async-start | bytes 393216 | tf_op jit(solution)/shard_map/all_to_all | solution.py:290
  154.6 1.5 shard_map.98
  156.2 10.0 %all-to-all-done.3 = bf16[24,8,512]{2,1,0:T(8,128)(2,1)S(1)} async-done(((bf16[24,8,512]{2,1,0:T(8,128)(2,1)}), bf16[24,8,512]{2,1,0:T(8,128)(2,1)S(1)}, u32[]{:S(2)}, u32[]{:S(2)}) %all-to-all-start.3) | async-done | bytes 196640 | tf_op jit(solution)/shard_map/all_to_all | solution.py:290
  166.1 0.6 shard_map.102
Async XLA Ops:
  2.2 18.0 %collective-permute-start = (bf16[32,2048]{1,0:T(8,128)(2,1)S(1)}, bf16[32,2048]{1,0:T(8,128)(2,1)S(1)}, u32[]{:S(2)}, u32[]{:S(2)}) collective-permute-start(bf16[32,2048]{1,0:T(8,128)(2,1)S(1)} %get-tuple-element.18), channel_id=1, source_target_pairs={{0,32},{32,64},{64,96},{96,128},{128,160},{160,192},{192,224},{224... | collective-permute-start | bytes 393224 | tf_op jit(solution)/shard_map/ppermute | solution.py:377
  6.5 14.9 %collective-permute-start.1 = (bf16[32,2048]{1,0:T(8,128)(2,1)S(1)}, bf16[32,2048]{1,0:T(8,128)(2,1)S(1)}, u32[]{:S(2)}, u32[]{:S(2)}) collective-permute-start(bf16[32,2048]{1,0:T(8,128)(2,1)S(1)} %get-tuple-element.19), channel_id=1, source_target_pairs={{32,0},{64,32},{96,64},{128,96},{160,128},{192,160},{224,192},{256... | collective-permute-start | bytes 393224 | tf_op jit(solution)/shard_map/ppermute | solution.py:378
  21.4 52.0 %copy-start.2 = (bf16[1,2048,768]{2,1,0:T(8,128)(2,1)S(1)}, bf16[1,2048,768]{2,1,0:T(8,128)(2,1)}, u32[]{:S(2)}) copy-start(bf16[1,2048,768]{2,1,0:T(8,128)(2,1)} %up_ref.1) | copy-start | bytes 9437188
  21.4 52.0 %copy-start.3 = (bf16[1,768,2048]{2,1,0:T(8,128)(2,1)S(1)}, bf16[1,768,2048]{2,1,0:T(8,128)(2,1)}, u32[]{:S(2)}) copy-start(bf16[1,768,2048]{2,1,0:T(8,128)(2,1)} %down_ref.1) | copy-start | bytes 9437188
  22.2 51.2 %copy-start.1 = (bf16[1,2048,768]{2,1,0:T(8,128)(2,1)S(1)}, bf16[1,2048,768]{2,1,0:T(8,128)(2,1)}, u32[]{:S(2)}) copy-start(bf16[1,2048,768]{2,1,0:T(8,128)(2,1)} %gate_ref.1) | copy-start | bytes 9437188
  77.5 45.2 %copy-start = (bf16[128,2048]{1,0:T(8,128)(2,1)S(1)}, bf16[128,2048]{1,0:T(8,128)(2,1)}, u32[]{:S(2)}) copy-start(bf16[128,2048]{1,0:T(8,128)(2,1)} %grad_ref.1) | copy-start | bytes 1572868
  124.0 3.4 %collective-permute-start.2 = (bf16[256,512]{1,0:T(8,128)(2,1)S(1)}, bf16[256,512]{1,0:T(8,128)(2,1)S(1)}, u32[]{:S(2)}, u32[]{:S(2)}) collective-permute-start(bf16[256,512]{1,0:T(8,128)(2,1)S(1)} %get-tuple-element.33), channel_id=1, source_target_pairs={{0,1},{1,0},{2,3},{3,2},{4,5},{5,4},{6,7},{7,6},{8,9},{9,8},{10,11... | collective-permute-start | bytes 786440 | tf_op jit(solution)/shard_map/ppermute | solution.py:384
  145.3 20.8 %all-to-all-start.3 = ((bf16[24,8,512]{2,1,0:T(8,128)(2,1)}), bf16[24,8,512]{2,1,0:T(8,128)(2,1)S(1)}, u32[]{:S(2)}, u32[]{:S(2)}) async-start(bf16[24,8,512]{2,1,0:T(8,128)(2,1)} %bitcast.11), calls=%async_computation.3 | async-start | bytes 393216 | tf_op jit(solution)/shard_map/all_to_all | solution.py:290

commit v8 on v7

--- a/solution.py
+++ b/solution.py
@@ -253,7 +253,17 @@
         out_ref[rows, :] = (own + given_ref[rows, :].astype(f32)).astype(bf16)
 
 
-def output_kernel(rows_ref, high_ref, low_ref, late_high_ref, late_low_ref, out_ref):
+def output_kernel(
+    rows_ref,
+    high_ref,
+    low_ref,
+    late_high_ref,
+    late_low_ref,
+    factor_ref,
+    out_ref,
+    handed_ref,
+):
+    handed_ref[...] = factor_ref[...]
     rows, ends = rows_ref[:, :D], rows_ref[:, D:]
     late = mm(late_high_ref[...], ends) + mm(late_low_ref[...], ends)
     both = mm(high_ref[...], rows) + mm(low_ref[...], rows)
@@ -352,10 +362,13 @@
     )
 
 
-def layer_output(rows, high, low, late_high, late_low):
-    return call(output_kernel, shape((TOK_DEV, D), bf16), [VMEM] * 5, 4_000_000_000)(
-        rows, high, low, late_high, late_low
-    )
+def layer_output(rows, shares, factor):
+    return call(
+        output_kernel,
+        [shape((TOK_DEV, D), bf16), shape((EXPERTS, 2 * TOK_DEV), bf16)],
+        [VMEM] * 6,
+        4_000_000_000,
+    )(rows, *shares, factor)
 
 
 def partial_sum(terms):
@@ -382,8 +395,8 @@
     returned = exchange(computed, FSDP, WIN)
     other, factor = router_terms(returned, grad_out, balanced, order, place, late, weight)
     given = lax.ppermute(other, "core", [(0, 1), (1, 0)])
+    layer_out, factor = layer_output(returned, shares, factor)
     terms = exchange(join(factor, balanced, given), ("yl", "chip"), 2 * CHIPS)
-    layer_out = layer_output(returned, *shares)
     parts = exchange(partial_sum(terms), DP, 24)
     return (layer_out, last_sum(parts))
 

time: 167 us -> 167 us (level)
  blocking collectives: 113 us -> 135 us
  waiting for transfers between devices: 14.2 us -> 2.74 us
  starting transfers between devices: 27.6 us -> 18.3 us
    all_to_all x3 -> x4, blocking collectives: 113 us -> 135 us  [exchange(): lax.all_to_all(apart, axes, split_axis=0, concat_axis=0, tiled=True)]
    all_to_all x1 -> x0, waiting for transfers between devices: 9.99 us -> none  [exchange(): lax.all_to_all(apart, axes, split_axis=0, concat_axis=0, tiled=True)]
    all_to_all x1 -> x0, starting transfers between devices: 9.32 us -> none  [exchange(): lax.all_to_all(apart, axes, split_axis=0, concat_axis=0, tiled=True)]
  transfers between devices with their start and end apart: 4 -> 3, of which waited for: 4 -> 2; matrix products, arithmetic and copies ran while one was open for 0% -> 0% of each run, Pallas kernels for 1% -> 1%
where the time goes in v8:
time: 167 us
  blocking collectives  135 us (81%)
  starting transfers between devices  18.3 us (11%)
  Pallas kernels  10.3 us (6%)
  waiting for transfers between devices  2.74 us (2%)
    all_to_all x4, blocking collectives, exchange(): lax.all_to_all(apart, axes, split_axis=0, concat_axis=0, tiled=True)  135 us
    ppermute x1, starting transfers between devices, shards(): right = lax.ppermute(head, DP, [((i + 1) % ranks, i) for i in range(ranks)])  12.1 us
    ppermute x1, starting transfers between devices, shards(): left = lax.ppermute(tail, DP, [(i, (i + 1) % ranks) for i in range(ranks)])  4.29 us
    pallas_call x1, Pallas kernels, ffn(): call(ffn_kernel, shape((ROWS, WIDTH), bf16), [VMEM] * 4, 3700000000, [plt...  4.16 us
  transfers between devices with their start and end apart: 3, of which 2 were waited for; matrix products, arithmetic and copies ran while one was open for 0% of the time, Pallas kernels for 1%

profile of v8, /device:TPU:8, one launch (start us, length us, event | category | flops | bytes accessed | tf_op | source)
XLA Modules:
  0.0 166.7 jit_solution(747275565422371466)
XLA Ops:
  0.6 1.6 shard_map.95
  2.2 4.3 %collective-permute-start = (bf16[32,2048]{1,0:T(8,128)(2,1)S(1)}, bf16[32,2048]{1,0:T(8,128)(2,1)S(1)}, u32[]{:S(2)}, u32[]{:S(2)}) collective-permute-start(bf16[32,2048]{1,0:T(8,128)(2,1)S(1)} %get-tuple-element.20), channel_id=1, source_target_pairs={{0,32},{32,64},{64,96},{96,128},{128,160},{160,192},{192,224},{224... | collective-permute-start | bytes 393224 | tf_op jit(solution)/shard_map/ppermute | solution.py:390
  6.5 12.1 %collective-permute-start.1 = (bf16[32,2048]{1,0:T(8,128)(2,1)S(1)}, bf16[32,2048]{1,0:T(8,128)(2,1)S(1)}, u32[]{:S(2)}, u32[]{:S(2)}) collective-permute-start(bf16[32,2048]{1,0:T(8,128)(2,1)S(1)} %get-tuple-element.21), channel_id=1, source_target_pairs={{32,0},{64,32},{96,64},{128,96},{160,128},{192,160},{224,192},{256... | collective-permute-start | bytes 393224 | tf_op jit(solution)/shard_map/ppermute | solution.py:391
  18.7 1.6 collective-permute-done.left_ref
  20.2 1.2 collective-permute-done.1.right_ref
  21.4 0.0 copy-start.2
  21.4 0.0 copy-start.3
  21.4 0.7 shard_map.96
  22.2 0.0 copy-start.1
  22.2 51.2 %all_to_all.20 = bf16[32,8,3072]{2,1,0:T(8,128)(2,1)S(1)} all-to-all(bf16[32,8,3072]{2,1,0:T(8,128)(2,1)S(1)} %bitcast.15), channel_id=1, replica_groups=mesh['yl'=2,'z'=12,'chip'=16,'core'=2] {'chip','core'}, dimensions={0} | all-to-all | bytes 3145728 | tf_op jit(solution)/shard_map/all_to_all | solution.py:300
  73.4 0.0 copy-done.2
  73.4 0.0 copy-done.3
  73.4 0.0 copy-done.1
  73.4 4.2 %shard_map.97 = bf16[256,3072]{1,0:T(8,128)(2,1)S(1)} custom-call(bf16[256,3072]{1,0:T(8,128)(2,1)S(1)} %bitcast.16, bf16[1,2048,768]{2,1,0:T(8,128)(2,1)S(1)} %copy-done.1, bf16[1,2048,768]{2,1,0:T(8,128)(2,1)S(1)} %copy-done.2, bf16[1,768,2048]{2,1,0:T(8,128)(2,1)S(1)} %copy-done.3), custom_call_target="tpu_custom_call" | custom-call | flops 3700000000 | bytes 3145728 | tf_op jit(solution)/shard_map/pallas_call | solution.py:341
  77.5 0.0 copy-start
  77.6 45.2 %all_to_all.21 = bf16[32,8,3072]{2,1,0:T(8,128)(2,1)S(1)} all-to-all(bf16[32,8,3072]{2,1,0:T(8,128)(2,1)S(1)} %bitcast.17), channel_id=1, replica_groups=mesh['yl'=2,'z'=12,'chip'=16,'core'=2] {'chip','core'}, dimensions={0} | all-to-all | bytes 3145728 | tf_op jit(solution)/shard_map/all_to_all | solution.py:300
  122.7 0.0 copy-done
  122.7 1.3 shard_map.98
  124.0 1.9 %collective-permute-start.2 = (bf16[256,512]{1,0:T(8,128)(2,1)S(1)}, bf16[256,512]{1,0:T(8,128)(2,1)S(1)}, u32[]{:S(2)}, u32[]{:S(2)}) collective-permute-start(bf16[256,512]{1,0:T(8,128)(2,1)S(1)} %get-tuple-element.37), channel_id=1, source_target_pairs={{0,1},{1,0},{2,3},{3,2},{4,5},{5,4},{6,7},{7,6},{8,9},{9,8},{10,11... | collective-permute-start | bytes 786440 | tf_op jit(solution)/shard_map/ppermute | solution.py:397
  125.9 1.5 shard_map.99
  127.4 0.0 collective-permute-done.2.given_ref
  127.4 0.3 shard_map.100
  127.8 17.1 %all_to_all.22 = bf16[32,8,512]{2,1,0:T(8,128)(2,1)S(1)} all-to-all(bf16[32,8,512]{2,1,0:T(8,128)(2,1)S(1)} %bitcast.18), channel_id=1, replica_groups=mesh['yl'=2,'z'=12,'chip'=16,'core'=2] {'yl','chip'}, dimensions={0} | all-to-all | bytes 524288 | tf_op jit(solution)/shard_map/all_to_all | solution.py:300
  144.9 21.1 %all_to_all.23 = bf16[24,8,512]{2,1,0:T(8,128)(2,1)S(1)} all-to-all(bf16[24,8,512]{2,1,0:T(8,128)(2,1)S(1)} %bitcast.20), channel_id=1, replica_groups=mesh['yl'=2,'z'=12,'chip'=16,'core'=2] {'yl','z'}, dimensions={0} | all-to-all | bytes 393216 | tf_op jit(solution)/shard_map/all_to_all | solution.py:300
  166.1 0.6 shard_map.102
  (1 shorter events, 0.0 us)
Async XLA Ops:
  2.2 18.0 %collective-permute-start = (bf16[32,2048]{1,0:T(8,128)(2,1)S(1)}, bf16[32,2048]{1,0:T(8,128)(2,1)S(1)}, u32[]{:S(2)}, u32[]{:S(2)}) collective-permute-start(bf16[32,2048]{1,0:T(8,128)(2,1)S(1)} %get-tuple-element.20), channel_id=1, source_target_pairs={{0,32},{32,64},{64,96},{96,128},{128,160},{160,192},{192,224},{224... | collective-permute-start | bytes 393224 | tf_op jit(solution)/shard_map/ppermute | solution.py:390
  6.5 14.9 %collective-permute-start.1 = (bf16[32,2048]{1,0:T(8,128)(2,1)S(1)}, bf16[32,2048]{1,0:T(8,128)(2,1)S(1)}, u32[]{:S(2)}, u32[]{:S(2)}) collective-permute-start(bf16[32,2048]{1,0:T(8,128)(2,1)S(1)} %get-tuple-element.21), channel_id=1, source_target_pairs={{32,0},{64,32},{96,64},{128,96},{160,128},{192,160},{224,192},{256... | collective-permute-start | bytes 393224 | tf_op jit(solution)/shard_map/ppermute | solution.py:391
  21.4 52.0 %copy-start.2 = (bf16[1,2048,768]{2,1,0:T(8,128)(2,1)S(1)}, bf16[1,2048,768]{2,1,0:T(8,128)(2,1)}, u32[]{:S(2)}) copy-start(bf16[1,2048,768]{2,1,0:T(8,128)(2,1)} %up_ref.1) | copy-start | bytes 9437188
  21.4 52.0 %copy-start.3 = (bf16[1,768,2048]{2,1,0:T(8,128)(2,1)S(1)}, bf16[1,768,2048]{2,1,0:T(8,128)(2,1)}, u32[]{:S(2)}) copy-start(bf16[1,768,2048]{2,1,0:T(8,128)(2,1)} %down_ref.1) | copy-start | bytes 9437188
  22.2 51.2 %copy-start.1 = (bf16[1,2048,768]{2,1,0:T(8,128)(2,1)S(1)}, bf16[1,2048,768]{2,1,0:T(8,128)(2,1)}, u32[]{:S(2)}) copy-start(bf16[1,2048,768]{2,1,0:T(8,128)(2,1)} %gate_ref.1) | copy-start | bytes 9437188
  77.5 45.2 %copy-start = (bf16[128,2048]{1,0:T(8,128)(2,1)S(1)}, bf16[128,2048]{1,0:T(8,128)(2,1)}, u32[]{:S(2)}) copy-start(bf16[128,2048]{1,0:T(8,128)(2,1)} %grad_ref.1) | copy-start | bytes 1572868
  124.0 3.4 %collective-permute-start.2 = (bf16[256,512]{1,0:T(8,128)(2,1)S(1)}, bf16[256,512]{1,0:T(8,128)(2,1)S(1)}, u32[]{:S(2)}, u32[]{:S(2)}) collective-permute-start(bf16[256,512]{1,0:T(8,128)(2,1)S(1)} %get-tuple-element.37), channel_id=1, source_target_pairs={{0,1},{1,0},{2,3},{3,2},{4,5},{5,4},{6,7},{7,6},{8,9},{9,8},{10,11... | collective-permute-start | bytes 786440 | tf_op jit(solution)/shard_map/ppermute | solution.py:397

commit v9 on v8

--- a/solution.py
+++ b/solution.py
@@ -294,10 +294,24 @@
     return jax.ShapeDtypeStruct(dims, dtype)
 
 
-def exchange(blocks, axes, peers):
+def exchange(blocks, axes, peers, groups=None):
     rows, cols = blocks.shape
     apart = blocks.reshape(peers, rows // peers, cols)
-    return lax.all_to_all(apart, axes, split_axis=0, concat_axis=0, tiled=True).reshape(rows, cols)
+    return lax.all_to_all(
+        apart, axes, split_axis=0, concat_axis=0, axis_index_groups=groups, tiled=True
+    ).reshape(rows, cols)
+
+
+def expert_groups():
+    return [
+        [
+            (((side ^ (chip >= CHIPS // 2)) * 12 + z) * CHIPS + chip) * 2 + core
+            for chip in range(CHIPS)
+            for core in range(2)
+        ]
+        for z in range(12)
+        for side in range(2)
+    ]
 
 
 def borders(rank, core, flows, rollout, ids, logits):
@@ -390,9 +404,9 @@
     left = lax.ppermute(tail, DP, [(i, (i + 1) % ranks) for i in range(ranks)])
     right = lax.ppermute(head, DP, [((i + 1) % ranks, i) for i in range(ranks)])
     outgoing, balanced = dispatch(left, right, held, settle, place, late)
-    rows = exchange(outgoing, FSDP, WIN)
+    rows = exchange(outgoing, DP + FSDP, WIN, expert_groups())
     computed = ffn(rows, w_gate, w_up, w_down)
-    returned = exchange(computed, FSDP, WIN)
+    returned = exchange(computed, DP + FSDP, WIN, expert_groups())
     other, factor = router_terms(returned, grad_out, balanced, order, place, late, weight)
     given = lax.ppermute(other, "core", [(0, 1), (1, 0)])
     layer_out, factor = layer_output(returned, shares, factor)

time: 167 us -> 165 us (0.988)
  blocking collectives: 135 us -> 131 us
    all_to_all x4, blocking collectives: 135 us -> 131 us  [exchange(): lax.all_to_all(apart, axes, split_axis=0, concat_axis=0, axis_index_group...]
where the time goes in v9:
time: 165 us; the launch traced here: 164 us
  blocking collectives  131 us (79%)
  starting transfers between devices  19.4 us (12%)
  Pallas kernels  10.3 us (6%)
  waiting for transfers between devices  2.74 us (2%)
    all_to_all x4, blocking collectives, exchange(): lax.all_to_all(apart, axes, split_axis=0, concat_axis=0, axis_index_group...  131 us
    ppermute x1, starting transfers between devices, shards(): right = lax.ppermute(head, DP, [((i + 1) % ranks, i) for i in range(ranks)])  12.1 us
    ppermute x1, starting transfers between devices, shards(): left = lax.ppermute(tail, DP, [(i, (i + 1) % ranks) for i in range(ranks)])  4.29 us
    pallas_call x1, Pallas kernels, ffn(): call(ffn_kernel, shape((ROWS, WIDTH), bf16), [VMEM] * 4, 3700000000, [plt...  4.16 us
  transfers between devices with their start and end apart: 3, of which 2 were waited for; matrix products, arithmetic and copies ran while one was open for 0% of the time, Pallas kernels for 1%

profile of v9, /device:TPU:8, one launch (start us, length us, event | category | flops | bytes accessed | tf_op | source)
XLA Modules:
  0.0 164.3 jit_solution(14327392210007517349)
XLA Ops:
  0.6 1.6 shard_map.95
  2.2 4.3 %collective-permute-start = (bf16[32,2048]{1,0:T(8,128)(2,1)S(1)}, bf16[32,2048]{1,0:T(8,128)(2,1)S(1)}, u32[]{:S(2)}, u32[]{:S(2)}) collective-permute-start(bf16[32,2048]{1,0:T(8,128)(2,1)S(1)} %get-tuple-element.20), channel_id=1, source_target_pairs={{0,32},{32,64},{64,96},{96,128},{128,160},{160,192},{192,224},{224... | collective-permute-start | bytes 393224 | tf_op jit(solution)/shard_map/ppermute | solution.py:404
  6.5 12.1 %collective-permute-start.1 = (bf16[32,2048]{1,0:T(8,128)(2,1)S(1)}, bf16[32,2048]{1,0:T(8,128)(2,1)S(1)}, u32[]{:S(2)}, u32[]{:S(2)}) collective-permute-start(bf16[32,2048]{1,0:T(8,128)(2,1)S(1)} %get-tuple-element.21), channel_id=1, source_target_pairs={{32,0},{64,32},{96,64},{128,96},{160,128},{192,160},{224,192},{256... | collective-permute-start | bytes 393224 | tf_op jit(solution)/shard_map/ppermute | solution.py:405
  18.7 1.6 collective-permute-done.left_ref
  20.2 1.2 collective-permute-done.1.right_ref
  21.4 0.0 copy-start.2
  21.4 0.0 copy-start.3
  21.4 0.7 shard_map.96
  22.2 0.0 copy-start.1
  22.2 48.5 %all_to_all.20 = bf16[32,8,3072]{2,1,0:T(8,128)(2,1)S(1)} all-to-all(bf16[32,8,3072]{2,1,0:T(8,128)(2,1)S(1)} %bitcast.15), channel_id=1, replica_groups={{0,1,2,3,4,5,6,7,8,9,10,11,12,13,14,15,400,401,402,403,404,405,406,407,..., dimensions={0} | all-to-all | bytes 3145728 | tf_op jit(solution)/shard_map/all_to_all | solution.py:300
  70.7 0.0 copy-done.2
  70.7 0.0 copy-done.3
  70.7 0.0 copy-done.1
  70.7 4.2 %shard_map.97 = bf16[256,3072]{1,0:T(8,128)(2,1)S(1)} custom-call(bf16[256,3072]{1,0:T(8,128)(2,1)S(1)} %bitcast.16, bf16[1,2048,768]{2,1,0:T(8,128)(2,1)S(1)} %copy-done.1, bf16[1,2048,768]{2,1,0:T(8,128)(2,1)S(1)} %copy-done.2, bf16[1,768,2048]{2,1,0:T(8,128)(2,1)S(1)} %copy-done.3), custom_call_target="tpu_custom_call" | custom-call | flops 3700000000 | bytes 3145728 | tf_op jit(solution)/shard_map/pallas_call | solution.py:355
  74.8 0.0 copy-start
  74.9 44.6 %all_to_all.21 = bf16[32,8,3072]{2,1,0:T(8,128)(2,1)S(1)} all-to-all(bf16[32,8,3072]{2,1,0:T(8,128)(2,1)S(1)} %bitcast.17), channel_id=1, replica_groups={{0,1,2,3,4,5,6,7,8,9,10,11,12,13,14,15,400,401,402,403,404,405,406,407,..., dimensions={0} | all-to-all | bytes 3145728 | tf_op jit(solution)/shard_map/all_to_all | solution.py:300
  119.4 0.0 copy-done
  119.4 1.3 shard_map.98
  120.7 3.0 %collective-permute-start.2 = (bf16[256,512]{1,0:T(8,128)(2,1)S(1)}, bf16[256,512]{1,0:T(8,128)(2,1)S(1)}, u32[]{:S(2)}, u32[]{:S(2)}) collective-permute-start(bf16[256,512]{1,0:T(8,128)(2,1)S(1)} %get-tuple-element.37), channel_id=1, source_target_pairs={{0,1},{1,0},{2,3},{3,2},{4,5},{5,4},{6,7},{7,6},{8,9},{9,8},{10,11... | collective-permute-start | bytes 786440 | tf_op jit(solution)/shard_map/ppermute | solution.py:411
  123.7 1.5 shard_map.99
  125.2 0.0 collective-permute-done.2.given_ref
  125.2 0.3 shard_map.100
  125.6 18.3 %all_to_all.22 = bf16[32,8,512]{2,1,0:T(8,128)(2,1)S(1)} all-to-all(bf16[32,8,512]{2,1,0:T(8,128)(2,1)S(1)} %bitcast.18), channel_id=1, replica_groups=mesh['yl'=2,'z'=12,'chip'=16,'core'=2] {'yl','chip'}, dimensions={0} | all-to-all | bytes 524288 | tf_op jit(solution)/shard_map/all_to_all | solution.py:300
  143.9 19.7 %all_to_all.23 = bf16[24,8,512]{2,1,0:T(8,128)(2,1)S(1)} all-to-all(bf16[24,8,512]{2,1,0:T(8,128)(2,1)S(1)} %bitcast.20), channel_id=1, replica_groups=mesh['yl'=2,'z'=12,'chip'=16,'core'=2] {'yl','z'}, dimensions={0} | all-to-all | bytes 393216 | tf_op jit(solution)/shard_map/all_to_all | solution.py:300
  163.7 0.6 shard_map.102
  (1 shorter events, 0.0 us)
Async XLA Ops:
  2.2 18.0 %collective-permute-start = (bf16[32,2048]{1,0:T(8,128)(2,1)S(1)}, bf16[32,2048]{1,0:T(8,128)(2,1)S(1)}, u32[]{:S(2)}, u32[]{:S(2)}) collective-permute-start(bf16[32,2048]{1,0:T(8,128)(2,1)S(1)} %get-tuple-element.20), channel_id=1, source_target_pairs={{0,32},{32,64},{64,96},{96,128},{128,160},{160,192},{192,224},{224... | collective-permute-start | bytes 393224 | tf_op jit(solution)/shard_map/ppermute | solution.py:404
  6.5 14.9 %collective-permute-start.1 = (bf16[32,2048]{1,0:T(8,128)(2,1)S(1)}, bf16[32,2048]{1,0:T(8,128)(2,1)S(1)}, u32[]{:S(2)}, u32[]{:S(2)}) collective-permute-start(bf16[32,2048]{1,0:T(8,128)(2,1)S(1)} %get-tuple-element.21), channel_id=1, source_target_pairs={{32,0},{64,32},{96,64},{128,96},{160,128},{192,160},{224,192},{256... | collective-permute-start | bytes 393224 | tf_op jit(solution)/shard_map/ppermute | solution.py:405
  21.4 49.3 %copy-start.2 = (bf16[1,2048,768]{2,1,0:T(8,128)(2,1)S(1)}, bf16[1,2048,768]{2,1,0:T(8,128)(2,1)}, u32[]{:S(2)}) copy-start(bf16[1,2048,768]{2,1,0:T(8,128)(2,1)} %up_ref.1) | copy-start | bytes 9437188
  21.4 49.3 %copy-start.3 = (bf16[1,768,2048]{2,1,0:T(8,128)(2,1)S(1)}, bf16[1,768,2048]{2,1,0:T(8,128)(2,1)}, u32[]{:S(2)}) copy-start(bf16[1,768,2048]{2,1,0:T(8,128)(2,1)} %down_ref.1) | copy-start | bytes 9437188
  22.2 48.5 %copy-start.1 = (bf16[1,2048,768]{2,1,0:T(8,128)(2,1)S(1)}, bf16[1,2048,768]{2,1,0:T(8,128)(2,1)}, u32[]{:S(2)}) copy-start(bf16[1,2048,768]{2,1,0:T(8,128)(2,1)} %gate_ref.1) | copy-start | bytes 9437188
  74.8 44.6 %copy-start = (bf16[128,2048]{1,0:T(8,128)(2,1)S(1)}, bf16[128,2048]{1,0:T(8,128)(2,1)}, u32[]{:S(2)}) copy-start(bf16[128,2048]{1,0:T(8,128)(2,1)} %grad_ref.1) | copy-start | bytes 1572868
  120.7 4.6 %collective-permute-start.2 = (bf16[256,512]{1,0:T(8,128)(2,1)S(1)}, bf16[256,512]{1,0:T(8,128)(2,1)S(1)}, u32[]{:S(2)}, u32[]{:S(2)}) collective-permute-start(bf16[256,512]{1,0:T(8,128)(2,1)S(1)} %get-tuple-element.37), channel_id=1, source_target_pairs={{0,1},{1,0},{2,3},{3,2},{4,5},{5,4},{6,7},{7,6},{8,9},{9,8},{10,11... | collective-permute-start | bytes 786440 | tf_op jit(solution)/shard_map/ppermute | solution.py:411

commit v10 on v9

--- a/solution.py
+++ b/solution.py
@@ -69,7 +69,6 @@
     rollout_hbm,
     ids_hbm,
     logits_hbm,
-    head_ref,
     tail_ref,
     held_ref,
     settle_ref,
@@ -119,7 +118,6 @@
     at = iota((MOVE, SRC_DEV), 0) + (live - MOVE)
     pick = (iota((MOVE, SRC_DEV), 1) == at).astype(bf16)
     held_copy.wait()
-    head_ref[...] = held_ref[:MOVE, :]
     tail_ref[...] = mm(pick, held_ref[...]).astype(bf16)
 
 
@@ -319,7 +317,6 @@
         border_kernel,
         [
             shape((MOVE, D), bf16),
-            shape((MOVE, D), bf16),
             shape((SRC_DEV, D), bf16),
             shape((TOK_DEV, SPAN), bf16),
             shape((2 * EXPERTS, EXPERTS), bf16),
@@ -398,11 +395,11 @@
     rank = lax.axis_index(DP).reshape(1)
     core = lax.axis_index("core").reshape(1)
     flows = flows.T
-    head, tail, held, settle, order, place, late, weight, *shares = borders(
+    right = lax.ppermute(rollout[:MOVE], DP, [((i + 1) % ranks, i) for i in range(ranks)])
+    tail, held, settle, order, place, late, weight, *shares = borders(
         rank, core, flows, rollout, route_ids.T, route_logits.T
     )
     left = lax.ppermute(tail, DP, [(i, (i + 1) % ranks) for i in range(ranks)])
-    right = lax.ppermute(head, DP, [((i + 1) % ranks, i) for i in range(ranks)])
     outgoing, balanced = dispatch(left, right, held, settle, place, late)
     rows = exchange(outgoing, DP + FSDP, WIN, expert_groups())
     computed = ffn(rows, w_gate, w_up, w_down)

time: 165 us -> 166 us (level)
  the two profiles are of different devices: /device:TPU:8 before, /device:TPU:16 now
where the time goes in v10:
time: 166 us
  blocking collectives  126 us (76%)
  starting transfers between devices  20.8 us (13%)
  Pallas kernels  10.3 us (6%)
  waiting for transfers between devices  7.04 us (4%)
    all_to_all x4, blocking collectives, exchange(): lax.all_to_all(apart, axes, split_axis=0, concat_axis=0, axis_index_group...  126 us
    ppermute x1, starting transfers between devices, shards(): lax.ppermute(rollout[:MOVE], DP, [((i + 1) % ranks, i) for i in range(ran...  15.6 us
    ppermute x1, waiting for transfers between devices, shards(): left = lax.ppermute(tail, DP, [(i, (i + 1) % ranks) for i in range(ranks)])  7.03 us
    pallas_call x1, Pallas kernels, ffn(): call(ffn_kernel, shape((ROWS, WIDTH), bf16), [VMEM] * 4, 3700000000, [plt...  4.17 us
    ppermute x1, starting transfers between devices, shards(): given = lax.ppermute(other, 'core', [(0, 1), (1, 0)])  3.33 us
  transfers between devices with their start and end apart: 3, of which 1 were waited for; matrix products, arithmetic and copies ran while one was open for 0% of the time, Pallas kernels for 2%

profile of v10, /device:TPU:16, one launch (start us, length us, event | category | flops | bytes accessed | tf_op | source)
XLA Modules:
  0.0 165.6 jit_solution(5674509942582431118)
XLA Ops:
  0.6 0.9 slice.3
  1.5 15.6 %collective-permute-start.1 = (bf16[32,2048]{1,0:T(8,128)(2,1)S(1)}, bf16[32,2048]{1,0:T(8,128)(2,1)S(1)}, u32[]{:S(2)}, u32[]{:S(2)}) collective-permute-start(bf16[32,2048]{1,0:T(8,128)(2,1)S(1)} %slice.3), channel_id=1, source_target_pairs={{32,0},{64,32},{96,64},{128,96},{160,128},{192,160},{224,192},{256... | collective-permute-start | bytes 393224 | tf_op jit(solution)/shard_map/ppermute | solution.py:398
  17.2 1.6 shard_map.95
  18.8 1.9 %collective-permute-start = (bf16[32,2048]{1,0:T(8,128)(2,1)S(1)}, bf16[32,2048]{1,0:T(8,128)(2,1)S(1)}, u32[]{:S(2)}, u32[]{:S(2)}) collective-permute-start(bf16[32,2048]{1,0:T(8,128)(2,1)S(1)} %get-tuple-element.19), channel_id=1, source_target_pairs={{0,32},{32,64},{64,96},{96,128},{128,160},{160,192},{192,224},{224... | collective-permute-start | bytes 393224 | tf_op jit(solution)/shard_map/ppermute | solution.py:402
  20.7 0.0 collective-permute-done.1.right_ref
  20.7 7.0 %collective-permute-done.left_ref = bf16[32,2048]{1,0:T(8,128)(2,1)S(1)} collective-permute-done((bf16[32,2048]{1,0:T(8,128)(2,1)S(1)}, bf16[32,2048]{1,0:T(8,128)(2,1)S(1)}, u32[]{:S(2)}, u32[]{:S(2)}) %collective-permute-start) | collective-permute-done | bytes 131104 | tf_op jit(solution)/shard_map/ppermute | solution.py:402
  27.7 0.0 copy-start.2
  27.7 0.0 copy-start.3
  27.8 0.7 shard_map.96
  28.5 0.0 copy-start.1
  28.5 46.1 %all_to_all.20 = bf16[32,8,3072]{2,1,0:T(8,128)(2,1)S(1)} all-to-all(bf16[32,8,3072]{2,1,0:T(8,128)(2,1)S(1)} %bitcast.15), channel_id=1, replica_groups={{0,1,2,3,4,5,6,7,8,9,10,11,12,13,14,15,400,401,402,403,404,405,406,407,..., dimensions={0} | all-to-all | bytes 3145728 | tf_op jit(solution)/shard_map/all_to_all | solution.py:298
  74.6 0.0 copy-done.2
  74.6 0.0 copy-done.3
  74.6 0.0 copy-done.1
  74.6 4.2 %shard_map.97 = bf16[256,3072]{1,0:T(8,128)(2,1)S(1)} custom-call(bf16[256,3072]{1,0:T(8,128)(2,1)S(1)} %bitcast.16, bf16[1,2048,768]{2,1,0:T(8,128)(2,1)S(1)} %copy-done.1, bf16[1,2048,768]{2,1,0:T(8,128)(2,1)S(1)} %copy-done.2, bf16[1,768,2048]{2,1,0:T(8,128)(2,1)S(1)} %copy-done.3), custom_call_target="tpu_custom_call" | custom-call | flops 3700000000 | bytes 3145728 | tf_op jit(solution)/shard_map/pallas_call | solution.py:352
  78.8 0.0 copy-start
  78.8 44.3 %all_to_all.21 = bf16[32,8,3072]{2,1,0:T(8,128)(2,1)S(1)} all-to-all(bf16[32,8,3072]{2,1,0:T(8,128)(2,1)S(1)} %bitcast.17), channel_id=1, replica_groups={{0,1,2,3,4,5,6,7,8,9,10,11,12,13,14,15,400,401,402,403,404,405,406,407,..., dimensions={0} | all-to-all | bytes 3145728 | tf_op jit(solution)/shard_map/all_to_all | solution.py:298
  123.1 0.0 copy-done
  123.1 1.3 shard_map.98
  124.4 3.3 %collective-permute-start.2 = (bf16[256,512]{1,0:T(8,128)(2,1)S(1)}, bf16[256,512]{1,0:T(8,128)(2,1)S(1)}, u32[]{:S(2)}, u32[]{:S(2)}) collective-permute-start(bf16[256,512]{1,0:T(8,128)(2,1)S(1)} %get-tuple-element.35), channel_id=1, source_target_pairs={{0,1},{1,0},{2,3},{3,2},{4,5},{5,4},{6,7},{7,6},{8,9},{9,8},{10,11... | collective-permute-start | bytes 786440 | tf_op jit(solution)/shard_map/ppermute | solution.py:408
  127.7 1.5 shard_map.99
  129.2 0.0 collective-permute-done.2.given_ref
  129.2 0.3 shard_map.100
  129.6 18.6 %all_to_all.22 = bf16[32,8,512]{2,1,0:T(8,128)(2,1)S(1)} all-to-all(bf16[32,8,512]{2,1,0:T(8,128)(2,1)S(1)} %bitcast.18), channel_id=1, replica_groups=mesh['yl'=2,'z'=12,'chip'=16,'core'=2] {'yl','chip'}, dimensions={0} | all-to-all | bytes 524288 | tf_op jit(solution)/shard_map/all_to_all | solution.py:298
  148.2 16.8 %all_to_all.23 = bf16[24,8,512]{2,1,0:T(8,128)(2,1)S(1)} all-to-all(bf16[24,8,512]{2,1,0:T(8,128)(2,1)S(1)} %bitcast.20), channel_id=1, replica_groups=mesh['yl'=2,'z'=12,'chip'=16,'core'=2] {'yl','z'}, dimensions={0} | all-to-all | bytes 393216 | tf_op jit(solution)/shard_map/all_to_all | solution.py:298
  165.0 0.6 shard_map.102
  (1 shorter events, 0.0 us)
Async XLA Ops:
  1.5 19.2 %collective-permute-start.1 = (bf16[32,2048]{1,0:T(8,128)(2,1)S(1)}, bf16[32,2048]{1,0:T(8,128)(2,1)S(1)}, u32[]{:S(2)}, u32[]{:S(2)}) collective-permute-start(bf16[32,2048]{1,0:T(8,128)(2,1)S(1)} %slice.3), channel_id=1, source_target_pairs={{32,0},{64,32},{96,64},{128,96},{160,128},{192,160},{224,192},{256... | collective-permute-start | bytes 393224 | tf_op jit(solution)/shard_map/ppermute | solution.py:398
  18.8 9.0 %collective-permute-start = (bf16[32,2048]{1,0:T(8,128)(2,1)S(1)}, bf16[32,2048]{1,0:T(8,128)(2,1)S(1)}, u32[]{:S(2)}, u32[]{:S(2)}) collective-permute-start(bf16[32,2048]{1,0:T(8,128)(2,1)S(1)} %get-tuple-element.19), channel_id=1, source_target_pairs={{0,32},{32,64},{64,96},{96,128},{128,160},{160,192},{192,224},{224... | collective-permute-start | bytes 393224 | tf_op jit(solution)/shard_map/ppermute | solution.py:402
  27.7 46.9 %copy-start.2 = (bf16[1,2048,768]{2,1,0:T(8,128)(2,1)S(1)}, bf16[1,2048,768]{2,1,0:T(8,128)(2,1)}, u32[]{:S(2)}) copy-start(bf16[1,2048,768]{2,1,0:T(8,128)(2,1)} %up_ref.1) | copy-start | bytes 9437188
  27.7 46.9 %copy-start.3 = (bf16[1,768,2048]{2,1,0:T(8,128)(2,1)S(1)}, bf16[1,768,2048]{2,1,0:T(8,128)(2,1)}, u32[]{:S(2)}) copy-start(bf16[1,768,2048]{2,1,0:T(8,128)(2,1)} %down_ref.1) | copy-start | bytes 9437188
  28.5 46.1 %copy-start.1 = (bf16[1,2048,768]{2,1,0:T(8,128)(2,1)S(1)}, bf16[1,2048,768]{2,1,0:T(8,128)(2,1)}, u32[]{:S(2)}) copy-start(bf16[1,2048,768]{2,1,0:T(8,128)(2,1)} %gate_ref.1) | copy-start | bytes 9437188
  78.8 44.3 %copy-start = (bf16[128,2048]{1,0:T(8,128)(2,1)S(1)}, bf16[128,2048]{1,0:T(8,128)(2,1)}, u32[]{:S(2)}) copy-start(bf16[128,2048]{1,0:T(8,128)(2,1)} %grad_ref.1) | copy-start | bytes 1572868
  124.4 4.8 %collective-permute-start.2 = (bf16[256,512]{1,0:T(8,128)(2,1)S(1)}, bf16[256,512]{1,0:T(8,128)(2,1)S(1)}, u32[]{:S(2)}, u32[]{:S(2)}) collective-permute-start(bf16[256,512]{1,0:T(8,128)(2,1)S(1)} %get-tuple-element.35), channel_id=1, source_target_pairs={{0,1},{1,0},{2,3},{3,2},{4,5},{5,4},{6,7},{7,6},{8,9},{9,8},{10,11... | collective-permute-start | bytes 786440 | tf_op jit(solution)/shard_map/ppermute | solution.py:408

commit v11 on v9

--- a/solution.py
+++ b/solution.py
@@ -26,7 +26,7 @@
 DP = ("yl", "z")
 FSDP = ("chip", "core")
 CHIPS = 16
-FF_CHUNK = 256
+FF_CHUNK = 768
 bf16, f32, i32 = jnp.bfloat16, jnp.float32, jnp.int32
 VMEM = pl.BlockSpec(memory_space=pltpu.VMEM)
 SMEM = pl.BlockSpec(memory_space=pltpu.SMEM)

time: 165 us -> 165 us (level)
  no operation moved by 1% of the time
where the time goes in v11:
time: 165 us; the launch traced here: 164 us
  blocking collectives  131 us (79%)
  starting transfers between devices  19.4 us (12%)
  Pallas kernels  10.3 us (6%)
  waiting for transfers between devices  2.74 us (2%)
    all_to_all x4, blocking collectives, exchange(): lax.all_to_all(apart, axes, split_axis=0, concat_axis=0, axis_index_group...  131 us
    ppermute x1, starting transfers between devices, shards(): right = lax.ppermute(head, DP, [((i + 1) % ranks, i) for i in range(ranks)])  12.1 us
    ppermute x1, starting transfers between devices, shards(): left = lax.ppermute(tail, DP, [(i, (i + 1) % ranks) for i in range(ranks)])  4.29 us
    pallas_call x1, Pallas kernels, ffn(): call(ffn_kernel, shape((ROWS, WIDTH), bf16), [VMEM] * 4, 3700000000, [plt...  4.16 us
  transfers between devices with their start and end apart: 3, of which 2 were waited for; matrix products, arithmetic and copies ran while one was open for 0% of the time, Pallas kernels for 1%

profile of v11, /device:TPU:8, one launch (start us, length us, event | category | flops | bytes accessed | tf_op | source)
XLA Modules:
  0.0 164.3 jit_solution(4454364672550536815)
XLA Ops:
  0.6 1.6 shard_map.95
  2.2 4.3 %collective-permute-start = (bf16[32,2048]{1,0:T(8,128)(2,1)S(1)}, bf16[32,2048]{1,0:T(8,128)(2,1)S(1)}, u32[]{:S(2)}, u32[]{:S(2)}) collective-permute-start(bf16[32,2048]{1,0:T(8,128)(2,1)S(1)} %get-tuple-element.20), channel_id=1, source_target_pairs={{0,32},{32,64},{64,96},{96,128},{128,160},{160,192},{192,224},{224... | collective-permute-start | bytes 393224 | tf_op jit(solution)/shard_map/ppermute | solution.py:404
  6.5 12.1 %collective-permute-start.1 = (bf16[32,2048]{1,0:T(8,128)(2,1)S(1)}, bf16[32,2048]{1,0:T(8,128)(2,1)S(1)}, u32[]{:S(2)}, u32[]{:S(2)}) collective-permute-start(bf16[32,2048]{1,0:T(8,128)(2,1)S(1)} %get-tuple-element.21), channel_id=1, source_target_pairs={{32,0},{64,32},{96,64},{128,96},{160,128},{192,160},{224,192},{256... | collective-permute-start | bytes 393224 | tf_op jit(solution)/shard_map/ppermute | solution.py:405
  18.7 1.6 collective-permute-done.left_ref
  20.2 1.2 collective-permute-done.1.right_ref
  21.4 0.0 copy-start.2
  21.4 0.0 copy-start.3
  21.4 0.7 shard_map.96
  22.2 0.0 copy-start.1
  22.2 48.5 %all_to_all.20 = bf16[32,8,3072]{2,1,0:T(8,128)(2,1)S(1)} all-to-all(bf16[32,8,3072]{2,1,0:T(8,128)(2,1)S(1)} %bitcast.15), channel_id=1, replica_groups={{0,1,2,3,4,5,6,7,8,9,10,11,12,13,14,15,400,401,402,403,404,405,406,407,..., dimensions={0} | all-to-all | bytes 3145728 | tf_op jit(solution)/shard_map/all_to_all | solution.py:300
  70.7 0.0 copy-done.2
  70.7 0.0 copy-done.3
  70.7 0.0 copy-done.1
  70.7 4.2 %shard_map.97 = bf16[256,3072]{1,0:T(8,128)(2,1)S(1)} custom-call(bf16[256,3072]{1,0:T(8,128)(2,1)S(1)} %bitcast.16, bf16[1,2048,768]{2,1,0:T(8,128)(2,1)S(1)} %copy-done.1, bf16[1,2048,768]{2,1,0:T(8,128)(2,1)S(1)} %copy-done.2, bf16[1,768,2048]{2,1,0:T(8,128)(2,1)S(1)} %copy-done.3), custom_call_target="tpu_custom_call" | custom-call | flops 3700000000 | bytes 3145728 | tf_op jit(solution)/shard_map/pallas_call | solution.py:355
  74.8 0.0 copy-start
  74.9 44.6 %all_to_all.21 = bf16[32,8,3072]{2,1,0:T(8,128)(2,1)S(1)} all-to-all(bf16[32,8,3072]{2,1,0:T(8,128)(2,1)S(1)} %bitcast.17), channel_id=1, replica_groups={{0,1,2,3,4,5,6,7,8,9,10,11,12,13,14,15,400,401,402,403,404,405,406,407,..., dimensions={0} | all-to-all | bytes 3145728 | tf_op jit(solution)/shard_map/all_to_all | solution.py:300
  119.4 0.0 copy-done
  119.4 1.3 shard_map.98
  120.7 3.0 %collective-permute-start.2 = (bf16[256,512]{1,0:T(8,128)(2,1)S(1)}, bf16[256,512]{1,0:T(8,128)(2,1)S(1)}, u32[]{:S(2)}, u32[]{:S(2)}) collective-permute-start(bf16[256,512]{1,0:T(8,128)(2,1)S(1)} %get-tuple-element.37), channel_id=1, source_target_pairs={{0,1},{1,0},{2,3},{3,2},{4,5},{5,4},{6,7},{7,6},{8,9},{9,8},{10,11... | collective-permute-start | bytes 786440 | tf_op jit(solution)/shard_map/ppermute | solution.py:411
  123.7 1.5 shard_map.99
  125.2 0.0 collective-permute-done.2.given_ref
  125.2 0.3 shard_map.100
  125.6 18.3 %all_to_all.22 = bf16[32,8,512]{2,1,0:T(8,128)(2,1)S(1)} all-to-all(bf16[32,8,512]{2,1,0:T(8,128)(2,1)S(1)} %bitcast.18), channel_id=1, replica_groups=mesh['yl'=2,'z'=12,'chip'=16,'core'=2] {'yl','chip'}, dimensions={0} | all-to-all | bytes 524288 | tf_op jit(solution)/shard_map/all_to_all | solution.py:300
  143.9 19.7 %all_to_all.23 = bf16[24,8,512]{2,1,0:T(8,128)(2,1)S(1)} all-to-all(bf16[24,8,512]{2,1,0:T(8,128)(2,1)S(1)} %bitcast.20), channel_id=1, replica_groups=mesh['yl'=2,'z'=12,'chip'=16,'core'=2] {'yl','z'}, dimensions={0} | all-to-all | bytes 393216 | tf_op jit(solution)/shard_map/all_to_all | solution.py:300
  163.6 0.6 shard_map.102
  (1 shorter events, 0.0 us)
Async XLA Ops:
  2.2 18.0 %collective-permute-start = (bf16[32,2048]{1,0:T(8,128)(2,1)S(1)}, bf16[32,2048]{1,0:T(8,128)(2,1)S(1)}, u32[]{:S(2)}, u32[]{:S(2)}) collective-permute-start(bf16[32,2048]{1,0:T(8,128)(2,1)S(1)} %get-tuple-element.20), channel_id=1, source_target_pairs={{0,32},{32,64},{64,96},{96,128},{128,160},{160,192},{192,224},{224... | collective-permute-start | bytes 393224 | tf_op jit(solution)/shard_map/ppermute | solution.py:404
  6.5 14.9 %collective-permute-start.1 = (bf16[32,2048]{1,0:T(8,128)(2,1)S(1)}, bf16[32,2048]{1,0:T(8,128)(2,1)S(1)}, u32[]{:S(2)}, u32[]{:S(2)}) collective-permute-start(bf16[32,2048]{1,0:T(8,128)(2,1)S(1)} %get-tuple-element.21), channel_id=1, source_target_pairs={{32,0},{64,32},{96,64},{128,96},{160,128},{192,160},{224,192},{256... | collective-permute-start | bytes 393224 | tf_op jit(solution)/shard_map/ppermute | solution.py:405
  21.4 49.3 %copy-start.2 = (bf16[1,2048,768]{2,1,0:T(8,128)(2,1)S(1)}, bf16[1,2048,768]{2,1,0:T(8,128)(2,1)}, u32[]{:S(2)}) copy-start(bf16[1,2048,768]{2,1,0:T(8,128)(2,1)} %up_ref.1) | copy-start | bytes 9437188
  21.4 49.3 %copy-start.3 = (bf16[1,768,2048]{2,1,0:T(8,128)(2,1)S(1)}, bf16[1,768,2048]{2,1,0:T(8,128)(2,1)}, u32[]{:S(2)}) copy-start(bf16[1,768,2048]{2,1,0:T(8,128)(2,1)} %down_ref.1) | copy-start | bytes 9437188
  22.2 48.5 %copy-start.1 = (bf16[1,2048,768]{2,1,0:T(8,128)(2,1)S(1)}, bf16[1,2048,768]{2,1,0:T(8,128)(2,1)}, u32[]{:S(2)}) copy-start(bf16[1,2048,768]{2,1,0:T(8,128)(2,1)} %gate_ref.1) | copy-start | bytes 9437188
  74.8 44.6 %copy-start = (bf16[128,2048]{1,0:T(8,128)(2,1)S(1)}, bf16[128,2048]{1,0:T(8,128)(2,1)}, u32[]{:S(2)}) copy-start(bf16[128,2048]{1,0:T(8,128)(2,1)} %grad_ref.1) | copy-start | bytes 1572868
  120.7 4.5 %collective-permute-start.2 = (bf16[256,512]{1,0:T(8,128)(2,1)S(1)}, bf16[256,512]{1,0:T(8,128)(2,1)S(1)}, u32[]{:S(2)}, u32[]{:S(2)}) collective-permute-start(bf16[256,512]{1,0:T(8,128)(2,1)S(1)} %get-tuple-element.37), channel_id=1, source_target_pairs={{0,1},{1,0},{2,3},{3,2},{4,5},{5,4},{6,7},{7,6},{8,9},{9,8},{10,11... | collective-permute-start | bytes 786440 | tf_op jit(solution)/shard_map/ppermute | solution.py:411
